TPU v7x, 128 devices: a whole 4x4x4 slice. The times are simulated.
128 devices in a mesh: section: 2 (over x_lo), dp: 16 (over z, y), ctx: 4 (over x_hi, core).
Axes of the slice: x: 4 (x_hi: 2, x_lo: 2; x = x_hi * 2 + x_lo), y: 4, z: 4, core: 2. Of those that a mesh axis runs over, the one named last changes fastest.
Arguments:
- ends_in: bfloat16 [2, 2, 16, 256, 1024], P('section', None, 'dp', 'ctx'), may hold values from -6 to 6
- lengths: int32 [2, 16, 3], P(None, 'dp'), may hold values from 1 to 224, 256 in all within a row
- qkv_w: float32 [2, 1024, 3072], P('section', 'dp'), may hold values from -0.1875 to 0.1875
- out_w: float32 [2, 1024, 1024], P('section', 'dp'), may hold values from -1.5 to 1.5
- gate_w: float32 [2, 1024, 2816], P('section', 'dp'), may hold values from -0.1875 to 0.1875
- up_w: float32 [2, 1024, 2816], P('section', 'dp'), may hold values from -0.1875 to 0.1875
- down_w: float32 [2, 2816, 1024], P('section', 'dp'), may hold values from -0.109375 to 0.109375
- gains: float32 [2, 2, 1024], P('section', None, 'dp'), may hold values from 0.5 to 1.5
Outputs:
- edges: bfloat16 [2, 2, 16, 256, 1024], P('section', None, 'dp', 'ctx')
- qkv_grad: float32 [2, 1024, 3072], P('section', 'dp')
- out_grad: float32 [2, 1024, 1024], P('section', 'dp')
- gate_grad: float32 [2, 1024, 2816], P('section', 'dp')
- up_grad: float32 [2, 1024, 2816], P('section', 'dp')
- down_grad: float32 [2, 2816, 1024], P('section', 'dp')
- gains_grad: float32 [2, 2, 1024], P('section', None, 'dp')
Inputs may be any that keep to these rules, and one draw needn't show every extreme that they name: Each row of lengths holds 3 positive document lengths that sum to 256; the longest is exactly 224.
All inputs are finite; a program needn't handle non-finite values.
Results may differ from a plain program's by a relative error of at most 0.025.
Values may be sent and summed in bfloat16 or wider, within the bound.
A program may use at most 576 MiB of HBM per device.

v0:
```python
import jax
import jax.numpy as jnp
from jax import lax
from jax.sharding import PartitionSpec as P

HEAD_DIM = 64


epsilon = 1e-05
heads_per_block = 4


def from_behind(value, axis, steps):
    count = lax.axis_size(axis)
    leading, last = (max(0, -steps), min(count, count - steps))
    return lax.ppermute(value, axis, [(source, source + steps) for source in range(leading, last)])


def shortened(x):
    return jax.tree.map(lambda a: a.astype(jnp.bfloat16) if a.dtype == jnp.float32 else a, x)


def matmul(left, right):
    return jnp.dot(left, right, preferred_element_type=jnp.float32)


def matmul_left_t(left, right):
    return lax.dot_general(
        left, right, (((0,), (0,)), ((), ())), preferred_element_type=jnp.float32
    )


def matmul_right_t(left, right):
    return lax.dot_general(
        left, right, (((1,), (1,)), ((), ())), preferred_element_type=jnp.float32
    )


def run_if(active, function, operands):

    def skipped(*inner_ops):
        return jax.tree.map(jnp.zeros_like, function(*inner_ops))

    return lax.cond(active, function, skipped, *operands)


def rotary_tables(offsets, head_dim):
    half_dim = head_dim // 2
    frequency = 10000.0 ** (-jnp.arange(half_dim, dtype=jnp.float32) / half_dim)
    phases = offsets.astype(jnp.float32)[:, None] * frequency[None, :]
    return (jnp.cos(phases)[:, None, :], jnp.sin(phases)[:, None, :])


def rotate(heads_in, cosine, sine_table):
    half_dim = heads_in.shape[-1] // 2
    front_half = heads_in[..., :half_dim]
    back_half = heads_in[..., half_dim:]
    return jnp.concatenate(
        [
            front_half * cosine - back_half * sine_table,
            back_half * cosine + front_half * sine_table,
        ],
        axis=-1,
    )


def unrotate(grads_in, cosine, sine_table):
    half_dim = grads_in.shape[-1] // 2
    front_half = grads_in[..., :half_dim]
    back_half = grads_in[..., half_dim:]
    return jnp.concatenate(
        [
            front_half * cosine + back_half * sine_table,
            back_half * cosine - front_half * sine_table,
        ],
        axis=-1,
    )


def layout(doc_lengths, token_index):
    doc_ends = jnp.cumsum(doc_lengths)
    doc_starts = doc_ends - doc_lengths
    inside = (token_index[:, None] >= doc_starts[None, :]) & (
        token_index[:, None] < doc_ends[None, :]
    )
    doc_ids = jnp.sum((token_index[:, None] >= doc_ends[None, :]).astype(jnp.int32), axis=1)
    offsets = token_index - jnp.sum(jnp.where(inside, doc_starts[None, :], 0), axis=1)
    return (doc_ids, offsets)


def split_heads(tensor, head_dim):
    row_count = tensor.shape[0]
    blocks = tensor.shape[1] // (head_dim * heads_per_block)
    return tensor.reshape(row_count, blocks, heads_per_block, head_dim).transpose(1, 0, 2, 3)


def merge_heads(tensor):
    blocks, row_count, group_size, head_dim = tensor.shape
    return tensor.transpose(1, 0, 2, 3).reshape(row_count, blocks * group_size * head_dim)


def attend_forward(queries, key_rows, value_rows, allowed, head_dim):
    score_scale = head_dim ** (-0.5)

    def one_block(operands):
        q_part, k_part, v_part = operands
        scores = (
            jnp.einsum("qhd,khd->hqk", q_part, k_part, preferred_element_type=jnp.float32)
            * score_scale
        )
        scores = jnp.where(allowed[None], scores, -1e30)
        row_max = jnp.max(scores, axis=-1, keepdims=True)
        shifted = jnp.exp(scores - row_max)
        row_total = jnp.sum(shifted, axis=-1, keepdims=True)
        weights = (shifted / row_total).astype(jnp.bfloat16)
        attended = jnp.einsum("hqk,khd->qhd", weights, v_part, preferred_element_type=jnp.float32)
        return (attended, (row_max + jnp.log(row_total))[..., 0])

    attended, log_norm = lax.map(
        one_block,
        (
            split_heads(queries, head_dim),
            split_heads(key_rows, head_dim),
            split_heads(value_rows, head_dim),
        ),
    )
    return (merge_heads(attended).astype(jnp.bfloat16), log_norm)


def attend_backward(queries, key_rows, value_rows, grad_out, log_norm, allowed, head_dim):
    score_scale = head_dim ** (-0.5)

    def one_block(operands):
        q_part, k_part, v_part, g_part, norm_part = operands
        scores = (
            jnp.einsum("qhd,khd->hqk", q_part, k_part, preferred_element_type=jnp.float32)
            * score_scale
        )
        scores = jnp.where(allowed[None], scores, -1e30)
        weights = jnp.exp(scores - norm_part[..., None])
        grad_w = jnp.einsum("qhd,khd->hqk", g_part, v_part, preferred_element_type=jnp.float32)
        grad_s = (weights * (grad_w - jnp.sum(weights * grad_w, axis=-1, keepdims=True))).astype(
            jnp.bfloat16
        )
        grad_q = (
            jnp.einsum("hqk,khd->qhd", grad_s, k_part, preferred_element_type=jnp.float32)
            * score_scale
        )
        grad_k = (
            jnp.einsum("hqk,qhd->khd", grad_s, q_part, preferred_element_type=jnp.float32)
            * score_scale
        )
        grad_v = jnp.einsum(
            "hqk,qhd->khd", weights.astype(jnp.bfloat16), g_part, preferred_element_type=jnp.float32
        )
        return (grad_q, grad_k, grad_v)

    grad_q, grad_k, grad_v = lax.map(
        one_block,
        (
            split_heads(queries, head_dim),
            split_heads(key_rows, head_dim),
            split_heads(value_rows, head_dim),
            split_heads(grad_out, head_dim),
            log_norm,
        ),
    )
    return (merge_heads(grad_q), merge_heads(grad_k), merge_heads(grad_v))


def project(tokens_in, mixed_in, mix, gain_one, qkv_w, cosine, sine_table, head_dim):
    row_count, model_width = tokens_in.shape
    head_count = model_width // head_dim
    inv_one = lax.rsqrt(jnp.mean(tokens_in * tokens_in, axis=-1, keepdims=True) + epsilon)
    normed = (tokens_in * inv_one * gain_one).astype(jnp.bfloat16)
    packed = matmul(normed, qkv_w)
    queries = rotate(
        packed[:, :model_width].reshape(row_count, head_count, head_dim), cosine, sine_table
    )
    key_rows = rotate(
        packed[:, model_width : 2 * model_width].reshape(row_count, head_count, head_dim),
        cosine,
        sine_table,
    )
    value_rows = (1.0 - mix) * packed[:, 2 * model_width :] + mix * mixed_in.astype(jnp.float32)
    return (
        queries.reshape(row_count, model_width).astype(jnp.bfloat16),
        key_rows.reshape(row_count, model_width).astype(jnp.bfloat16),
        value_rows.astype(jnp.bfloat16),
    )


def finish(tokens_in, attended, gain_two, out_w, gate_w, up_w, down_w):
    hidden = tokens_in + matmul(attended, out_w)
    inv_two = lax.rsqrt(jnp.mean(hidden * hidden, axis=-1, keepdims=True) + epsilon)
    normed_two = (hidden * inv_two * gain_two).astype(jnp.bfloat16)
    gate_act = matmul(normed_two, gate_w)
    up_act = matmul(normed_two, up_w)
    product = (jax.nn.silu(gate_act) * up_act).astype(jnp.bfloat16)
    return (hidden + matmul(product, down_w), hidden, gate_act, up_act)


def back_tail(grad_y, hidden, gate_act, up_act, attended, gain_two, out_w, gate_w, up_w, down_w):
    inv_two = lax.rsqrt(jnp.mean(hidden * hidden, axis=-1, keepdims=True) + epsilon)
    normed_two = (hidden * inv_two * gain_two).astype(jnp.bfloat16)
    sigma = jax.nn.sigmoid(gate_act)
    product = (jax.nn.silu(gate_act) * up_act).astype(jnp.bfloat16)
    grad_y_b = grad_y.astype(jnp.bfloat16)
    grad_down_w = matmul_left_t(product, grad_y_b)
    grad_product = matmul_right_t(grad_y_b, down_w)
    grad_gate = (grad_product * up_act * sigma * (1.0 + gate_act * (1.0 - sigma))).astype(
        jnp.bfloat16
    )
    grad_up = (grad_product * jax.nn.silu(gate_act)).astype(jnp.bfloat16)
    grad_gate_w = matmul_left_t(normed_two, grad_gate)
    grad_up_w = matmul_left_t(normed_two, grad_up)
    grad_normed = matmul_right_t(grad_gate, gate_w) + matmul_right_t(grad_up, up_w)
    grad_gain_two = jnp.sum(grad_normed * hidden * inv_two, axis=0)
    scaled = grad_normed * gain_two
    grad_hidden = (
        grad_y
        + inv_two * scaled
        - hidden * inv_two**3 * jnp.mean(scaled * hidden, axis=-1, keepdims=True)
    )
    grad_att_in = grad_hidden.astype(jnp.bfloat16)
    grad_out_w = matmul_left_t(attended, grad_att_in)
    grad_attended = matmul_right_t(grad_att_in, out_w).astype(jnp.bfloat16)
    return (
        grad_hidden,
        grad_attended,
        grad_out_w,
        grad_gate_w,
        grad_up_w,
        grad_down_w,
        grad_gain_two,
    )


def back_head(
    grad_q,
    grad_k,
    grad_v,
    recv_value,
    mix,
    tokens_in,
    grad_hidden,
    gain_one,
    qkv_w,
    cosine,
    sine_table,
    head_dim,
):
    row_count, model_width = tokens_in.shape
    head_count = model_width // head_dim
    value_total = (grad_v + recv_value.astype(jnp.float32)).astype(jnp.bfloat16).astype(jnp.float32)
    sent_value = (mix * value_total).astype(jnp.bfloat16)

    def back_rope(grad_in):
        rounded = (
            grad_in.astype(jnp.bfloat16)
            .astype(jnp.float32)
            .reshape(row_count, head_count, head_dim)
        )
        return unrotate(rounded, cosine, sine_table).reshape(row_count, model_width)

    grad_packed = jnp.concatenate(
        [back_rope(grad_q), back_rope(grad_k), (1.0 - mix) * value_total], axis=1
    ).astype(jnp.bfloat16)
    inv_one = lax.rsqrt(jnp.mean(tokens_in * tokens_in, axis=-1, keepdims=True) + epsilon)
    normed = (tokens_in * inv_one * gain_one).astype(jnp.bfloat16)
    grad_qkv_w = matmul_left_t(normed, grad_packed)
    grad_normed = matmul_right_t(grad_packed, qkv_w)
    grad_gain_one = jnp.sum(grad_normed * tokens_in * inv_one, axis=0)
    scaled = grad_normed * gain_one
    grad_tokens = (
        grad_hidden
        + inv_one * scaled
        - tokens_in * inv_one**3 * jnp.mean(scaled * tokens_in, axis=-1, keepdims=True)
    )
    return (grad_tokens, sent_value, grad_qkv_w, grad_gain_one)


def per_device(ends_in, lengths, qkv_w, out_w, gate_w, up_w, down_w, gains):
    head_dim = HEAD_DIM
    section_index = lax.axis_index("section")
    first_section = section_index == 0
    mix = 0.5 * section_index.astype(jnp.float32)
    shards = (
        qkv_w[0].astype(jnp.bfloat16),
        out_w[0].astype(jnp.bfloat16),
        gate_w[0].astype(jnp.bfloat16),
        up_w[0].astype(jnp.bfloat16),
        down_w[0].astype(jnp.bfloat16),
        gains[0].astype(jnp.bfloat16),
    )
    qkv_full, out_full, gate_full, up_full, down_full, gain_full = (
        lax.all_gather(shards[0], "dp", axis=0, tiled=True),
        lax.all_gather(shards[1], "dp", axis=0, tiled=True),
        lax.all_gather(shards[2], "dp", axis=0, tiled=True),
        lax.all_gather(shards[3], "dp", axis=0, tiled=True),
        lax.all_gather(shards[4], "dp", axis=0, tiled=True),
        lax.all_gather(shards[5], "dp", axis=1, tiled=True),
    )
    gain_one = gain_full[0].astype(jnp.float32)
    gain_two = gain_full[1].astype(jnp.float32)
    local_rows = ends_in[0, :, 0]
    doc_table = lengths[:, 0]
    micro_count = local_rows.shape[0]
    row_count = local_rows.shape[1]
    model_width = local_rows.shape[2]
    seq_length = row_count * lax.axis_size("ctx")
    query_index = lax.axis_index("ctx") * row_count + jnp.arange(row_count, dtype=jnp.int32)
    key_index = jnp.arange(seq_length, dtype=jnp.int32)

    def geometry(micro_index):
        doc_lengths = lax.dynamic_index_in_dim(doc_table, micro_index, 0, keepdims=False)
        query_docs, offsets = layout(doc_lengths, query_index)
        key_docs, unused_offsets = layout(doc_lengths, key_index)
        allowed = (query_docs[:, None] == key_docs[None, :]) & (
            key_index[None, :] <= query_index[:, None]
        )
        cosine, sine_table = rotary_tables(offsets, head_dim)
        return (allowed, cosine, sine_table)

    recv_rows = jnp.zeros((row_count, model_width), jnp.bfloat16)
    recv_value = jnp.zeros((row_count, model_width), jnp.bfloat16)
    saved = []
    front_outputs = []
    for loop_step in range(micro_count + 1):
        micro_index = jnp.clip(loop_step - section_index, 0, micro_count - 1)
        active = (loop_step - section_index >= 0) & (loop_step - section_index < micro_count)
        own_rows = local_rows[min(loop_step, micro_count - 1)]
        tokens_in = jnp.where(first_section, own_rows, recv_rows).astype(jnp.float32)
        allowed, cosine, sine_table = geometry(micro_index)
        queries, key_part, value_part = run_if(
            active,
            lambda tokens_arg, mixed_arg: project(
                tokens_arg, mixed_arg, mix, gain_one, qkv_full, cosine, sine_table, head_dim
            ),
            (tokens_in, recv_value),
        )
        key_rows, value_rows = (
            lax.all_gather(key_part, "ctx", axis=0, tiled=True),
            lax.all_gather(value_part, "ctx", axis=0, tiled=True),
        )
        attended, log_norm = run_if(
            active,
            lambda query_arg, key_arg, value_arg: attend_forward(
                query_arg, key_arg, value_arg, allowed, head_dim
            ),
            (queries, key_rows, value_rows),
        )
        layer_out, hidden, gate_act, up_act = run_if(
            active,
            lambda tokens_arg, attended_arg: finish(
                tokens_arg, attended_arg, gain_two, out_full, gate_full, up_full, down_full
            ),
            (tokens_in, attended),
        )
        if loop_step < micro_count:
            recv_rows, recv_value = from_behind(
                (layer_out.astype(jnp.bfloat16), value_part), "section", 1
            )
        saved.append(
            (tokens_in, queries, key_rows, value_rows, attended, log_norm, hidden, gate_act, up_act)
        )
        front_outputs.append(layer_out)
    stacked = tuple((jnp.stack(column) for column in zip(*saved)))
    grad_totals = (
        jnp.zeros(qkv_full.shape, jnp.float32),
        jnp.zeros(out_full.shape, jnp.float32),
        jnp.zeros(gate_full.shape, jnp.float32),
        jnp.zeros(up_full.shape, jnp.float32),
        jnp.zeros(down_full.shape, jnp.float32),
        jnp.zeros(gain_full.shape, jnp.float32),
    )
    recv_grad = jnp.zeros((row_count, model_width), jnp.bfloat16)
    recv_grad_value = jnp.zeros((row_count, model_width), jnp.bfloat16)
    input_grads = []
    for loop_step in range(micro_count + 1):
        micro_raw = micro_count - 1 - loop_step + (1 - section_index)
        active = (micro_raw >= 0) & (micro_raw < micro_count)
        micro_index = jnp.clip(micro_raw, 0, micro_count - 1)
        saved_step = micro_index + section_index
        tokens_in, queries, key_rows, value_rows, attended, log_norm, hidden, gate_act, up_act = (
            tuple(
                (
                    lax.dynamic_index_in_dim(column, saved_step, 0, keepdims=False)
                    for column in stacked
                )
            )
        )
        allowed, cosine, sine_table = geometry(micro_index)
        cotangent = lax.dynamic_index_in_dim(local_rows, micro_index, 0, keepdims=False)
        grad_y = jnp.where(first_section, recv_grad, cotangent).astype(jnp.float32)
        (
            grad_hidden,
            grad_attended,
            grad_out_w,
            grad_gate_w,
            grad_up_w,
            grad_down_w,
            grad_gain_two,
        ) = run_if(
            active,
            lambda grad_arg: back_tail(
                grad_arg,
                hidden,
                gate_act,
                up_act,
                attended,
                gain_two,
                out_full,
                gate_full,
                up_full,
                down_full,
            ),
            (grad_y,),
        )
        grad_q, grad_k_full, grad_v_full = run_if(
            active,
            lambda grad_arg: attend_backward(
                queries, key_rows, value_rows, grad_arg, log_norm, allowed, head_dim
            ),
            (grad_attended,),
        )
        grad_k, grad_v = (
            lax.psum_scatter(
                grad_k_full.astype(jnp.bfloat16), "ctx", scatter_dimension=0, tiled=True
            ).astype(jnp.float32),
            lax.psum_scatter(
                grad_v_full.astype(jnp.bfloat16), "ctx", scatter_dimension=0, tiled=True
            ).astype(jnp.float32),
        )
        grad_tokens, sent_value, grad_qkv_w, grad_gain_one = run_if(
            active,
            lambda q_arg, k_arg, v_arg, r_arg: back_head(
                q_arg,
                k_arg,
                v_arg,
                r_arg,
                mix,
                tokens_in,
                grad_hidden,
                gain_one,
                qkv_full,
                cosine,
                sine_table,
                head_dim,
            ),
            (grad_q, grad_k, grad_v, recv_grad_value),
        )
        if loop_step < micro_count:
            recv_grad, recv_grad_value = from_behind(
                (grad_tokens.astype(jnp.bfloat16), sent_value), "section", -1
            )
        input_grads.append(grad_tokens)
        grad_step = (
            grad_qkv_w,
            grad_out_w,
            grad_gate_w,
            grad_up_w,
            grad_down_w,
            jnp.stack([grad_gain_one, grad_gain_two]),
        )
        grad_totals = tuple(
            (total_part + step_part for total_part, step_part in zip(grad_totals, grad_step))
        )
    edge_rows = []
    for micro_index in range(micro_count):
        edge_rows.append(
            jnp.where(
                first_section,
                input_grads[micro_count - micro_index],
                front_outputs[micro_index + 1],
            )
        )
    edges = jnp.stack(edge_rows).astype(jnp.bfloat16)[None, :, None]
    pieces = (
        lax.psum_scatter(
            grad_totals[0].astype(jnp.bfloat16), "dp", scatter_dimension=0, tiled=True
        ).astype(jnp.float32),
        lax.psum_scatter(
            grad_totals[1].astype(jnp.bfloat16), "dp", scatter_dimension=0, tiled=True
        ).astype(jnp.float32),
        lax.psum_scatter(
            grad_totals[2].astype(jnp.bfloat16), "dp", scatter_dimension=0, tiled=True
        ).astype(jnp.float32),
        lax.psum_scatter(
            grad_totals[3].astype(jnp.bfloat16), "dp", scatter_dimension=0, tiled=True
        ).astype(jnp.float32),
        lax.psum_scatter(
            grad_totals[4].astype(jnp.bfloat16), "dp", scatter_dimension=0, tiled=True
        ).astype(jnp.float32),
        lax.psum_scatter(
            grad_totals[5].astype(jnp.bfloat16), "dp", scatter_dimension=1, tiled=True
        ).astype(jnp.float32),
    )
    reduced = jax.tree.map(
        lambda part: part.astype(jnp.float32), lax.psum(shortened(pieces), "ctx")
    )
    return (edges,) + tuple((reduced_part[None] for reduced_part in reduced))


def solution(mesh):
    in_specs = (
        P("section", None, "dp", "ctx", None),
        P(None, "dp", None),
        P("section", "dp", None),
        P("section", "dp", None),
        P("section", "dp", None),
        P("section", "dp", None),
        P("section", "dp", None),
        P("section", None, "dp"),
    )
    out_specs = (
        P("section", None, "dp", "ctx", None),
        P("section", "dp", None),
        P("section", "dp", None),
        P("section", "dp", None),
        P("section", "dp", None),
        P("section", "dp", None),
        P("section", None, "dp"),
    )
    return jax.shard_map(
        per_device, mesh=mesh, in_specs=in_specs, out_specs=out_specs, check_vma=False
    )
```

profile of v0, /device:TPU:1, one launch (start us, length us, event | category | flops | bytes accessed | tf_op | source)
XLA Modules:
  0.0 1495.8 jit_solution(18133609084798044771)
XLA Ops:
  17.6 23.4 %all-gather = bf16[1,2,1024]{1,0,2:T(2,128)(2,1)S(1)} all-gather(bf16[1,2,64]{1,0,2:T(2,128)(2,1)S(1)} %copy.222), channel_id=2, replica_groups=mesh['section'=2,'dp'=16,'ctx'=4] {'dp'}, dimensions={2}, use_global_device_ids=true | all-gather | bytes 4352 | tf_op jit(solution)/shard_map/all_gather | solution.py:302
  43.1 6.3 fusion.271
  49.4 26.6 %all-gather.12.cloned.1.call-done = bf16[1,1024,3072]{2,1,0:T(8,128)(2,1)} async-done(((bf16[1,64,3072]{2,1,0:T(8,128)(2,1)}), bf16[1,1024,3072]{2,1,0:T(8,128)(2,1)}) %all-gather.12.cloned.1.call-update) | async-done | bytes 6291472 | tf_op jit(solution)/shard_map/all_gather | solution.py:297
  76.0 8.1 conditional.18
  85.5 11.3 all_gather.39
  96.7 9.2 all_gather.38
  106.0 10.9 conditional.19
  108.8 8.0 while.102
  122.1 61.8 %all-gather.16.cloned.1.call-done = bf16[1,1024,2816]{2,1,0:T(8,128)(2,1)} async-done(((bf16[1,64,2816]{2,1,0:T(8,128)(2,1)}), bf16[1,1024,2816]{2,1,0:T(8,128)(2,1)}) %all-gather.16.cloned.1.call-update) | async-done | bytes 5767184 | tf_op jit(solution)/shard_map/all_gather | solution.py:299
  183.9 61.2 %all-gather.18.cloned.1.call-done = bf16[1,1024,2816]{2,1,0:T(8,128)(2,1)} async-done(((bf16[1,64,2816]{2,1,0:T(8,128)(2,1)}), bf16[1,1024,2816]{2,1,0:T(8,128)(2,1)}) %all-gather.18.cloned.1.call-update) | async-done | bytes 5767184 | tf_op jit(solution)/shard_map/all_gather | solution.py:300
  245.0 61.2 %all-gather.20.cloned.1.call-done = bf16[1,2816,1024]{2,1,0:T(8,128)(2,1)} async-done(((bf16[1,176,1024]{2,1,0:T(8,128)(2,1)}), bf16[1,2816,1024]{2,1,0:T(8,128)(2,1)}) %all-gather.20.cloned.1.call-update) | async-done | bytes 5767184 | tf_op jit(solution)/shard_map/all_gather | solution.py:301
  306.2 13.8 conditional.20
  329.3 6.6 conditional.21
  337.9 10.7 all_gather.45
  348.6 9.2 all_gather.44
  357.9 20.6 %conditional.22 = (bf16[64,1024]{0,1:T(8,128)(2,1)}, f32[1,4,4,64]{3,2,1,0:T(4,128)}) conditional(s32[]{:T(128)} %convert_element_type.629, () %tuple.256, (bf16[64,1024]{1,0:T(8,128)(2,1)}, bf16[256,1024]{1,0:T(8,128)(2,1)}, bf16[256,1024]{1,0:T(8,128)(2,1)}, pred[64,256]{1,0:T(8,128)(4,1)S(1)}) %tuple.679), branch_computations={%region_23.24_spmd, %region_24.29_spmd} | conditional | flops 17301248 | bytes 3664065 | solution.py:44
  363.3 15.2 %while.103 = (s32[]{:T(128)}, bf16[4,64,4,64]{1,3,2,0:T(8,128)(2,1)}, f32[4,4,64]{2,1,0:T(4,128)}, bf16[4,256,4,64]{1,3,2,0:T(8,128)(2,1)}, pred[64,256]{1,0:T(8...) while((s32[]{:T(128)}, ...), condition=%wide.region_28.28_spmd, body=%wide.region_25.27_spmd.sunk | while | flops 17301248 | bytes 1304681 | solution.py:119
  378.5 12.8 conditional.23
  406.0 9.5 all_gather.46
  415.5 9.6 all_gather.47
  440.4 19.7 %conditional.27 = (f32[64,1024]{1,0:T(8,128)}, bf16[64,1024]{1,0:T(8,128)(2,1)}, f32[1024,1024]{1,0:T(8,128)}, f32[1024,2816]{1,0:T(8,128)}, f32[1024,2816]{1,0:...) conditional(s32[]{:T(128)} %convert_element_type.635, () %tuple.274, ...), branch_computations={%region_48.49_spmd, %region_49.53_spmd.clone} | conditional | flops 2488155392 | bytes 113598856 | solution.py:44
  444.3 5.0 broadcast.837.clone
  449.3 5.7 broadcast.838
  455.0 4.9 broadcast.837
  474.1 123.6 %reduce-scatter.15.cloned.1.call-done = bf16[64,1024]{1,0:T(8,128)(2,1)} async-done(((bf16[256,1024]{1,0:T(8,128)(2,1)}), bf16[64,1024]{1,0:T(8,128)(2,1)}) %reduce-scatter.15.cloned.1.call-update) | async-done | bytes 131088 | tf_op jit(solution)/shard_map/reduce_scatter | solution.py:428
  597.7 31.4 %reduce-scatter.17.cloned.1.call-done = bf16[64,1024]{1,0:T(8,128)(2,1)} async-done(((bf16[256,1024]{1,0:T(8,128)(2,1)}), bf16[64,1024]{1,0:T(8,128)(2,1)}) %reduce-scatter.17.cloned.1.call-update) | async-done | bytes 131088 | tf_op jit(solution)/shard_map/reduce_scatter | solution.py:431
  629.1 7.8 conditional.29
  630.8 6.1 broadcast.850
  638.2 20.1 %collective-permute-done.4 = bf16[64,1024]{1,0:T(8,128)(2,1)S(1)} collective-permute-done((bf16[64,1024]{1,0:T(8,128)(2,1)}, bf16[64,1024]{1,0:T(8,128)(2,1)S(1)}, u32[]{:S(2)}, u32[]{:S(2)}) %collective-permute-start.4) | collective-permute-done | bytes 131104 | tf_op jit(solution)/shard_map/ppermute | solution.py:16
  659.2 33.5 %conditional.30 = (f32[64,1024]{1,0:T(8,128)S(1)}, bf16[64,1024]{1,0:T(8,128)(2,1)}, f32[1024,1024]{1,0:T(8,128)}, f32[1024,2816]{1,0:T(8,128)}, f32[1024,2816]{...) conditional(s32[]{:T(128)} %convert_element_type.629, () %tuple.271, (f32[3,64,1024]{2,1,0:T(8,128)S(1)}, ...), branch_computations={%region_65.66_spmd, %region_66.70_spmd} | conditional | flops 2488155392 | bytes 115696568 | solution.py:44
  659.2 5.1 multiply_convert_fusion.22
  673.5 7.3 fusion.106
  680.8 6.0 fusion.127
  686.8 5.9 fusion.129
  693.4 31.5 %conditional.31 = (bf16[64,1024]{0,1:T(8,128)(2,1)}, bf16[256,1024]{0,1:T(8,128)(2,1)}, bf16[256,1024]{0,1:T(8,128)(2,1)}) conditional(s32[]{:T(128)} %convert_element_type.629, () %tuple.270, (bf16[3,64,1024]{2,1,0:T(8,128)(2,1)}, s32[]{:T(128)}, bf16[3,256,1024]{2,1,0:T(8,128)(2,1)}, bf16[3,256,1024]{2,1,0:T(8,128)(2,1)}, ...), branch_computations={%region_70.71_spmd, %region_71.75_spmd} | conditional | flops 42614528 | bytes 12516625 | solution.py:44
  705.0 19.9 %while.106 = (s32[]{:T(128)}, bf16[4,64,4,64]{1,3,2,0:T(8,128)(2,1)}, bf16[4,256,4,64]{1,3,2,0:T(8,128)(2,1)}, bf16[4,256,4,64]{1,3,2,0:T(8,128)(2,1)}, bf16[4,2...) while((s32[]{:T(128)}, ...), condition=%wide.region_74.74_spmd, body=%wide.region_72.73_spmd.sunk | while | flops 42614528 | bytes 3333261 | solution.py:158
  730.6 26.0 %reduce-scatter.21.cloned.1.call-done = bf16[64,1024]{1,0:T(8,128)(2,1)} async-done(((bf16[256,1024]{1,0:T(8,128)(2,1)}), bf16[64,1024]{1,0:T(8,128)(2,1)}) %reduce-scatter.21.cloned.1.call-update) | async-done | bytes 131088 | tf_op jit(solution)/shard_map/reduce_scatter | solution.py:431
  757.6 30.4 %reduce-scatter.19.cloned.1.call-done = bf16[64,1024]{1,0:T(8,128)(2,1)} async-done(((bf16[256,1024]{1,0:T(8,128)(2,1)}), bf16[64,1024]{1,0:T(8,128)(2,1)}) %reduce-scatter.19.cloned.1.call-update) | async-done | bytes 131088 | tf_op jit(solution)/shard_map/reduce_scatter | solution.py:428
  788.0 26.4 %conditional.32 = (bf16[64,1024]{1,0:T(8,128)(2,1)S(1)}, bf16[64,1024]{1,0:T(8,128)(2,1)S(1)}, f32[1024,3072]{1,0:T(8,128)}, f32[1,1024]{1,0:T(1,128)S(1)}) conditional(s32[]{:T(128)} %convert_element_type.629, () %tuple.269, (f32[3,64,1024]{2,1,0:T(8,128)}, s32[]{:T(128)}, bf16[64,1024]{0,1:T(8,128)(2,1)}, f32[64,1,32]{2,0,1:T(8,128)S(1)}, ...), branch_computations={%region_77.78_spmd, %region_78.82_spmd} | conditional | flops 810417344 | bytes 30510316 | solution.py:44
  800.7 5.1 fusion.160
  807.3 7.1 fusion.161
  821.7 33.6 %conditional.33 = (f32[64,1024]{1,0:T(8,128)S(1)}, bf16[64,1024]{1,0:T(8,128)(2,1)}, f32[1024,1024]{1,0:T(8,128)}, f32[1024,2816]{1,0:T(8,128)}, f32[1024,2816]{...) conditional(s32[]{:T(128)} %convert_element_type.602, () %tuple.264, (f32[3,64,1024]{2,1,0:T(8,128)S(1)}, ...), branch_computations={%region_82.83_spmd, %region_83.87_spmd} | conditional | flops 2488155392 | bytes 115696568 | solution.py:44
  821.9 5.1 multiply_convert_fusion.24
  836.2 7.3 fusion.177
  843.5 5.9 fusion.198
  849.4 5.9 fusion.200
  855.3 21.2 %conditional.34 = (bf16[64,1024]{0,1:T(8,128)(2,1)}, bf16[256,1024]{0,1:T(8,128)(2,1)}, bf16[256,1024]{0,1:T(8,128)(2,1)}) conditional(s32[]{:T(128)} %convert_element_type.602, () %tuple.261, (bf16[3,64,1024]{2,1,0:T(8,128)(2,1)}, s32[]{:T(128)}, bf16[3,256,1024]{2,1,0:T(8,128)(2,1)}, bf16[3,256,1024]{2,1,0:T(8,128)(2,1)}, ...), branch_computations={%region_87.88_spmd, %region_88.92_spmd} | conditional | flops 42614528 | bytes 12549393 | solution.py:44
  863.7 12.9 while.107
  881.0 7.3 add_convert_fusion.15
  888.4 14.4 add_convert_fusion.14
  902.9 14.3 add_convert_fusion.13
  917.3 15.2 %add_convert_fusion.12 = bf16[2816,1024]{1,0:T(8,128)(2,1)} fusion(f32[2816,1024]{1,0:T(8,128)} %get-tuple-element.1298, f32[2816,1024]{1,0:T(8,128)} %get-tuple-element.1296, f32[2816,1024]{1,0:T(8,128)} %get-tuple-element.1297), kind=kLoop, calls=%fused_computation.482 | loop fusion | flops 8650752 | bytes 40370176 | tf_op jit(solution)/shard_map/convert_element_type | solution.py:493
  939.1 16.0 %conditional.35 = (bf16[64,1024]{1,0:T(8,128)(2,1)S(1)}, f32[1024,3072]{1,0:T(8,128)}, f32[1,1024]{1,0:T(1,128)S(1)}) conditional(s32[]{:T(128)} %convert_element_type.602, () %tuple.248, (f32[3,64,1024]{2,1,0:T(8,128)S(1)}, s32[]{:T(128)}, bf16[64,1024]{0,1:T(8,128)(2,1)}, f32[64,1,32]{2,0,1:T(8,128)}, f32[64,1,32]{2,0,1:T(8,128)}, ...), branch_computations={%region_94.95_spmd, %region_95.99_spmd} | conditional | flops 810286272 | bytes 25070904 | solution.py:44
  943.5 4.9 fusion.229
  948.6 6.5 fusion.230
  955.1 16.3 %add_convert_fusion.11 = bf16[1024,3072]{1,0:T(8,128)(2,1)} fusion(f32[1024,3072]{1,0:T(8,128)} %get-tuple-element.1286, f32[1024,3072]{1,0:T(8,128)} %get-tuple-element.1284, f32[1024,3072]{1,0:T(8,128)} %get-tuple-element.1285), kind=kLoop, calls=%fused_computation.481 | loop fusion | flops 9437184 | bytes 44040192 | tf_op jit(solution)/shard_map/convert_element_type | solution.py:481
  973.1 40.9 %reduce-scatter.29.cloned.1.call-done = bf16[64,1024]{1,0:T(8,128)(2,1)} async-done(((bf16[1024,1024]{1,0:T(8,128)(2,1)}), bf16[64,1024]{1,0:T(8,128)(2,1)}) %reduce-scatter.29.cloned.1.call-update) | async-done | bytes 131088 | tf_op jit(solution)/shard_map/reduce_scatter | solution.py:483
  1014.0 83.6 %reduce-scatter.31.cloned.1.call-done = bf16[64,2816]{1,0:T(8,128)(2,1)} async-done(((bf16[1024,2816]{1,0:T(8,128)(2,1)}), bf16[64,2816]{1,0:T(8,128)(2,1)}) %reduce-scatter.31.cloned.1.call-update) | async-done | bytes 360464 | tf_op jit(solution)/shard_map/reduce_scatter | solution.py:486
  1097.6 83.1 %reduce-scatter.33.cloned.1.call-done = bf16[64,2816]{1,0:T(8,128)(2,1)} async-done(((bf16[1024,2816]{1,0:T(8,128)(2,1)}), bf16[64,2816]{1,0:T(8,128)(2,1)}) %reduce-scatter.33.cloned.1.call-update) | async-done | bytes 360464 | tf_op jit(solution)/shard_map/reduce_scatter | solution.py:489
  1180.7 83.0 %reduce-scatter.35.cloned.1.call-done = bf16[176,1024]{1,0:T(8,128)(2,1)} async-done(((bf16[2816,1024]{1,0:T(8,128)(2,1)}), bf16[176,1024]{1,0:T(8,128)(2,1)}) %reduce-scatter.35.cloned.1.call-update) | async-done | bytes 360464 | tf_op jit(solution)/shard_map/reduce_scatter | solution.py:492
  1263.7 84.4 %reduce-scatter.27.cloned.1.call-done = bf16[64,3072]{1,0:T(8,128)(2,1)} async-done(((bf16[1024,3072]{1,0:T(8,128)(2,1)}), bf16[64,3072]{1,0:T(8,128)(2,1)}) %reduce-scatter.27.cloned.1.call-update) | async-done | bytes 393232 | tf_op jit(solution)/shard_map/reduce_scatter | solution.py:480
  1349.0 74.0 %reduce-scatter.37.cloned.1.call-done = bf16[64,2]{1,0:T(8,128)(2,1)} async-done(((bf16[1024,2]{1,0:T(8,128)(2,1)}), bf16[64,2]{1,0:T(8,128)(2,1)}) %reduce-scatter.37.cloned.1.call-update) | async-done | bytes 272
  1423.7 8.8 psum.47
  1433.1 46.2 %all-reduce.3.cloned.1.call-done = (bf16[1,64,3072]{2,1,0:T(8,128)(2,1)}, bf16[1,64,1024]{2,1,0:T(8,128)(2,1)}, bf16[1,64,2816]{2,1,0:T(8,128)(2,1)}, bf16[1,64,2816]{2,1,0:T(8,128)(2,1)}, bf16[1,176,1024]{2,1,0:T(8,128)(2,1)}) async-done(((bf16[1,64,3072]{2,1,0:T(8,128)(2,1)}, bf16[1,64,1024]{2,1,0:T(8,128)(2,1)}, bf16[1,64,2816]{2,1,0:T(8,128)(2,1)}, bf16[1,64,2816]{2,1,0:T(8,128)(2,1)}, ...) | async-done | bytes 1605648 | tf_op jit(solution)/shard_map/psum | solution.py:500
  (449 shorter events, 290.7 us)
Async XLA Ops:
  7.2 9.7 copy-start.46
  7.2 9.7 copy-start.45
  7.2 35.2 %copy-start.19 = (bf16[1,2,1,64,1024]{4,3,2,1,0:T(8,128)(2,1)S(1)}, bf16[1,2,1,64,1024]{4,3,2,1,0:T(8,128)(2,1)}, u32[]{:S(2)}) copy-start(bf16[1,2,1,64,1024]{4,3,2,1,0:T(8,128)(2,1)} %param.56) | copy-start | bytes 786436
  7.2 68.8 %all-gather.12.cloned.1.call-start = ((), (), s32[]{:S(2)}) async-start(), calls=%async_computation.23 | async-start | bytes 6684672 | tf_op jit(solution)/shard_map/all_gather | solution.py:297
  9.2 112.8 %all-gather.14.cloned.1.call-start = ((), (), s32[]{:S(2)}) async-start(), calls=%async_computation.24 | async-start | bytes 2228224 | tf_op jit(solution)/shard_map/all_gather | solution.py:298
  10.9 173.0 %all-gather.16.cloned.1.call-start = ((), (), s32[]{:S(2)}) async-start(), calls=%async_computation.25 | async-start | bytes 6127616 | tf_op jit(solution)/shard_map/all_gather | solution.py:299
  12.9 232.2 %all-gather.18.cloned.1.call-start = ((), (), s32[]{:S(2)}) async-start(), calls=%async_computation.26 | async-start | bytes 6127616 | tf_op jit(solution)/shard_map/all_gather | solution.py:300
  14.8 291.4 %all-gather.20.cloned.1.call-start = ((), (), s32[]{:S(2)}) async-start(), calls=%async_computation.27 | async-start | bytes 6127616 | tf_op jit(solution)/shard_map/all_gather | solution.py:301
  16.8 580.9 %reduce-scatter.15.cloned.1.call-start = ((), (), s32[]{:S(2)}) async-start(), calls=%async_computation.12 | async-start | bytes 655360 | tf_op jit(solution)/shard_map/reduce_scatter | solution.py:428
  41.4 64.5 %copy-start.20 = (pred[64,256]{1,0:T(8,128)(4,1)}, pred[64,256]{1,0:T(8,128)(4,1)S(1)}, u32[]{:S(2)}) copy-start(pred[64,256]{1,0:T(8,128)(4,1)S(1)} %get-tuple-element.2318) | copy-start | bytes 49156
  84.2 245.2 %collective-permute-start.1 = (bf16[64,1024]{1,0:T(8,128)(2,1)}, bf16[64,1024]{1,0:T(8,128)(2,1)S(1)}, u32[]{:S(2)}, u32[]{:S(2)}) collective-permute-start(bf16[64,1024]{1,0:T(8,128)(2,1)} %get-tuple-element.1236), channel_id=1, source_target_pairs={{0,64},{1,65},{2,66},{3,67},{4,68},{5,69},{6,70},{7,71},{8,72},{9,... | collective-permute-start | bytes 393224 | tf_op jit(solution)/shard_map/ppermute | solution.py:16
  306.4 8.1 copy-start
  309.5 7.9 slice-start
  309.6 7.9 slice-start.1
  320.0 9.3 collective-permute-start
  336.0 21.9 %copy-start.26 = (bf16[64,1024]{1,0:T(8,128)(2,1)}, bf16[64,1024]{1,0:T(8,128)(2,1)S(1)}, u32[]{:S(2)}) copy-start(bf16[64,1024]{1,0:T(8,128)(2,1)S(1)} %get-tuple-element.1239) | copy-start | bytes 393220
  336.0 21.9 %copy-start.30 = (bf16[1,64,1024]{2,1,0:T(8,128)(2,1)}, bf16[1,64,1024]{2,1,0:T(8,128)(2,1)S(1)}, u32[]{:S(2)}) copy-start(bf16[1,64,1024]{2,1,0:T(8,128)(2,1)S(1)} %get-tuple-element.1245) | copy-start | bytes 393220
  336.0 67.0 %collective-permute-start.3 = (bf16[64,1024]{1,0:T(8,128)(2,1)}, bf16[64,1024]{1,0:T(8,128)(2,1)}, u32[]{:S(2)}, u32[]{:S(2)}) collective-permute-start(bf16[64,1024]{1,0:T(8,128)(2,1)} %get-tuple-element.1241), channel_id=1, source_target_pairs={{0,64},{1,65},{2,66},{3,67},{4,68},{5,69},{6,70},{7,71},{8,72},{9,... | collective-permute-start | bytes 393224 | tf_op jit(solution)/shard_map/ppermute | solution.py:16
  357.9 20.6 %copy-start.9 = (bf16[1,1024,1024]{2,1,0:T(8,128)(2,1)S(1)}, bf16[1,1024,1024]{2,1,0:T(8,128)(2,1)}, u32[]{:S(2)}) copy-start(bf16[1,1024,1024]{2,1,0:T(8,128)(2,1)} %all-gather.14.cloned.1.call-done) | copy-start | bytes 6291460
  378.5 14.8 copy-start.31
  378.5 7.3 copy-start.1
  380.9 7.9 slice-start.2
  380.9 7.9 slice-start.3
  391.3 10.6 copy-start.32
  391.3 10.6 collective-permute-start.2
  433.5 6.2 copy-start.34
  460.2 5.4 copy-start.39
  470.0 159.1 %reduce-scatter.17.cloned.1.call-start = ((), (), s32[]{:S(2)}) async-start(), calls=%async_computation.13 | async-start | bytes 655360 | tf_op jit(solution)/shard_map/reduce_scatter | solution.py:431
  472.1 284.5 %reduce-scatter.21.cloned.1.call-start = ((), (), s32[]{:S(2)}) async-start(), calls=%async_computation.15 | async-start | bytes 655360 | tf_op jit(solution)/shard_map/reduce_scatter | solution.py:431
  636.9 22.3 %copy-start.41 = (f32[1,1024]{1,0:T(1,128)}, f32[1,1024]{1,0:T(1,128)S(1)}, u32[]{:S(2)}) copy-start(f32[1,1024]{1,0:T(1,128)S(1)} %get-tuple-element.1299) | copy-start | bytes 12292
  636.9 21.3 %collective-permute-start.4 = (bf16[64,1024]{1,0:T(8,128)(2,1)}, bf16[64,1024]{1,0:T(8,128)(2,1)S(1)}, u32[]{:S(2)}, u32[]{:S(2)}) collective-permute-start(bf16[64,1024]{1,0:T(8,128)(2,1)} %get-tuple-element.1268), channel_id=1, source_target_pairs={{64,0},{65,1},{66,2},{67,3},{68,4},{69,5},{70,6},{71,7},{72,8},{73... | collective-permute-start | bytes 393224 | tf_op jit(solution)/shard_map/ppermute | solution.py:16
  659.2 5.1 copy-start.4
  659.2 7.1 copy-start.7
  668.4 12.4 copy-start.13
  686.8 5.9 copy-start.14
  727.0 61.0 %reduce-scatter.19.cloned.1.call-start = ((), (), s32[]{:S(2)}) async-start(), calls=%async_computation.14 | async-start | bytes 655360 | tf_op jit(solution)/shard_map/reduce_scatter | solution.py:428
  729.1 205.6 %reduce-scatter.25.cloned.1.call-start = ((), (), s32[]{:S(2)}) async-start(), calls=%async_computation.17 | async-start | bytes 655360 | tf_op jit(solution)/shard_map/reduce_scatter | solution.py:431
  729.2 28.4 %collective-permute-start.5 = (bf16[64,1024]{1,0:T(8,128)(2,1)}, bf16[64,1024]{1,0:T(8,128)(2,1)S(1)}, u32[]{:S(2)}, u32[]{:S(2)}) collective-permute-start(bf16[64,1024]{1,0:T(8,128)(2,1)} %get-tuple-element.1272), channel_id=1, source_target_pairs={{64,0},{65,1},{66,2},{67,3},{68,4},{69,5},{70,6},{71,7},{72,8},{73... | collective-permute-start | bytes 393224 | tf_op jit(solution)/shard_map/ppermute | solution.py:16
  797.3 8.5 copy-start.16
  800.7 5.2 copy-start.12
  807.3 7.1 copy-start.27
  807.3 7.1 copy-start.36
  814.4 7.2 copy-start.43
  814.4 7.2 copy-start.28
  814.4 7.2 copy-start.37
  814.4 6.2 collective-permute-start.6
  821.6 33.7 %copy-start.21 = (pred[64,256]{1,0:T(8,128)(4,1)S(1)}, pred[64,256]{1,0:T(8,128)(4,1)}, u32[]{:S(2)}) copy-start(pred[64,256]{1,0:T(8,128)(4,1)} %copy-done.20) | copy-start | bytes 49156
  821.9 5.1 copy-start.5
  821.9 7.1 copy-start.8
  831.1 12.4 copy-start.17
  849.4 5.9 copy-start.18
  878.6 60.5 %reduce-scatter.23.cloned.1.call-start = ((), (), s32[]{:S(2)}) async-start(), calls=%async_computation.16 | async-start | bytes 655360 | tf_op jit(solution)/shard_map/reduce_scatter | solution.py:428
  880.7 133.3 %reduce-scatter.29.cloned.1.call-start = ((), (), s32[]{:S(2)}) async-start(), calls=%async_computation.19 | async-start | bytes 2228224 | tf_op jit(solution)/shard_map/reduce_scatter | solution.py:483
  888.3 209.3 %reduce-scatter.31.cloned.1.call-start = ((), (), s32[]{:S(2)}) async-start(), calls=%async_computation.20 | async-start | bytes 6127616 | tf_op jit(solution)/shard_map/reduce_scatter | solution.py:486
  902.8 277.8 %reduce-scatter.33.cloned.1.call-start = ((), (), s32[]{:S(2)}) async-start(), calls=%async_computation.21 | async-start | bytes 6127616 | tf_op jit(solution)/shard_map/reduce_scatter | solution.py:489
  917.2 346.4 %reduce-scatter.35.cloned.1.call-start = ((), (), s32[]{:S(2)}) async-start(), calls=%async_computation.22 | async-start | bytes 6127616 | tf_op jit(solution)/shard_map/reduce_scatter | solution.py:492
  932.5 6.6 copy-start.10
  932.5 415.6 %reduce-scatter.27.cloned.1.call-start = ((), (), s32[]{:S(2)}) async-start(), calls=%async_computation.18 | async-start | bytes 6684672 | tf_op jit(solution)/shard_map/reduce_scatter | solution.py:480
  933.4 5.7 collective-permute-start.7
  971.4 376.7 %copy-start.29 = (bf16[64,1024]{1,0:T(8,128)(2,1)S(1)}, bf16[64,1024]{1,0:T(8,128)(2,1)}, u32[]{:S(2)}) copy-start(bf16[64,1024]{1,0:T(8,128)(2,1)} %copy-done.28) | copy-start | bytes 393220
  971.4 376.7 %copy-start.35 = (bf16[64,1024]{1,0:T(8,128)(2,1)S(1)}, bf16[64,1024]{1,0:T(8,128)(2,1)}, u32[]{:S(2)}) copy-start(bf16[64,1024]{1,0:T(8,128)(2,1)} %copy-done.34) | copy-start | bytes 393220
  971.5 376.7 %copy-start.33 = (bf16[64,1024]{1,0:T(8,128)(2,1)S(1)}, bf16[64,1024]{1,0:T(8,128)(2,1)}, u32[]{:S(2)}) copy-start(bf16[64,1024]{1,0:T(8,128)(2,1)} %copy-done.32) | copy-start | bytes 393220
  971.5 451.5 %reduce-scatter.37.cloned.1.call-start = ((), (), s32[]{:S(2)}) async-start(), calls=%async_computation.28 | async-start | bytes 278528
  973.1 506.2 %all-reduce.3.cloned.1.call-start = ((), (), s32[]{:S(2)}) async-start(), calls=%async_computation.29 | async-start | bytes 3211264 | tf_op jit(solution)/shard_map/psum | solution.py:500
  (8 other events, 5.6 us)
Sparse Core Ops, SparseCore 0:
  10.7 65.2 all-gather.11
  78.2 43.8 all-gather.13
  124.8 59.0 all-gather.15
  186.4 58.5 all-gather.17
  247.6 58.5 all-gather.19
  470.1 127.4 reduce-scatter.14
  601.0 28.0 reduce-scatter.16
  727.1 29.4 reduce-scatter.20
  760.0 27.9 reduce-scatter.18
  878.7 28.2 reduce-scatter.24
  910.4 27.9 reduce-scatter.22
  941.6 72.3 reduce-scatter.28
  1017.7 79.8 reduce-scatter.30
  1101.2 79.3 reduce-scatter.32
  1184.3 79.3 reduce-scatter.34
  1267.4 80.7 reduce-scatter.26
  1352.0 70.8 reduce-scatter.36
  1425.7 53.5 all-reduce.2
where the time goes:
time: 1510 us; the launch traced here: 1500 us
  waiting for transfers between devices  951 us (63%)
  matrix products  169 us (11%)
  other arithmetic  130 us (9%)
  local copies, waits for them, and re-layouts  124 us (8%)
  blocking collectives  91.7 us (6%)
  between operations  15.3 us (1%)
    reduce_scatter x3, waiting for transfers between devices, per_device(): lax.psum_scatter(grad_k_full.astype(jnp.bfloat16), 'ctx', scatter_dimensi...  154 us
    reduce_scatter x1, waiting for transfers between devices, per_device(): lax.psum_scatter(grad_totals[0].astype(jnp.bfloat16), 'dp', scatter_dimen...  84.4 us
    reduce_scatter x1, waiting for transfers between devices, per_device(): lax.psum_scatter(grad_totals[2].astype(jnp.bfloat16), 'dp', scatter_dimen...  83.6 us
    reduce_scatter x1, waiting for transfers between devices, per_device(): lax.psum_scatter(grad_totals[3].astype(jnp.bfloat16), 'dp', scatter_dimen...  83.1 us
    reduce_scatter x1, waiting for transfers between devices, per_device(): lax.psum_scatter(grad_totals[4].astype(jnp.bfloat16), 'dp', scatter_dimen...  83 us
    unnamed x19, waiting for transfers between devices  74.3 us
    all_gather x1, waiting for transfers between devices, per_device(): lax.all_gather(shards[2], 'dp', axis=0, tiled=True)  61.8 us
    all_gather x1, waiting for transfers between devices, per_device(): lax.all_gather(shards[3], 'dp', axis=0, tiled=True)  61.2 us
  transfers between devices with their start and end apart: 26, of which 19 were waited for; matrix products, arithmetic and copies ran while one was open for 13% of the time, Pallas kernels for 0%

commit v1 on v0

v1 whole, which is shorter than its diff:
```python
import jax
import jax.numpy as jnp
from jax import lax
from jax.experimental import pallas as pl
from jax.experimental.pallas import tpu as pltpu
from jax.sharding import PartitionSpec as P

T = 256
D = 1024
FF = 2816
FX = FF // 4
FP = 768
HX = 256
SH = 64
DR = 176
BT = 64
EPS = 1e-5
MESH = pl.DeviceIdType.MESH
BF = jnp.bfloat16
F32 = jnp.float32


def dot(a, b):
    return jnp.dot(a, b, preferred_element_type=F32)


def dot_nt(a, b):
    return lax.dot_general(a, b, (((1,), (1,)), ((), ())), preferred_element_type=F32)


def dot_tn(a, b):
    return lax.dot_general(a, b, (((0,), (0,)), ((), ())), preferred_element_type=F32)


N_SEM = 400
N_LOC = 24


def kernel(
    lengths, ends, q_src, o_src, gu_src, d_src, gain_src, cos_ref, sa_ref, sb_ref,
    oq_hbm, oo_hbm, ogu_hbm, od_hbm, edge_hbm, gsum_hbm,
    Wq, Wo, Wgu, Wd, Gn,
    E, X1, DY0, N1, N1s, N2, N2s, H, QKV, PR, O, Os, GU, M, Ms, DGU, DGUs, DP, DPs, DHB, DHBs, DYs, DH,
    PS, PRV,
    Gq, Go, Ggu, Gd, R1q, R1o, R1gu, R1d, R2q, R2o, R2gu, R2d, Sq, So, Sgu, Sd, OUTq, OUTo, OUTgu, OUTd,
    FSq, FSo, FSgu, FSd, GS, GR, TT, EO,
    ssem, rsem, lsem,
):
    s = lax.axis_index("section")
    dp = lax.axis_index("dp")
    c = lax.axis_index("ctx")
    xh = lax.div(c, 2)
    k = lax.rem(c, 2)
    x = xh * 2 + s
    z = lax.div(dp, 4)
    y = lax.rem(dp, 4)

    def dev(x_, y_, z_, k_):
        return (lax.rem(x_, 2), z_ * 4 + y_, lax.div(x_, 2) * 2 + k_)

    def ring(v):
        return [lax.rem(v + 1, 4), lax.rem(v + 3, 4), lax.rem(v + 2, 4)]

    X3, Y3, Z3 = ring(x), ring(y), ring(z)
    PX = [dev(v, y, z, k) for v in X3]
    PY = [dev(x, v, z, k) for v in Y3]
    PZ = [dev(x, y, v, k) for v in Z3]
    SIB = dev(x, y, z, 1 - k)

    bar = pltpu.get_barrier_semaphore()
    partners = PX + PY + PZ + [SIB]
    for p in partners:
        pl.semaphore_signal(bar, inc=1, device_id=p, device_id_type=MESH)
    pl.semaphore_wait(bar, len(partners))

    counter = [0, 0]
    sent = []

    def rc(src, dst, to, recv=None, cond=None, keep=True):
        i = counter[0]
        counter[0] += 1
        desc = pltpu.make_async_remote_copy(
            src_ref=src, dst_ref=dst, send_sem=ssem.at[i], recv_sem=rsem.at[i if recv is None else recv],
            device_id=to, device_id_type=MESH,
        )
        if keep:
            sent.append((cond, desc))
        return desc

    def push(src, dst, to):
        desc = rc(src, dst, to)
        desc.start()
        return desc

    def push3(srcs, dsts, to):
        return [push(a, b, t) for a, b, t in zip(srcs, dsts, to)]

    def wait_recv(descs):
        for desc in descs:
            desc.wait_recv()

    def flush():
        for cond, desc in sent:
            if cond is None:
                desc.wait_send()
            else:
                @pl.when(cond)
                def _(desc=desc):
                    desc.wait_send()
        sent.clear()

    def local(src, dst):
        i = counter[1]
        counter[1] += 1
        return pltpu.make_async_copy(src, dst, lsem.at[i])

    def half(width):
        return pl.ds(pl.multiple_of(k * (width // 2), 128), width // 2)

    def other_half(width):
        return pl.ds(pl.multiple_of((1 - k) * (width // 2), 128), width // 2)

    own = pl.ds(pl.multiple_of(x * BT, BT), BT)

    tx = lax.rem(x + 3 - 2 * k, 4)
    TO = dev(tx, y, z, k)
    REG = {"q": (Wq, 768), "o": (Wo, 1024), "gu": (Wgu, 2 * FP)}
    pre, loc = {}, {}

    def src_of(name, sl):
        if name == "q":
            return q_src.at[sl, :, half(768)]
        if name == "gu":
            return gu_src.at[sl, :, half(2 * FP)]
        return o_src.at[:, half(1024)]

    loc["g"] = local(gain_src, Gn.at[s, z, y])
    pre["g"] = rc(gain_src, Gn.at[s, z, y], TO)
    loc["g"].start()
    pre["g"].start()
    for name, (W, width) in REG.items():
        pre[name] = rc(src_of(name, tx), W.at[s, z, y, :, half(width)], TO)
        pre[name].start()
        loc[name] = local(src_of(name, x), W.at[s, z, y, :, half(width)])
        loc[name].start()
    down_rows = pl.ds(pl.multiple_of(y * DR, 16), DR)
    pre["d"] = rc(d_src.at[:, half(D)], Wd.at[s, down_rows, half(D)], TO, cond=(z == tx))
    loc["d"] = local(d_src.at[:, half(D)], Wd.at[s, down_rows, half(D)])

    @pl.when(z == tx)
    def _():
        pre["d"].start()

    @pl.when(z == x)
    def _():
        loc["d"].start()

    mine = pl.ds(pl.multiple_of(xh * 128 + k * 64, 64), 64)
    e_loc = local(ends.at[k], E.at[s, mine])
    e_loc.start()
    e_sib = push(ends.at[1 - k], E.at[s, mine], SIB)

    ag = {}

    def ready(l, name):
        @pl.when(s == l)
        def _():
            loc[name].wait()

        @pl.when(s != l)
        def _():
            pre[name].wait_recv()

    def ag1(l, name):
        if name == "d":
            descs = []
            for j in range(3):
                desc = rc(Wd.at[l, down_rows, half(D)], Wd.at[l, down_rows, half(D)], PZ[j],
                          recv=None if j == 0 else ag[l, "dz", "i"], cond=(z == x))
                if j == 0:
                    ag[l, "dz", "i"] = counter[0] - 1
                descs.append(desc)
            ag[l, "dz"] = descs

            @pl.when(z == x)
            def _():
                ready(l, "d")
                for desc in descs:
                    desc.start()
            return
        ready(l, name)
        if name == "g":
            ref = Gn.at[l, z, y]
            ag[l, name, 1] = (push3([ref] * 3, [ref] * 3, PY), [])
            return
        W, width = REG[name]
        a = W.at[l, z, y, pl.ds(0, 32), half(width)]
        b = W.at[l, z, y, pl.ds(32, 32), half(width)]
        ag[l, name, 1] = (push3([a] * 3, [a] * 3, PY), push3([b] * 3, [b] * 3, PZ))

    def ag2(l, name):
        if name == "d":
            @pl.when(z != x)
            def _():
                ag[l, "dz"][0].wait_recv()

            ref = Wd.at[l, down_rows, half(D)]
            ag[l, name, 2] = push3([ref] * 3, [ref] * 3, PY)
            return
        first = ag[l, name, 1]
        wait_recv(first[0])
        if name == "g":
            ref = Gn.at[l, z]
            ag[l, name, 2] = push3([ref] * 3, [ref] * 3, PZ)
            return
        W, width = REG[name]
        a = W.at[l, z, :, pl.ds(0, 32), half(width)]
        sent_a = push3([a] * 3, [a] * 3, PZ)
        wait_recv(first[1])
        b = W.at[l, :, y, pl.ds(32, 32), half(width)]
        ag[l, name, 2] = sent_a + push3([b] * 3, [b] * 3, PY)

    def ag3(l, name):
        wait_recv(ag[l, name, 2])
        if name == "g":
            return
        if name == "d":
            ref = Wd.at[l, pl.ds(0, FX), half(D)]
        else:
            W, width = REG[name]
            ref = W.at[l, :, :, :, half(width)]
        ag[l, name, 3] = push(ref, ref, SIB)

    def ag_done(l, name):
        wait_recv([ag[l, name, 3]])

    def gather_blocks(ref):
        return push3([ref] * 3, [ref] * 3, PX)

    def scatter_sums(i, value_of):
        for b in range(4):
            PS[i, b] = value_of(b)
        return push3([PS.at[i, v] for v in X3], [PRV.at[i, j] for j in range(3)], PX)

    def summed(i, descs):
        total = PS[i, x].astype(F32)
        for j, desc in enumerate(descs):
            desc.wait_recv()
            total = total + PRV[i, j].astype(F32)
        return total

    GRAD = {"q": (Gq, R1q, R2q, Sq, OUTq, FSq, 384), "o": (Go, R1o, R2o, So, OUTo, FSo, 128),
            "gu": (Ggu, R1gu, R2gu, Sgu, OUTgu, FSgu, FP)}
    rs = {}

    def rs1(l, name):
        if name == "d":
            rs[l, name, 1] = push3(
                [Gd.at[l, pl.ds(pl.multiple_of(v * DR, 16), DR)] for v in Y3], [R1d.at[l, j] for j in range(3)], PY)
            return
        G, R1, R2, S, OUT, FS, width = GRAD[name]
        a = push3([G.at[l, v, :, pl.ds(0, 32)] for v in Z3], [R1.at[l, 0, j] for j in range(3)], PZ)
        b = push3([G.at[l, :, v, pl.ds(32, 32)] for v in Y3], [R1.at[l, 1, j] for j in range(3)], PY)
        rs[l, name, 1] = (a, b)

    def rs2(l, name):
        first = rs[l, name, 1]
        if name == "d":
            wait_recv(first)
            Sd[l] = (Gd[l, down_rows].astype(F32) + R1d[l, 0].astype(F32) + R1d[l, 1].astype(F32)
                     + R1d[l, 2].astype(F32)).astype(BF)
            j_of = [lax.rem(x + 4 - z, 4) == 1, lax.rem(x + 4 - z, 4) == 3, lax.rem(x + 4 - z, 4) == 2]
            descs = []
            for j in range(3):
                desc = rc(Sd.at[l], R2d.at[l, j], PZ[j], cond=j_of[j])

                @pl.when(j_of[j])
                def _(desc=desc):
                    desc.start()
                descs.append(desc)
            rs[l, name, 2] = descs
            return
        G, R1, R2, S, OUT, FS, width = GRAD[name]
        wait_recv(first[0])
        S[l, 0] = (G[l, z, :, pl.ds(0, 32)].astype(F32) + R1[l, 0, 0].astype(F32) + R1[l, 0, 1].astype(F32)
                   + R1[l, 0, 2].astype(F32)).astype(BF)
        a = push3([S.at[l, 0, v] for v in Y3], [R2.at[l, 0, j] for j in range(3)], PY)
        wait_recv(first[1])
        S[l, 1] = (G[l, :, y, pl.ds(32, 32)].astype(F32) + R1[l, 1, 0].astype(F32) + R1[l, 1, 1].astype(F32)
                   + R1[l, 1, 2].astype(F32)).astype(BF)
        b = push3([S.at[l, 1, v] for v in Z3], [R2.at[l, 1, j] for j in range(3)], PZ)
        rs[l, name, 2] = (a, b)

    def rs3(l, name):
        second = rs[l, name, 2]
        if name == "d":
            idx = counter[0]
            far = rc(OUTd.at[k], OUTd.at[k], PX[2], cond=(z == x) & (s == l))
            near = [rc(FSd, OUTd.at[k], PX[j], recv=idx, cond=(z == x) & (s != l)) for j in range(2)]

            @pl.when(z == x)
            def _():
                wait_recv(second)
                total = (Sd[l].astype(F32) + R2d[l, 0].astype(F32) + R2d[l, 1].astype(F32)
                         + R2d[l, 2].astype(F32)).astype(BF)

                @pl.when(s == l)
                def _():
                    OUTd[k] = total
                    far.start()

                @pl.when(s != l)
                def _():
                    FSd[...] = total
                    for desc in near:
                        desc.start()
            rs[l, name, 3] = far
            return
        G, R1, R2, S, OUT, FS, width = GRAD[name]
        wait_recv(second[0])
        wait_recv(second[1])
        top = (S[l, 0, y].astype(F32) + R2[l, 0, 0].astype(F32) + R2[l, 0, 1].astype(F32)
               + R2[l, 0, 2].astype(F32)).astype(BF)
        low = (S[l, 1, z].astype(F32) + R2[l, 1, 0].astype(F32) + R2[l, 1, 1].astype(F32)
               + R2[l, 1, 2].astype(F32)).astype(BF)
        slot = OUT.at[k, x]
        far = rc(slot, slot, PX[2], cond=(s == l))
        near = [rc(FS, slot, PX[j], cond=(s != l)) for j in range(2)]

        @pl.when(s == l)
        def _():
            OUT[k, x, 0:32] = top
            OUT[k, x, 32:64] = low
            far.start()

        @pl.when(s != l)
        def _():
            FS[0:32] = top
            FS[32:64] = low
            for desc in near:
                desc.start()
        rs[l, name, 3] = [far] + near

    def rs4(l, name):
        third = rs[l, name, 3]
        if name == "d":
            ref = OUTd.at[k]
            fin = rc(ref, ref, SIB, cond=(s == l))

            @pl.when(s == l)
            def _():
                @pl.when(z != x)
                def _():
                    third.wait_recv()
                fin.start()
        else:
            ref = GRAD[name][4].at[k]
            fin = rc(ref, ref, SIB, cond=(s == l))

            @pl.when(s == l)
            def _():
                wait_recv(third)
                fin.start()
        rs[l, name, 4] = fin

    def rs5(l, name):
        @pl.when(s == l)
        def _():
            rs[l, name, 4].wait_recv()

    def edge(l, value):
        moved = rc(TT.at[l, s], TT.at[l, s], PX[0] if l == 1 else PX[1], cond=(s != l))
        TT[l, s] = value
        swap = rc(TT.at[l, 1 - k], EO.at[k], SIB, cond=(s == l))

        @pl.when(s != l)
        def _():
            moved.start()

        def finish():
            @pl.when(s == l)
            def _():
                moved.wait_recv()
                swap.start()
                EO[k] = TT[l, k]

        def done():
            @pl.when(s == l)
            def _():
                swap.wait_recv()
        return finish, done

    e0 = lengths[k, 0]
    e1 = e0 + lengths[k, 1]
    qi = lax.broadcasted_iota(jnp.int32, (T, T), 0)
    ki = lax.broadcasted_iota(jnp.int32, (T, T), 1)

    def doc(i):
        return jnp.where(i >= e0, 1, 0) + jnp.where(i >= e1, 1, 0)

    def allowed():
        return (doc(qi) == doc(ki)) & (ki <= qi)

    lane = lax.broadcasted_iota(jnp.int32, (T, 128), 1)

    def head(value, hh):
        return jnp.where((lane < 64) if hh == 0 else (lane >= 64), value, jnp.zeros_like(value))

    def rope(v):
        return v * cos_ref[...] + pltpu.roll(v, HX - 32, 1) * sa_ref[...] + pltpu.roll(v, 32, 1) * sb_ref[...]

    def rope_t(v):
        return v * cos_ref[...] - pltpu.roll(v, HX - 32, 1) * sa_ref[...] - pltpu.roll(v, 32, 1) * sb_ref[...]

    def gain(l, i):
        tiles = []
        for t in range(8):
            a = Gn[l, t // 2, 2 * (t % 2)].astype(F32) + Gn[l, t // 2, 2 * (t % 2) + 1].astype(F32)
            tiles.append(a[i : i + 1])
        return jnp.concatenate(tiles, axis=1)

    def mix(l):
        return 0.5 * l

    def norm_one(l, XR):
        g = gain(l, 0)
        for b in range(4):
            r = pl.ds(b * 64, 64)
            xf = XR[r, :].astype(F32)
            inv = lax.rsqrt(jnp.mean(xf * xf, axis=-1, keepdims=True) + EPS)
            N1[l, r, :] = (xf * inv * g).astype(BF)
        return push(N1.at[l], N1s.at[l], SIB)

    def wq(l):
        return Wq[l].reshape(D, 768)

    def project(l):
        n = N1[l]
        w = wq(l)
        QKV[l, 0] = rope(dot(n, w[:, 0:256])).astype(BF)
        QKV[l, 1] = rope(dot(n, w[:, 256:512])).astype(BF)
        v = dot(n, w[:, 512:768])
        if l == 1:
            v = 0.5 * v + 0.5 * QKV[0, 2].astype(F32)
        QKV[l, 2] = v.astype(BF)

    def attend(l):
        ok = allowed()
        for t in range(2):
            cols = pl.ds(128 * t, 128)
            qt, kt, vt = QKV[l, 0, :, cols], QKV[l, 1, :, cols], QKV[l, 2, :, cols]
            acc = jnp.zeros((T, 128), F32)
            for hh in range(2):
                sc = jnp.where(ok, dot_nt(head(qt, hh), kt) * 0.125, -1e30)
                ex = jnp.exp(sc - jnp.max(sc, axis=-1, keepdims=True))
                pr = (ex / jnp.sum(ex, axis=-1, keepdims=True)).astype(BF)
                PR[l, 2 * t + hh] = pr
                acc = acc + dot(pr, head(vt, hh))
            O[l, x, :, cols] = acc.astype(BF)
        got = gather_blocks(O.at[l, x])
        return got

    def hidden(l, XR, got):
        wait_recv(got)
        osib = push(O.at[l], Os.at[l], SIB)
        g = gain(l, 1)
        w = Wo[l].reshape(D, D)
        o = jnp.concatenate([O[l, b] for b in range(4)], axis=1)
        H[l] = XR[...].astype(F32) + dot(o, w)
        for b in range(4):
            r = pl.ds(b * 64, 64)
            hf = H[l, r, :]
            inv = lax.rsqrt(jnp.mean(hf * hf, axis=-1, keepdims=True) + EPS)
            N2[l, r, :] = (hf * inv * g).astype(BF)
        nsib = push(N2.at[l], N2s.at[l], SIB)
        return osib, nsib

    def gate_up(l):
        n = N2[l]
        GU[l, 0] = dot(n, Wgu[l, :, :, :, 0:FP].reshape(D, FP))
        GU[l, 1] = dot(n, Wgu[l, :, :, :, FP : 2 * FP].reshape(D, FP))
        for b in range(4):
            r = pl.ds(b * 64, 64)
            ga, up = GU[l, 0, r, :], GU[l, 1, r, :]
            M[l, r, :] = (ga * jax.nn.sigmoid(ga) * up).astype(BF)
        return push(M.at[l], Ms.at[l], SIB)

    def down(l, i):
        part = dot(M[l], Wd[l]).astype(BF)
        return scatter_sums(i, lambda b: part[b * 64 : (b + 1) * 64])

    def back_ff(l, DY, i):
        dy = DY[...]
        dm = dot_nt(dy, Wd[l])
        ga, up = GU[l, 0], GU[l, 1]
        sg = jax.nn.sigmoid(ga)
        DGU[l, 0] = (dm * up * sg * (1.0 + ga * (1.0 - sg))).astype(BF)
        DGU[l, 1] = (dm * ga * sg).astype(BF)
        sib = push(DGU.at[l, 1 - k], DGUs.at[l], SIB)
        part = (dot_nt(DGU[l, 0], Wgu[l, :, :, :, 0:FP].reshape(D, FP))
                + dot_nt(DGU[l, 1], Wgu[l, :, :, :, FP : 2 * FP].reshape(D, FP))).astype(BF)
        got = scatter_sums(i, lambda b: part[b * 64 : (b + 1) * 64])
        return sib, got

    def grads_ff(l, DY, msib, dysib, nsib, gsib):
        cols = half(D)
        wait_recv([msib, dysib])
        Gd[l] = (dot_tn(M[l], DY[:, cols]) + dot_tn(Ms[l], DYs[l])).astype(BF)
        rs1(l, "d")
        wait_recv([nsib, gsib])
        Ggu[l] = (dot_tn(N2[l], DGU[l, k]) + dot_tn(N2s[l], DGUs[l])).astype(BF).reshape(4, 4, SH, FP)
        rs1(l, "gu")

    def back_hidden(l, DY, i, got):
        dn = summed(i, got)
        hf = H[l, own, :]
        g = gain(l, 1)
        inv = lax.rsqrt(jnp.mean(hf * hf, axis=-1, keepdims=True) + EPS)
        GS[2 * l + 1 : 2 * l + 2] = jnp.sum(dn * hf * inv, axis=0, keepdims=True)
        e = dn * g
        dh = DY[own, :].astype(F32) + inv * e - hf * (inv * inv * inv) * jnp.mean(e * hf, axis=-1, keepdims=True)
        DH[l] = dh
        DHB[l, own, :] = dh.astype(BF)
        return gather_blocks(DHB.at[l, own])

    def back_attend(l, got, i):
        wait_recv(got)
        hs = pl.ds(pl.multiple_of(x * HX + (1 - k) * 128, 128), 128)
        hsib = push(DHB.at[l, :, hs], DHBs.at[l], SIB)
        do = dot_nt(DHB[l], Wo[l, x].reshape(HX, D)).astype(BF)
        dqs, dks, dvs = [], [], []
        for t in range(2):
            cols = pl.ds(128 * t, 128)
            qt, kt, vt = QKV[l, 0, :, cols], QKV[l, 1, :, cols], QKV[l, 2, :, cols]
            dot_ = do[:, 128 * t : 128 * (t + 1)]
            dq = dk = dv = jnp.zeros((T, 128), F32)
            for hh in range(2):
                pr = PR[l, 2 * t + hh]
                pf = pr.astype(F32)
                dom = head(dot_, hh)
                dpp = dot_nt(dom, vt)
                ds = (pf * (dpp - jnp.sum(pf * dpp, axis=-1, keepdims=True))).astype(BF)
                dq = dq + dot(ds, head(kt, hh))
                dk = dk + dot_tn(ds, head(qt, hh))
                dv = dv + dot_tn(pr, dom)
            dqs.append(dq)
            dks.append(dk)
            dvs.append(dv)
        dq = (jnp.concatenate(dqs, axis=1) * 0.125).astype(BF).astype(F32)
        dk = (jnp.concatenate(dks, axis=1) * 0.125).astype(BF).astype(F32)
        dv = jnp.concatenate(dvs, axis=1)
        DP[l, :, 0:256] = rope_t(dq).astype(BF)
        DP[l, :, 256:512] = rope_t(dk).astype(BF)
        if l == 1:
            dvt = dv.astype(BF)
            DP[l, :, 512:768] = (0.5 * dvt.astype(F32)).astype(BF)
        else:
            dvt = (dv + DP[1, :, 512:768].astype(F32)).astype(BF)
            DP[l, :, 512:768] = dvt
        psib = push(DP.at[l, :, other_half(768)], DPs.at[l], SIB)
        part = dot_nt(DP[l], wq(l)).astype(BF)
        got = scatter_sums(i, lambda b: part[b * 64 : (b + 1) * 64])
        return hsib, psib, got

    def grads_att(l, n1sib, osib, hsib, psib):
        wait_recv([n1sib, psib])
        Gq[l] = (dot_tn(N1[l], DP[l, :, half(768)]) + dot_tn(N1s[l], DPs[l])).astype(BF).reshape(4, 4, SH, 384)
        rs1(l, "q")
        wait_recv([osib, hsib])
        hs = pl.ds(pl.multiple_of(x * HX + k * 128, 128), 128)
        for b in range(4):
            Go[l, b] = (dot_tn(O[l, b], DHB[l, :, hs]) + dot_tn(Os[l, b], DHBs[l])).astype(BF).reshape(4, SH, 128)
        rs1(l, "o")

    def back_input(l, XR, i, got):
        dn = summed(i, got)
        xf = XR[own, :].astype(F32)
        g = gain(l, 0)
        inv = lax.rsqrt(jnp.mean(xf * xf, axis=-1, keepdims=True) + EPS)
        GS[2 * l : 2 * l + 1] = jnp.sum(dn * xf * inv, axis=0, keepdims=True)
        e = dn * g
        dx = DH[l] + inv * e - xf * (inv * inv * inv) * jnp.mean(e * xf, axis=-1, keepdims=True)
        return dx.astype(BF)

    X0 = E.at[0]
    DY1 = E.at[1]
    GS[...] = jnp.zeros_like(GS)
    for l in range(2):
        Wd[l, FX:FP, :] = jnp.zeros((FP - FX, D), BF)
    for name in ("g", "q", "o", "gu", "d"):
        ag1(0, name)
    e_loc.wait()
    e_sib.wait_recv()
    mine2 = pl.ds(pl.multiple_of(xh * 128, 128), 128)
    e_got = push3([E.at[s, mine2]] * 3, [E.at[s, mine2]] * 3, PX)
    ag2(0, "g")
    ag2(0, "q")
    ag2(0, "o")
    ag2(0, "gu")
    ag2(0, "d")
    ag3(0, "g")
    wait_recv(e_got)
    dysib = [None, push(DY1.at[:, other_half(D)], DYs.at[1], SIB)]
    n1sib = [norm_one(0, X0), None]
    ag3(0, "q")
    ag_done(0, "q")
    project(0)
    got = attend(0)
    for name in ("g", "q", "o", "gu", "d"):
        ag1(1, name)
    ag3(0, "o")
    ag3(0, "gu")
    ag3(0, "d")
    ag_done(0, "o")
    osib, nsib, msib = [None, None], [None, None], [None, None]
    osib[0], nsib[0] = hidden(0, X0, got)
    ag_done(0, "gu")
    msib[0] = gate_up(0)
    ag_done(0, "d")
    got = down(0, 0)
    for name in ("g", "q", "o", "gu", "d"):
        ag2(1, name)
    X1[own, :] = (summed(0, got) + H[0, own, :]).astype(BF)
    got = gather_blocks(X1.at[own])
    for name in ("g", "q", "o", "gu", "d"):
        ag3(1, name)
    wait_recv(got)
    n1sib[1] = norm_one(1, X1)
    ag_done(1, "q")
    project(1)
    got = attend(1)
    ag_done(1, "o")
    osib[1], nsib[1] = hidden(1, X1, got)
    ag_done(1, "gu")
    msib[1] = gate_up(1)
    ag_done(1, "d")
    y_got = down(1, 1)

    gsib, got = back_ff(1, DY1, 2)
    y_fin, y_done = edge(1, (summed(1, y_got) + H[1, own, :]).astype(BF))
    grads_ff(1, DY1, msib[1], dysib[1], nsib[1], gsib)
    got = back_hidden(1, DY1, 2, got)
    y_fin()
    hsib, psib, got = back_attend(1, got, 3)
    grads_att(1, n1sib[1], osib[1], hsib, psib)
    DY0[own, :] = back_input(1, X1, 3, got)
    got = gather_blocks(DY0.at[own])
    rs2(1, "d")
    rs2(1, "gu")
    wait_recv(got)
    dysib[0] = push(DY0.at[:, other_half(D)], DYs.at[0], SIB)

    gsib, got = back_ff(0, DY0, 4)
    rs2(1, "q")
    rs2(1, "o")
    grads_ff(0, DY0, msib[0], dysib[0], nsib[0], gsib)
    rs3(1, "d")
    rs3(1, "gu")
    got = back_hidden(0, DY0, 4, got)
    rs3(1, "q")
    rs3(1, "o")
    hsib, psib, got = back_attend(0, got, 5)
    rs2(0, "d")
    rs2(0, "gu")
    grads_att(0, n1sib[0], osib[0], hsib, psib)
    for name in ("d", "gu", "q", "o"):
        rs4(1, name)
    dx = back_input(0, X0, 5, got)
    x_fin, x_done = edge(0, dx)

    def gsum(i, to):
        descs = push3([GS] * len(to), [GR.at[i, j] for j in range(len(to))], to)
        for desc in descs:
            desc.wait()
        del sent[len(sent) - len(descs):]
        total = GS[...]
        for j in range(len(to)):
            total = total + GR[i, j]
        GS[...] = total

    gsum(0, PX)
    rs2(0, "q")
    rs2(0, "o")
    rs3(0, "d")
    rs3(0, "gu")
    gsum(1, PY)
    x_fin()
    gsum(2, PZ)
    rs3(0, "q")
    rs3(0, "o")
    gsum(3, [SIB])
    for name in ("d", "gu", "q", "o"):
        rs4(0, name)
    for name in ("d", "gu", "q", "o"):
        rs5(1, name)
        rs5(0, name)
    x_done()
    y_done()
    outs = [local(a, b) for a, b in
            ((OUTq, oq_hbm), (OUTo, oo_hbm), (OUTgu, ogu_hbm), (OUTd, od_hbm), (EO, edge_hbm), (GS, gsum_hbm))]
    for o in outs:
        o.start()
    flush()
    for o in outs:
        o.wait()


def run_kernel(lengths, ends, q_src, o_src, gu_src, d_src, gain_src, cos, sa, sb):
    V = pltpu.VMEM
    sh = jax.ShapeDtypeStruct
    any_ = pl.BlockSpec(memory_space=pl.ANY)
    vm = pl.BlockSpec(memory_space=pltpu.VMEM)
    out_shape = [
        sh((2, 4, SH, 384), BF), sh((2, 4, SH, 128), BF), sh((2, 4, SH, FP), BF), sh((2, DR, 512), BF),
        sh((2, BT, D), BF), sh((8, D), F32),
    ]
    scratch = [
        V((2, 4, 4, SH, 768), BF), V((2, 4, 4, SH, D), BF), V((2, 4, 4, SH, 2 * FP), BF), V((2, FP, D), BF),
        V((2, 4, 4, 16, 128), BF),
        V((2, T, D), BF), V((T, D), BF), V((T, D), BF),
        V((2, T, D), BF), V((2, T, D), BF), V((2, T, D), BF), V((2, T, D), BF),
        V((2, T, D), F32), V((2, 3, T, HX), BF), V((2, 4, T, T), BF),
        V((2, 4, T, HX), BF), V((2, 4, T, HX), BF),
        V((2, 2, T, FP), F32), V((2, T, FP), BF), V((2, T, FP), BF),
        V((2, 2, T, FP), BF), V((2, T, FP), BF),
        V((2, T, 768), BF), V((2, T, 384), BF),
        V((2, T, D), BF), V((2, T, 128), BF), V((2, T, 512), BF), V((2, BT, D), F32),
        V((6, 4, BT, D), BF), V((6, 3, BT, D), BF),
        V((2, 4, 4, SH, 384), BF), V((2, 4, 4, SH, 128), BF), V((2, 4, 4, SH, FP), BF), V((2, FP, 512), BF),
        V((2, 2, 3, 4, 32, 384), BF), V((2, 2, 3, 4, 32, 128), BF), V((2, 2, 3, 4, 32, FP), BF),
        V((2, 3, DR, 512), BF),
        V((2, 2, 3, 32, 384), BF), V((2, 2, 3, 32, 128), BF), V((2, 2, 3, 32, FP), BF), V((2, 3, DR, 512), BF),
        V((2, 2, 4, 32, 384), BF), V((2, 2, 4, 32, 128), BF), V((2, 2, 4, 32, FP), BF), V((2, DR, 512), BF),
        V((2, 4, SH, 384), BF), V((2, 4, SH, 128), BF), V((2, 4, SH, FP), BF), V((2, DR, 512), BF),
        V((SH, 384), BF), V((SH, 128), BF), V((SH, FP), BF), V((DR, 512), BF),
        V((8, D), F32), V((4, 3, 8, D), F32), V((2, 2, BT, D), BF), V((2, BT, D), BF),
        pltpu.SemaphoreType.DMA((N_SEM,)), pltpu.SemaphoreType.DMA((N_SEM,)), pltpu.SemaphoreType.DMA((N_LOC,)),
    ]
    return pl.pallas_call(
        kernel,
        out_shape=out_shape,
        in_specs=[pl.BlockSpec(memory_space=pltpu.SMEM)] + [any_] * 6 + [vm] * 3,
        out_specs=[any_] * 6,
        scratch_shapes=scratch,
        name="two_layers",
        compiler_params=pltpu.CompilerParams(
            collective_id=0, has_side_effects=True, vmem_limit_bytes=64 * 1024 * 1024 - 65536
        ),
    )(lengths, ends, q_src, o_src, gu_src, d_src, gain_src, cos, sa, sb)


def tables(doc_lengths):
    ends = jnp.cumsum(doc_lengths)
    i = jnp.arange(T, dtype=jnp.int32)
    start = jnp.where(i >= ends[1], ends[1], jnp.where(i >= ends[0], ends[0], 0))
    pos = (i - start).astype(F32)
    lane = jnp.arange(HX, dtype=jnp.int32) % 64
    freq = 10000.0 ** (-(lane % 32).astype(F32) / 32.0)
    phase = pos[:, None] * freq[None, :]
    cos, sin = jnp.cos(phase), jnp.sin(phase)
    first = (lane < 32)[None, :]
    return cos, jnp.where(first, -sin, 0.0), jnp.where(first, 0.0, sin)


def per_device(ends_in, lengths, qkv_w, out_w, gate_w, up_w, down_w, gains):
    s = lax.axis_index("section")
    d = lax.axis_index("dp")
    k = lax.rem(lax.axis_index("ctx"), 2)
    ends = ends_in[0, :, 0]
    doc = lengths[:, 0]
    q_src = qkv_w[0].astype(BF).reshape(SH, 3, 4, HX).transpose(2, 0, 1, 3).reshape(4, SH, 768)

    def ff_slices(w):
        return jnp.pad(w.astype(BF).reshape(SH, 4, FX), ((0, 0), (0, 0), (0, FP - FX))).transpose(1, 0, 2)

    gu_src = jnp.concatenate([ff_slices(gate_w[0]), ff_slices(up_w[0])], axis=2)
    o_src = out_w[0].astype(BF)
    d_src = down_w[0].astype(BF)
    gb = gains[0].astype(BF)
    odd = lax.rem(d, 2) == 1
    gain_src = jnp.where(odd, jnp.pad(gb, ((0, 14), (64, 0))), jnp.pad(gb, ((0, 14), (0, 64))))
    cos, sa, sb = tables(lax.dynamic_index_in_dim(doc, k, 0, keepdims=False))
    oq, oo, ogu, od, edge, gsum = run_kernel(doc, ends, q_src, o_src, gu_src, d_src, gain_src, cos, sa, sb)
    qkv = oq.transpose(2, 1, 0, 3).reshape(SH, 4, 3, HX).transpose(0, 2, 1, 3).reshape(SH, 3 * D).astype(F32)
    out = oo.transpose(2, 1, 0, 3).reshape(SH, D).astype(F32)
    gate = ogu[0].transpose(1, 0, 2)[:, :, :FX].reshape(SH, FF).astype(F32)
    up = ogu[1].transpose(1, 0, 2)[:, :, :FX].reshape(SH, FF).astype(F32)
    down = od.transpose(1, 0, 2).reshape(DR, D).astype(F32)
    gg = lax.dynamic_slice(gsum, (2 * s, d * SH), (2, SH))
    return edge[None, :, None], qkv[None], out[None], gate[None], up[None], down[None], gg[None]


def solution(mesh):
    in_specs = (
        P("section", None, "dp", "ctx", None),
        P(None, "dp", None),
        P("section", "dp", None),
        P("section", "dp", None),
        P("section", "dp", None),
        P("section", "dp", None),
        P("section", "dp", None),
        P("section", None, "dp"),
    )
    out_specs = (
        P("section", None, "dp", "ctx", None),
        P("section", "dp", None),
        P("section", "dp", None),
        P("section", "dp", None),
        P("section", "dp", None),
        P("section", "dp", None),
        P("section", None, "dp"),
    )
    return jax.shard_map(per_device, mesh=mesh, in_specs=in_specs, out_specs=out_specs, check_vma=False)
```

time: 1510 us -> 227 us (0.15)
  waiting for transfers between devices: 951 us -> 0 us
  Pallas kernels: 0 us -> 199 us
  matrix products: 169 us -> 0 us
  other arithmetic: 130 us -> 10.5 us
  local copies, waits for them, and re-layouts: 124 us -> 16.4 us
  blocking collectives: 91.7 us -> 0 us
    reduce_scatter x11 -> x0, waiting for transfers between devices: 586 us -> none  [the longest x3 154 us: per_device(): lax.psum_scatter(grad_k_full.astype(jnp.bfloat16), 'ctx', scatter_dimensi...]
    all_gather x5 -> x0, waiting for transfers between devices: 215 us -> none  [the longest x1 61.8 us: per_device(): lax.all_gather(shards[2], 'dp', axis=0, tiled=True)]
    pallas_call x0 -> x1, Pallas kernels: none -> 199 us  [run_kernel(): pl.pallas_call(kernel, out_shape=out_shape, in_specs=[pl.BlockSpec(memory...]
    dot_general x86 -> x0, matrix products: 169 us -> none  [the longest x10 59.3 us: matmul_left_t(): lax.dot_general(left, right, (((0,), (0,)), ((), ())), preferred_element_...]
    convert_element_type x35 -> x12, other arithmetic: 92.9 us -> 6.85 us  [the longest x1 1.62 us: per_device(): o_src = out_w[0].astype(BF)]
    all_gather x7 -> x0, blocking collectives: 82.9 us -> none  [the longest x3 31.5 us: per_device(): lax.all_gather(value_part, 'ctx', axis=0, tiled=True)]
    unnamed x19 -> x0, waiting for transfers between devices: 74.3 us -> none
    another operation x41 -> x0, local copies, waits for them, and re-layouts: 62.9 us -> none
  transfers between devices with their start and end apart: 26 -> 0, of which waited for: 19 -> 0; matrix products, arithmetic and copies ran while one was open for 13% -> 0% of each run, Pallas kernels for 0% -> 0%
where the time goes in v1:
time: 227 us
  Pallas kernels  199 us (88%)
  local copies, waits for them, and re-layouts  16.4 us (7%)
  other arithmetic  10.5 us (5%)
    pallas_call x1, Pallas kernels, run_kernel(): pl.pallas_call(kernel, out_shape=out_shape, in_specs=[pl.BlockSpec(memory...  199 us

profile of v1, /device:TPU:1, one launch (start us, length us, event | category | flops | bytes accessed | tf_op | source)
XLA Modules:
  0.0 226.9 jit_solution(9974888315543895327)
XLA Ops:
  0.6 0.7 dynamic-slice_bitcast_fusion.1
  1.3 0.2 reduce-window.4
  1.5 0.7 convert_bitcast_fusion.5
  2.2 0.6 fusion.10
  2.8 1.3 fusion.4
  4.1 0.7 pad_select_fusion.gain_src
  4.7 1.6 convert_bitcast_fusion.4.o_src
  6.4 0.0 copy-start.2
  6.4 1.2 convert_element_type.142
  7.6 0.5 convert_element_type.143
  8.1 0.0 copy-done.2
  8.2 0.5 convert_element_type.145
  8.7 0.1 pad_bitcast_fusion
  8.8 0.0 copy-start.3
  8.8 0.0 copy-start
  8.8 0.9 pad_maximum_fusion.gu_src
  9.7 0.4 copy-done.3
  10.2 0.8 convert_bitcast_fusion.2.d_src
  10.9 0.0 copy-done
  11.0 0.3 convert_element_type.139
  11.3 0.2 copy.37
  11.5 1.2 reshape.146.q_src
  12.7 1.8 fusion
  14.5 199.1 %two_layers.1 = (bf16[2,4,64,384]{3,2,1,0:T(8,128)(2,1)}, bf16[2,4,64,128]{3,2,1,0:T(8,128)(2,1)}, bf16[2,4,64,768]{3,2,1,0:T(8,128)(2,1)}, bf16[2,176,512]{2,1,...) custom-call(s32[2,3]{1,0:T(2,128)} %bitcast.43, bf16[2,64,1024]{2,1,0:T(8,128)(2,1)} %bitcast.41, ...), custom_call_target="tpu_custom_call" | custom-call | tf_op jit(solution)/shard_map/two_layers/pallas_call | solution.py:739
  213.7 0.0 copy-start.5
  213.7 1.4 dynamic-slice_bitcast_fusion
  215.1 0.9 convert_bitcast_fusion.3
  216.0 0.2 copy.31
  216.2 0.9 reshape.149
  217.1 0.0 copy-done.5
  217.1 0.1 convert_bitcast_fusion.1
  217.2 0.6 copy.34
  217.8 0.0 copy-start.4
  217.8 1.5 reshape.152
  219.2 0.0 copy-done.4
  219.2 0.1 convert_bitcast_fusion
  219.3 0.6 copy.29
  219.9 0.8 reshape.153
  220.7 0.2 copy.30
  221.0 0.0 copy-start.1
  221.0 1.3 reshape.148
  222.2 0.0 copy-done.1
  222.2 0.1 slice_bitcast_fusion
  222.3 0.1 slice_convert_fusion
  222.4 0.5 copy.33
  222.9 1.4 reshape.151
  224.3 0.1 slice_convert_fusion.1
  224.3 0.5 copy.32
  224.9 0.0 copy-start.6
  224.9 1.4 reshape.150
  226.2 0.0 copy-done.6
  226.2 0.7 copy.39
  (6 shorter events, 0.2 us)
Async XLA Ops:
  6.4 1.7 copy-start.2
  8.8 1.4 copy-start.3
  8.8 2.2 copy-start
  213.7 3.4 %copy-start.5 = (bf16[2,176,512]{2,1,0:T(8,128)(2,1)S(1)}, bf16[2,176,512]{2,1,0:T(8,128)(2,1)}, u32[]{:S(2)}) copy-start(bf16[2,176,512]{2,1,0:T(8,128)(2,1)} %get-tuple-element.17) | copy-start | bytes 1081348
  217.8 1.5 copy-start.4
  221.0 1.3 copy-start.1
  224.9 1.4 copy-start.6

commit v2 on v1

--- a/solution.py
+++ b/solution.py
@@ -32,13 +32,15 @@
     return lax.dot_general(a, b, (((0,), (0,)), ((), ())), preferred_element_type=F32)
 
 
-N_SEM = 400
-N_LOC = 24
+N_SEND = 64
+N_RECV = 264
+N_LOC = 12
+GROUP_BYTES = 4 * 1024 * 1024
 
 
 def kernel(
     lengths, ends, q_src, o_src, gu_src, d_src, gain_src, cos_ref, sa_ref, sb_ref,
-    oq_hbm, oo_hbm, ogu_hbm, od_hbm, edge_hbm, gsum_hbm,
+    oq_hbm, oo_hbm, ogu_hbm, od_hbm, edge_hbm, gsum_hbm, dummy,
     Wq, Wo, Wgu, Wd, Gn,
     E, X1, DY0, N1, N1s, N2, N2s, H, QKV, PR, O, Os, GU, M, Ms, DGU, DGUs, DP, DPs, DHB, DHBs, DYs, DH,
     PS, PRV,
@@ -73,22 +75,41 @@
         pl.semaphore_signal(bar, inc=1, device_id=p, device_id_type=MESH)
     pl.semaphore_wait(bar, len(partners))
 
-    counter = [0, 0]
+    counter = [0, 0, 0]
     sent = []
-
-    def rc(src, dst, to, recv=None, cond=None, keep=True):
-        i = counter[0]
+    groups = []
+
+    def size(ref):
+        n = 2 if ref.dtype == BF else 4
+        for v in ref.shape:
+            n *= v
+        return n
+
+    def new_recv():
         counter[0] += 1
+        return counter[0] - 1
+
+    def rc(src, dst, to, recv=None, cond=None):
+        recv = new_recv() if recv is None else recv
+        if cond is None:
+            if not groups or groups[-1][1] + size(src) > GROUP_BYTES:
+                groups.append([counter[2], 0])
+                counter[2] += 1
+            groups[-1][1] += size(src)
+            i = groups[-1][0]
+        else:
+            i = counter[2]
+            counter[2] += 1
         desc = pltpu.make_async_remote_copy(
-            src_ref=src, dst_ref=dst, send_sem=ssem.at[i], recv_sem=rsem.at[i if recv is None else recv],
+            src_ref=src, dst_ref=dst, send_sem=ssem.at[i], recv_sem=rsem.at[recv],
             device_id=to, device_id_type=MESH,
         )
-        if keep:
+        if cond is not None:
             sent.append((cond, desc))
         return desc
 
-    def push(src, dst, to):
-        desc = rc(src, dst, to)
+    def push(src, dst, to, recv=None):
+        desc = rc(src, dst, to, recv)
         desc.start()
         return desc
 
@@ -99,15 +120,74 @@
         for desc in descs:
             desc.wait_recv()
 
+    def wait_bytes(ref, recv):
+        pltpu.make_async_remote_copy(
+            src_ref=ref, dst_ref=ref, send_sem=ssem.at[0], recv_sem=rsem.at[recv], device_id=SIB, device_id_type=MESH,
+        ).wait_recv()
+
     def flush():
+        for i, total in groups:
+            ref = dummy.at[pl.ds(0, total // 4096)]
+            pltpu.make_async_copy(ref, ref, ssem.at[i]).wait()
         for cond, desc in sent:
-            if cond is None:
+            @pl.when(cond)
+            def _(desc=desc):
                 desc.wait_send()
-            else:
-                @pl.when(cond)
-                def _(desc=desc):
-                    desc.wait_send()
-        sent.clear()
+
+    class Gather:
+        def __init__(self, ring, blk, both):
+            (self.p, self.m, self.o), self.me, self.P, self.M = ring
+            self.blk, self.both = blk, both
+
+        def a(self):
+            self.r = [new_recv() for _ in range(3)]
+            h0, h1 = self.blk(self.me, 0), self.blk(self.me, 1)
+            push(h0, h0, self.P, self.r[0])
+            push(h1, h1, self.M, self.r[1])
+            push(h1, h1, self.P, self.r[2])
+            push(h0, h0, self.M, self.r[2])
+            return self
+
+        def b(self):
+            left, right = self.blk(self.m, 0), self.blk(self.p, 1)
+            wait_bytes(left, self.r[0])
+            push(left, left, self.P, self.r[2])
+            wait_bytes(right, self.r[1])
+            push(right, right, self.M, self.r[2])
+            return self
+
+        def c(self):
+            wait_bytes(self.both, self.r[2])
+
+    class Reduce:
+        def __init__(self, ring, part, buf, both):
+            (self.p, self.m, self.o), self.me, self.P, self.M = ring
+            self.part, self.buf, self.both = part, buf, both
+
+        def a(self):
+            self.r = [new_recv() for _ in range(3)]
+            part, buf = self.part, self.buf
+            push(part(self.o, 0), buf(0, 0), self.P, self.r[0])
+            push(part(self.o, 1), buf(0, 1), self.M, self.r[1])
+            push(part(self.p, 1), buf(1, 1), self.P, self.r[2])
+            push(part(self.m, 0), buf(2, 0), self.M, self.r[2])
+            return self
+
+        def b(self):
+            part, buf = self.part, self.buf
+            for h, j, to in ((0, self.p, self.P), (1, self.m, self.M)):
+                ref, got = part(j, h), buf(0, h)
+                wait_bytes(got, self.r[h])
+                ref[...] = (ref[...].astype(F32) + got[...].astype(F32)).astype(BF)
+                push(ref, buf(1 + h, h), to, self.r[2])
+            return self
+
+        def c(self):
+            wait_bytes(self.both, self.r[2])
+
+    RX = ((X3[0], X3[1], X3[2]), x, PX[0], PX[1])
+    RY = ((Y3[0], Y3[1], Y3[2]), y, PY[0], PY[1])
+    RZ = ((Z3[0], Z3[1], Z3[2]), z, PZ[0], PZ[1])
 
     def local(src, dst):
         i = counter[1]
@@ -171,59 +251,96 @@
         def _():
             pre[name].wait_recv()
 
-    def ag1(l, name):
+    def rows16(base, h):
+        return pl.ds(base + 16 * h, 16)
+
+    def quarter(h):
+        return pl.ds(pl.multiple_of(k * 512 + h * 256, 128), 256)
+
+    is_src, is_p, is_m, is_f = z == x, z == X3[0], z == X3[1], z == X3[2]
+
+    def s1a(l, name):
         if name == "d":
-            descs = []
-            for j in range(3):
-                desc = rc(Wd.at[l, down_rows, half(D)], Wd.at[l, down_rows, half(D)], PZ[j],
-                          recv=None if j == 0 else ag[l, "dz", "i"], cond=(z == x))
-                if j == 0:
-                    ag[l, "dz", "i"] = counter[0] - 1
-                descs.append(desc)
-            ag[l, "dz"] = descs
-
-            @pl.when(z == x)
+            ref = Wd.at[l, down_rows, half(D)]
+            idx = new_recv()
+            up = rc(ref, ref, PZ[0], recv=idx, cond=is_src)
+            dn = rc(ref, ref, PZ[1], recv=idx, cond=is_src)
+
+            @pl.when(is_src)
             def _():
                 ready(l, "d")
-                for desc in descs:
-                    desc.start()
+                up.start()
+                dn.start()
+            ag[l, "d", 1] = up, idx
             return
         ready(l, name)
         if name == "g":
             ref = Gn.at[l, z, y]
-            ag[l, name, 1] = (push3([ref] * 3, [ref] * 3, PY), [])
+            ag[l, name, 1] = new_recv()
+            for to in PY:
+                push(ref, ref, to, ag[l, name, 1])
             return
         W, width = REG[name]
-        a = W.at[l, z, y, pl.ds(0, 32), half(width)]
-        b = W.at[l, z, y, pl.ds(32, 32), half(width)]
-        ag[l, name, 1] = (push3([a] * 3, [a] * 3, PY), push3([b] * 3, [b] * 3, PZ))
-
-    def ag2(l, name):
+        cols = half(width)
+        ag[l, name, 1] = (
+            Gather(RY, lambda j, h: W.at[l, z, j, rows16(0, h), cols], W.at[l, z, pl.ds(0, 2), pl.ds(0, 32), cols]).a(),
+            Gather(RZ, lambda j, h: W.at[l, j, y, rows16(32, h), cols], W.at[l, pl.ds(0, 2), y, pl.ds(0, 32), cols]).a(),
+        )
+
+    def s1b(l, name):
+        if name == "g":
+            return
+        first = ag[l, name, 1]
         if name == "d":
-            @pl.when(z != x)
+            got, idx = first
+            h0, h1 = Wd.at[l, down_rows, quarter(0)], Wd.at[l, down_rows, quarter(1)]
+            to_f = [rc(h0, h0, PZ[0], recv=idx, cond=is_p), rc(h1, h1, PZ[1], recv=idx, cond=is_m)]
+            for cond, desc in zip((is_p, is_m), to_f):
+                @pl.when(cond)
+                def _(desc=desc):
+                    got.wait_recv()
+                    desc.start()
+            return
+        first[0].b()
+        first[1].b()
+
+    def s2a(l, name):
+        first = ag[l, name, 1]
+        if name == "g":
+            wait_bytes(Gn.at[l, z, pl.ds(0, 3)], first)
+            ref = Gn.at[l, z]
+            ag[l, name, 2] = new_recv()
+            for to in PZ:
+                push(ref, ref, to, ag[l, name, 2])
+            return
+        if name == "d":
+            @pl.when(is_f)
             def _():
-                ag[l, "dz"][0].wait_recv()
-
-            ref = Wd.at[l, down_rows, half(D)]
-            ag[l, name, 2] = push3([ref] * 3, [ref] * 3, PY)
-            return
-        first = ag[l, name, 1]
-        wait_recv(first[0])
+                first[0].wait_recv()
+
+            def blk(j, h):
+                return Wd.at[l, pl.ds(pl.multiple_of(j * DR, 16), DR), quarter(h)]
+            ag[l, name, 2] = (Gather(RY, blk, Wd.at[l, pl.ds(0, 2 * DR), half(D)]).a(),)
+            return
+        W, width = REG[name]
+        cols = half(width)
+        first[0].c()
+        ga = Gather(RZ, lambda j, h: W.at[l, j, :, rows16(0, h), cols], W.at[l, pl.ds(0, 2), :, pl.ds(0, 32), cols]).a()
+        first[1].c()
+        gb = Gather(RY, lambda j, h: W.at[l, :, j, rows16(32, h), cols], W.at[l, :, pl.ds(0, 2), pl.ds(0, 32), cols]).a()
+        ag[l, name, 2] = (ga, gb)
+
+    def s2b(l, name):
+        if name != "g":
+            for g in ag[l, name, 2]:
+                g.b()
+
+    def s3(l, name):
         if name == "g":
-            ref = Gn.at[l, z]
-            ag[l, name, 2] = push3([ref] * 3, [ref] * 3, PZ)
-            return
-        W, width = REG[name]
-        a = W.at[l, z, :, pl.ds(0, 32), half(width)]
-        sent_a = push3([a] * 3, [a] * 3, PZ)
-        wait_recv(first[1])
-        b = W.at[l, :, y, pl.ds(32, 32), half(width)]
-        ag[l, name, 2] = sent_a + push3([b] * 3, [b] * 3, PY)
-
-    def ag3(l, name):
-        wait_recv(ag[l, name, 2])
-        if name == "g":
-            return
+            wait_bytes(Gn.at[l, pl.ds(0, 3)], ag[l, name, 2])
+            return
+        for g in ag[l, name, 2]:
+            g.c()
         if name == "d":
             ref = Wd.at[l, pl.ds(0, FX), half(D)]
         else:
@@ -234,75 +351,103 @@
     def ag_done(l, name):
         wait_recv([ag[l, name, 3]])
 
-    def gather_blocks(ref):
-        return push3([ref] * 3, [ref] * 3, PX)
+    def gather_rows(ref):
+        return Gather(RX, lambda j, h: ref.at[pl.ds(pl.multiple_of(j * BT + h * 32, 32), 32)], ref.at[pl.ds(0, 128)]).a()
+
+    def gather_heads(l):
+        return Gather(RX, lambda j, h: O.at[l, j, pl.ds(h * 128, 128)], O.at[l, pl.ds(0, 2)]).a()
 
     def scatter_sums(i, value_of):
         for b in range(4):
             PS[i, b] = value_of(b)
-        return push3([PS.at[i, v] for v in X3], [PRV.at[i, j] for j in range(3)], PX)
-
-    def summed(i, descs):
-        total = PS[i, x].astype(F32)
-        for j, desc in enumerate(descs):
-            desc.wait_recv()
-            total = total + PRV[i, j].astype(F32)
-        return total
+        return Reduce(RX, lambda j, h: PS.at[i, j, pl.ds(h * 32, 32)], lambda n, h: PRV.at[i, n, pl.ds(h * 32, 32)],
+                      PRV.at[i, pl.ds(1, 2)]).a()
+
+    def summed(i, red):
+        red.c()
+        return PS[i, x].astype(F32) + PRV[i, 1].astype(F32) + PRV[i, 2].astype(F32)
 
     GRAD = {"q": (Gq, R1q, R2q, Sq, OUTq, FSq, 384), "o": (Go, R1o, R2o, So, OUTo, FSo, 128),
             "gu": (Ggu, R1gu, R2gu, Sgu, OUTgu, FSgu, FP)}
     rs = {}
 
-    def rs1(l, name):
+    def r1a(l, name):
         if name == "d":
-            rs[l, name, 1] = push3(
-                [Gd.at[l, pl.ds(pl.multiple_of(v * DR, 16), DR)] for v in Y3], [R1d.at[l, j] for j in range(3)], PY)
+            def part(j, h):
+                return Gd.at[l, pl.ds(pl.multiple_of(j * DR, 16), DR), pl.ds(h * 256, 256)]
+            rs[l, name, 1] = Reduce(RY, part, lambda n, h: R1d.at[l, n, :, pl.ds(h * 256, 256)], R1d.at[l, pl.ds(1, 2)]).a()
             return
         G, R1, R2, S, OUT, FS, width = GRAD[name]
-        a = push3([G.at[l, v, :, pl.ds(0, 32)] for v in Z3], [R1.at[l, 0, j] for j in range(3)], PZ)
-        b = push3([G.at[l, :, v, pl.ds(32, 32)] for v in Y3], [R1.at[l, 1, j] for j in range(3)], PY)
-        rs[l, name, 1] = (a, b)
-
-    def rs2(l, name):
+        rs[l, name, 1] = (
+            Reduce(RZ, lambda j, h: G.at[l, j, :, rows16(0, h)], lambda n, h: R1.at[l, 0, n, :, rows16(0, h)],
+                   R1.at[l, 0, pl.ds(1, 2)]).a(),
+            Reduce(RY, lambda j, h: G.at[l, :, j, rows16(32, h)], lambda n, h: R1.at[l, 1, n, :, rows16(0, h)],
+                   R1.at[l, 1, pl.ds(1, 2)]).a(),
+        )
+
+    def r1b(l, name):
         first = rs[l, name, 1]
         if name == "d":
-            wait_recv(first)
-            Sd[l] = (Gd[l, down_rows].astype(F32) + R1d[l, 0].astype(F32) + R1d[l, 1].astype(F32)
-                     + R1d[l, 2].astype(F32)).astype(BF)
-            j_of = [lax.rem(x + 4 - z, 4) == 1, lax.rem(x + 4 - z, 4) == 3, lax.rem(x + 4 - z, 4) == 2]
-            descs = []
-            for j in range(3):
-                desc = rc(Sd.at[l], R2d.at[l, j], PZ[j], cond=j_of[j])
-
-                @pl.when(j_of[j])
-                def _(desc=desc):
-                    desc.start()
-                descs.append(desc)
-            rs[l, name, 2] = descs
+            first.b()
+            return
+        first[0].b()
+        first[1].b()
+
+    def r2a(l, name):
+        first = rs[l, name, 1]
+        if name == "d":
+            first.c()
+            Sd[l] = (Gd[l, down_rows].astype(F32) + R1d[l, 1].astype(F32) + R1d[l, 2].astype(F32)).astype(BF)
+            idx = new_recv()
+            to = [rc(Sd.at[l, :, pl.ds(0, 256)], R2d.at[l, 0, :, pl.ds(0, 256)], PZ[1], recv=idx, cond=is_f),
+                  rc(Sd.at[l, :, pl.ds(256, 256)], R2d.at[l, 0, :, pl.ds(256, 256)], PZ[0], recv=idx, cond=is_f)]
+
+            @pl.when(is_f)
+            def _():
+                to[0].start()
+                to[1].start()
+            rs[l, name, 2] = to
             return
         G, R1, R2, S, OUT, FS, width = GRAD[name]
-        wait_recv(first[0])
-        S[l, 0] = (G[l, z, :, pl.ds(0, 32)].astype(F32) + R1[l, 0, 0].astype(F32) + R1[l, 0, 1].astype(F32)
-                   + R1[l, 0, 2].astype(F32)).astype(BF)
-        a = push3([S.at[l, 0, v] for v in Y3], [R2.at[l, 0, j] for j in range(3)], PY)
-        wait_recv(first[1])
-        S[l, 1] = (G[l, :, y, pl.ds(32, 32)].astype(F32) + R1[l, 1, 0].astype(F32) + R1[l, 1, 1].astype(F32)
-                   + R1[l, 1, 2].astype(F32)).astype(BF)
-        b = push3([S.at[l, 1, v] for v in Z3], [R2.at[l, 1, j] for j in range(3)], PZ)
+        first[0].c()
+        S[l, 0] = (G[l, z, :, pl.ds(0, 32)].astype(F32) + R1[l, 0, 1].astype(F32) + R1[l, 0, 2].astype(F32)).astype(BF)
+        a = Reduce(RY, lambda j, h: S.at[l, 0, j, rows16(0, h)], lambda n, h: R2.at[l, 0, n, rows16(0, h)],
+                   R2.at[l, 0, pl.ds(1, 2)]).a()
+        first[1].c()
+        S[l, 1] = (G[l, :, y, pl.ds(32, 32)].astype(F32) + R1[l, 1, 1].astype(F32) + R1[l, 1, 2].astype(F32)).astype(BF)
+        b = Reduce(RZ, lambda j, h: S.at[l, 1, j, rows16(0, h)], lambda n, h: R2.at[l, 1, n, rows16(0, h)],
+                   R2.at[l, 1, pl.ds(1, 2)]).a()
         rs[l, name, 2] = (a, b)
 
-    def rs3(l, name):
+    def r2b(l, name):
         second = rs[l, name, 2]
         if name == "d":
-            idx = counter[0]
-            far = rc(OUTd.at[k], OUTd.at[k], PX[2], cond=(z == x) & (s == l))
-            near = [rc(FSd, OUTd.at[k], PX[j], recv=idx, cond=(z == x) & (s != l)) for j in range(2)]
-
-            @pl.when(z == x)
+            idx = [new_recv(), new_recv()]
+            fin = [rc(Sd.at[l], R2d.at[l, 1], PZ[1], recv=idx[0], cond=is_p),
+                   rc(Sd.at[l], R2d.at[l, 2], PZ[0], recv=idx[1], cond=is_m)]
+            for cond, got, h, desc in ((is_p, second[0], 0, fin[0]), (is_m, second[1], 1, fin[1])):
+                @pl.when(cond)
+                def _(got=got, h=h, desc=desc):
+                    got.wait_recv()
+                    cols = pl.ds(256 * h, 256)
+                    Sd[l, :, cols] = (Sd[l, :, cols].astype(F32) + R2d[l, 0, :, cols].astype(F32)).astype(BF)
+                    desc.start()
+            rs[l, name, 3] = fin
+            return
+        second[0].b()
+        second[1].b()
+
+    def rs3(l, name):
+        idx = new_recv()
+        if name == "d":
+            fin = rs[l, name, 3]
+            far = rc(OUTd.at[k], OUTd.at[k], PX[2], recv=idx, cond=is_src & (s == l))
+            near = [rc(FSd, OUTd.at[k], PX[j], recv=idx, cond=is_src & (s != l)) for j in range(2)]
+
+            @pl.when(is_src)
             def _():
-                wait_recv(second)
-                total = (Sd[l].astype(F32) + R2d[l, 0].astype(F32) + R2d[l, 1].astype(F32)
-                         + R2d[l, 2].astype(F32)).astype(BF)
+                wait_recv(fin)
+                total = (Sd[l].astype(F32) + R2d[l, 1].astype(F32) + R2d[l, 2].astype(F32)).astype(BF)
 
                 @pl.when(s == l)
                 def _():
@@ -314,18 +459,17 @@
                     FSd[...] = total
                     for desc in near:
                         desc.start()
-            rs[l, name, 3] = far
+            rs[l, name, 4] = far
             return
         G, R1, R2, S, OUT, FS, width = GRAD[name]
-        wait_recv(second[0])
-        wait_recv(second[1])
-        top = (S[l, 0, y].astype(F32) + R2[l, 0, 0].astype(F32) + R2[l, 0, 1].astype(F32)
-               + R2[l, 0, 2].astype(F32)).astype(BF)
-        low = (S[l, 1, z].astype(F32) + R2[l, 1, 0].astype(F32) + R2[l, 1, 1].astype(F32)
-               + R2[l, 1, 2].astype(F32)).astype(BF)
+        second = rs[l, name, 2]
+        second[0].c()
+        second[1].c()
+        top = (S[l, 0, y].astype(F32) + R2[l, 0, 1].astype(F32) + R2[l, 0, 2].astype(F32)).astype(BF)
+        low = (S[l, 1, z].astype(F32) + R2[l, 1, 1].astype(F32) + R2[l, 1, 2].astype(F32)).astype(BF)
         slot = OUT.at[k, x]
-        far = rc(slot, slot, PX[2], cond=(s == l))
-        near = [rc(FS, slot, PX[j], cond=(s != l)) for j in range(2)]
+        far = rc(slot, slot, PX[2], recv=idx, cond=(s == l))
+        near = [rc(FS, slot, PX[j], recv=idx, cond=(s != l)) for j in range(2)]
 
         @pl.when(s == l)
         def _():
@@ -339,34 +483,28 @@
             FS[32:64] = low
             for desc in near:
                 desc.start()
-        rs[l, name, 3] = [far] + near
+        rs[l, name, 4] = idx
 
     def rs4(l, name):
-        third = rs[l, name, 3]
-        if name == "d":
-            ref = OUTd.at[k]
-            fin = rc(ref, ref, SIB, cond=(s == l))
-
-            @pl.when(s == l)
-            def _():
+        got = rs[l, name, 4]
+        ref = OUTd.at[k] if name == "d" else GRAD[name][4].at[k]
+        fin = rc(ref, ref, SIB, cond=(s == l))
+
+        @pl.when(s == l)
+        def _():
+            if name == "d":
                 @pl.when(z != x)
                 def _():
-                    third.wait_recv()
-                fin.start()
-        else:
-            ref = GRAD[name][4].at[k]
-            fin = rc(ref, ref, SIB, cond=(s == l))
-
-            @pl.when(s == l)
-            def _():
-                wait_recv(third)
-                fin.start()
-        rs[l, name, 4] = fin
+                    got.wait_recv()
+            else:
+                wait_bytes(GRAD[name][4].at[k, pl.ds(0, 3)], got)
+            fin.start()
+        rs[l, name, 5] = fin
 
     def rs5(l, name):
         @pl.when(s == l)
         def _():
-            rs[l, name, 4].wait_recv()
+            rs[l, name, 5].wait_recv()
 
     def edge(l, value):
         moved = rc(TT.at[l, s], TT.at[l, s], PX[0] if l == 1 else PX[1], cond=(s != l))
@@ -457,11 +595,10 @@
                 PR[l, 2 * t + hh] = pr
                 acc = acc + dot(pr, head(vt, hh))
             O[l, x, :, cols] = acc.astype(BF)
-        got = gather_blocks(O.at[l, x])
-        return got
+        return gather_heads(l)
 
     def hidden(l, XR, got):
-        wait_recv(got)
+        got.c()
         osib = push(O.at[l], Os.at[l], SIB)
         g = gain(l, 1)
         w = Wo[l].reshape(D, D)
@@ -502,29 +639,30 @@
         got = scatter_sums(i, lambda b: part[b * 64 : (b + 1) * 64])
         return sib, got
 
-    def grads_ff(l, DY, msib, dysib, nsib, gsib):
-        cols = half(D)
+    def grads_d(l, DY, msib, dysib):
         wait_recv([msib, dysib])
-        Gd[l] = (dot_tn(M[l], DY[:, cols]) + dot_tn(Ms[l], DYs[l])).astype(BF)
-        rs1(l, "d")
+        Gd[l] = (dot_tn(M[l], DY[:, half(D)]) + dot_tn(Ms[l], DYs[l])).astype(BF)
+        r1a(l, "d")
+
+    def grads_gu(l, nsib, gsib):
         wait_recv([nsib, gsib])
         Ggu[l] = (dot_tn(N2[l], DGU[l, k]) + dot_tn(N2s[l], DGUs[l])).astype(BF).reshape(4, 4, SH, FP)
-        rs1(l, "gu")
+        r1a(l, "gu")
 
     def back_hidden(l, DY, i, got):
         dn = summed(i, got)
         hf = H[l, own, :]
         g = gain(l, 1)
         inv = lax.rsqrt(jnp.mean(hf * hf, axis=-1, keepdims=True) + EPS)
-        GS[2 * l + 1 : 2 * l + 2] = jnp.sum(dn * hf * inv, axis=0, keepdims=True)
+        GS[0, 2 * l + 1 : 2 * l + 2] = jnp.sum(dn * hf * inv, axis=0, keepdims=True)
         e = dn * g
         dh = DY[own, :].astype(F32) + inv * e - hf * (inv * inv * inv) * jnp.mean(e * hf, axis=-1, keepdims=True)
         DH[l] = dh
         DHB[l, own, :] = dh.astype(BF)
-        return gather_blocks(DHB.at[l, own])
+        return gather_rows(DHB.at[l])
 
     def back_attend(l, got, i):
-        wait_recv(got)
+        got.c()
         hs = pl.ds(pl.multiple_of(x * HX + (1 - k) * 128, 128), 128)
         hsib = push(DHB.at[l, :, hs], DHBs.at[l], SIB)
         do = dot_nt(DHB[l], Wo[l, x].reshape(HX, D)).astype(BF)
@@ -562,133 +700,193 @@
         got = scatter_sums(i, lambda b: part[b * 64 : (b + 1) * 64])
         return hsib, psib, got
 
-    def grads_att(l, n1sib, osib, hsib, psib):
+    def grads_q(l, n1sib, psib):
         wait_recv([n1sib, psib])
         Gq[l] = (dot_tn(N1[l], DP[l, :, half(768)]) + dot_tn(N1s[l], DPs[l])).astype(BF).reshape(4, 4, SH, 384)
-        rs1(l, "q")
+        r1a(l, "q")
+
+    def grads_o(l, osib, hsib):
         wait_recv([osib, hsib])
         hs = pl.ds(pl.multiple_of(x * HX + k * 128, 128), 128)
         for b in range(4):
             Go[l, b] = (dot_tn(O[l, b], DHB[l, :, hs]) + dot_tn(Os[l, b], DHBs[l])).astype(BF).reshape(4, SH, 128)
-        rs1(l, "o")
+        r1a(l, "o")
 
     def back_input(l, XR, i, got):
         dn = summed(i, got)
         xf = XR[own, :].astype(F32)
         g = gain(l, 0)
         inv = lax.rsqrt(jnp.mean(xf * xf, axis=-1, keepdims=True) + EPS)
-        GS[2 * l : 2 * l + 1] = jnp.sum(dn * xf * inv, axis=0, keepdims=True)
+        GS[0, 2 * l : 2 * l + 1] = jnp.sum(dn * xf * inv, axis=0, keepdims=True)
         e = dn * g
         dx = DH[l] + inv * e - xf * (inv * inv * inv) * jnp.mean(e * xf, axis=-1, keepdims=True)
         return dx.astype(BF)
 
+    def gsum_a(i, to):
+        idx = new_recv()
+        for j, t in enumerate(to):
+            push(GS.at[i], GR.at[i, j], t, idx)
+        return i, len(to), idx
+
+    def gsum_b(sent_to):
+        i, n, idx = sent_to
+        wait_bytes(GR.at[i, pl.ds(0, n)], idx)
+        total = GS[i]
+        for j in range(n):
+            total = total + GR[i, j]
+        GS[i + 1] = total
+
     X0 = E.at[0]
     DY1 = E.at[1]
-    GS[...] = jnp.zeros_like(GS)
+    NAMES = ("g", "q", "o", "gu", "d")
+    GS[0] = jnp.zeros((8, D), F32)
     for l in range(2):
         Wd[l, FX:FP, :] = jnp.zeros((FP - FX, D), BF)
-    for name in ("g", "q", "o", "gu", "d"):
-        ag1(0, name)
+    for name in NAMES:
+        s1a(0, name)
     e_loc.wait()
     e_sib.wait_recv()
     mine2 = pl.ds(pl.multiple_of(xh * 128, 128), 128)
     e_got = push3([E.at[s, mine2]] * 3, [E.at[s, mine2]] * 3, PX)
-    ag2(0, "g")
-    ag2(0, "q")
-    ag2(0, "o")
-    ag2(0, "gu")
-    ag2(0, "d")
-    ag3(0, "g")
+    for name in NAMES:
+        s1b(0, name)
+    for name in NAMES:
+        s1a(1, name)
+    s2a(0, "g")
+    s2a(0, "q")
+    s2a(0, "o")
+    s2a(0, "gu")
+    s3(0, "g")
     wait_recv(e_got)
     dysib = [None, push(DY1.at[:, other_half(D)], DYs.at[1], SIB)]
     n1sib = [norm_one(0, X0), None]
-    ag3(0, "q")
+    s2b(0, "q")
+    s2a(0, "d")
+    s2b(0, "o")
+    s3(0, "q")
+    s2b(0, "gu")
+    for name in NAMES:
+        s1b(1, name)
     ag_done(0, "q")
     project(0)
+    s2b(0, "d")
+    s3(0, "o")
     got = attend(0)
-    for name in ("g", "q", "o", "gu", "d"):
-        ag1(1, name)
-    ag3(0, "o")
-    ag3(0, "gu")
-    ag3(0, "d")
+    s2a(1, "g")
+    s2a(1, "q")
+    got.b()
+    s3(0, "gu")
+    s2a(1, "o")
+    s2a(1, "gu")
+    s3(0, "d")
     ag_done(0, "o")
     osib, nsib, msib = [None, None], [None, None], [None, None]
     osib[0], nsib[0] = hidden(0, X0, got)
+    s2b(1, "q")
     ag_done(0, "gu")
     msib[0] = gate_up(0)
+    s2a(1, "d")
+    s2b(1, "o")
     ag_done(0, "d")
     got = down(0, 0)
-    for name in ("g", "q", "o", "gu", "d"):
-        ag2(1, name)
+    s2b(1, "gu")
+    s3(1, "g")
+    s3(1, "q")
+    got.b()
+    s2b(1, "d")
+    s3(1, "o")
     X1[own, :] = (summed(0, got) + H[0, own, :]).astype(BF)
-    got = gather_blocks(X1.at[own])
-    for name in ("g", "q", "o", "gu", "d"):
-        ag3(1, name)
-    wait_recv(got)
+    got = gather_rows(X1)
+    s3(1, "gu")
+    got.b()
+    s3(1, "d")
+    got.c()
     n1sib[1] = norm_one(1, X1)
     ag_done(1, "q")
     project(1)
     got = attend(1)
+    got.b()
     ag_done(1, "o")
     osib[1], nsib[1] = hidden(1, X1, got)
     ag_done(1, "gu")
     msib[1] = gate_up(1)
     ag_done(1, "d")
-    y_got = down(1, 1)
+    y_red = down(1, 1)
 
     gsib, got = back_ff(1, DY1, 2)
-    y_fin, y_done = edge(1, (summed(1, y_got) + H[1, own, :]).astype(BF))
-    grads_ff(1, DY1, msib[1], dysib[1], nsib[1], gsib)
+    y_red.b()
+    grads_d(1, DY1, msib[1], dysib[1])
+    got.b()
+    grads_gu(1, nsib[1], gsib)
+    y_fin, y_done = edge(1, (summed(1, y_red) + H[1, own, :]).astype(BF))
     got = back_hidden(1, DY1, 2, got)
+    r1b(1, "d")
+    got.b()
+    hsib, psib, got = back_attend(1, got, 3)
+    grads_q(1, n1sib[1], psib)
+    got.b()
+    grads_o(1, osib[1], hsib)
+    r1b(1, "gu")
+    r2a(1, "d")
+    DY0[own, :] = back_input(1, X1, 3, got)
+    got = gather_rows(DY0)
     y_fin()
-    hsib, psib, got = back_attend(1, got, 3)
-    grads_att(1, n1sib[1], osib[1], hsib, psib)
-    DY0[own, :] = back_input(1, X1, 3, got)
-    got = gather_blocks(DY0.at[own])
-    rs2(1, "d")
-    rs2(1, "gu")
-    wait_recv(got)
+    r1b(1, "q")
+    got.b()
+    r1b(1, "o")
+    r2a(1, "gu")
+    r2b(1, "d")
+    got.c()
     dysib[0] = push(DY0.at[:, other_half(D)], DYs.at[0], SIB)
 
     gsib, got = back_ff(0, DY0, 4)
-    rs2(1, "q")
-    rs2(1, "o")
-    grads_ff(0, DY0, msib[0], dysib[0], nsib[0], gsib)
+    grads_d(0, DY0, msib[0], dysib[0])
+    got.b()
+    r2a(1, "q")
+    r2a(1, "o")
+    grads_gu(0, nsib[0], gsib)
+    r2b(1, "gu")
     rs3(1, "d")
+    got = back_hidden(0, DY0, 4, got)
+    r1b(0, "d")
+    got.b()
+    r2b(1, "q")
+    r2b(1, "o")
+    hsib, psib, got = back_attend(0, got, 5)
+    grads_q(0, n1sib[0], psib)
+    got.b()
+    grads_o(0, osib[0], hsib)
+    r1b(0, "gu")
+    r2a(0, "d")
     rs3(1, "gu")
-    got = back_hidden(0, DY0, 4, got)
     rs3(1, "q")
     rs3(1, "o")
-    hsib, psib, got = back_attend(0, got, 5)
-    rs2(0, "d")
-    rs2(0, "gu")
-    grads_att(0, n1sib[0], osib[0], hsib, psib)
+    dx = back_input(0, X0, 5, got)
+    x_fin, x_done = edge(0, dx)
+    g0 = gsum_a(0, PX)
+    r1b(0, "q")
+    r1b(0, "o")
+    r2a(0, "gu")
+    r2b(0, "d")
+    gsum_b(g0)
+    g0 = gsum_a(1, PY)
+    x_fin()
     for name in ("d", "gu", "q", "o"):
         rs4(1, name)
-    dx = back_input(0, X0, 5, got)
-    x_fin, x_done = edge(0, dx)
-
-    def gsum(i, to):
-        descs = push3([GS] * len(to), [GR.at[i, j] for j in range(len(to))], to)
-        for desc in descs:
-            desc.wait()
-        del sent[len(sent) - len(descs):]
-        total = GS[...]
-        for j in range(len(to)):
-            total = total + GR[i, j]
-        GS[...] = total
-
-    gsum(0, PX)
-    rs2(0, "q")
-    rs2(0, "o")
+    r2a(0, "q")
+    r2a(0, "o")
+    gsum_b(g0)
+    g0 = gsum_a(2, PZ)
     rs3(0, "d")
+    r2b(0, "gu")
+    r2b(0, "q")
+    r2b(0, "o")
+    gsum_b(g0)
+    g0 = gsum_a(3, [SIB])
     rs3(0, "gu")
-    gsum(1, PY)
-    x_fin()
-    gsum(2, PZ)
     rs3(0, "q")
     rs3(0, "o")
-    gsum(3, [SIB])
+    gsum_b(g0)
     for name in ("d", "gu", "q", "o"):
         rs4(0, name)
     for name in ("d", "gu", "q", "o"):
@@ -697,12 +895,13 @@
     x_done()
     y_done()
     outs = [local(a, b) for a, b in
-            ((OUTq, oq_hbm), (OUTo, oo_hbm), (OUTgu, ogu_hbm), (OUTd, od_hbm), (EO, edge_hbm), (GS, gsum_hbm))]
+            ((OUTq, oq_hbm), (OUTo, oo_hbm), (OUTgu, ogu_hbm), (OUTd, od_hbm), (EO, edge_hbm), (GS.at[4], gsum_hbm))]
     for o in outs:
         o.start()
     flush()
     for o in outs:
         o.wait()
+    assert counter[0] <= N_RECV and counter[1] <= N_LOC and counter[2] <= N_SEND, counter
 
 
 def run_kernel(lengths, ends, q_src, o_src, gu_src, d_src, gain_src, cos, sa, sb):
@@ -712,7 +911,7 @@
     vm = pl.BlockSpec(memory_space=pltpu.VMEM)
     out_shape = [
         sh((2, 4, SH, 384), BF), sh((2, 4, SH, 128), BF), sh((2, 4, SH, FP), BF), sh((2, DR, 512), BF),
-        sh((2, BT, D), BF), sh((8, D), F32),
+        sh((2, BT, D), BF), sh((8, D), F32), sh((GROUP_BYTES // 4096, 16, 128), BF),
     ]
     scratch = [
         V((2, 4, 4, SH, 768), BF), V((2, 4, 4, SH, D), BF), V((2, 4, 4, SH, 2 * FP), BF), V((2, FP, D), BF),
@@ -733,14 +932,14 @@
         V((2, 2, 4, 32, 384), BF), V((2, 2, 4, 32, 128), BF), V((2, 2, 4, 32, FP), BF), V((2, DR, 512), BF),
         V((2, 4, SH, 384), BF), V((2, 4, SH, 128), BF), V((2, 4, SH, FP), BF), V((2, DR, 512), BF),
         V((SH, 384), BF), V((SH, 128), BF), V((SH, FP), BF), V((DR, 512), BF),
-        V((8, D), F32), V((4, 3, 8, D), F32), V((2, 2, BT, D), BF), V((2, BT, D), BF),
-        pltpu.SemaphoreType.DMA((N_SEM,)), pltpu.SemaphoreType.DMA((N_SEM,)), pltpu.SemaphoreType.DMA((N_LOC,)),
+        V((5, 8, D), F32), V((4, 3, 8, D), F32), V((2, 2, BT, D), BF), V((2, BT, D), BF),
+        pltpu.SemaphoreType.DMA((N_SEND,)), pltpu.SemaphoreType.DMA((N_RECV,)), pltpu.SemaphoreType.DMA((N_LOC,)),
     ]
     return pl.pallas_call(
         kernel,
         out_shape=out_shape,
         in_specs=[pl.BlockSpec(memory_space=pltpu.SMEM)] + [any_] * 6 + [vm] * 3,
-        out_specs=[any_] * 6,
+        out_specs=[any_] * 7,
         scratch_shapes=scratch,
         name="two_layers",
         compiler_params=pltpu.CompilerParams(
@@ -780,7 +979,7 @@
     odd = lax.rem(d, 2) == 1
     gain_src = jnp.where(odd, jnp.pad(gb, ((0, 14), (64, 0))), jnp.pad(gb, ((0, 14), (0, 64))))
     cos, sa, sb = tables(lax.dynamic_index_in_dim(doc, k, 0, keepdims=False))
-    oq, oo, ogu, od, edge, gsum = run_kernel(doc, ends, q_src, o_src, gu_src, d_src, gain_src, cos, sa, sb)
+    oq, oo, ogu, od, edge, gsum, _ = run_kernel(doc, ends, q_src, o_src, gu_src, d_src, gain_src, cos, sa, sb)
     qkv = oq.transpose(2, 1, 0, 3).reshape(SH, 4, 3, HX).transpose(0, 2, 1, 3).reshape(SH, 3 * D).astype(F32)
     out = oo.transpose(2, 1, 0, 3).reshape(SH, D).astype(F32)
     gate = ogu[0].transpose(1, 0, 2)[:, :, :FX].reshape(SH, FF).astype(F32)

time: 227 us -> 209 us (0.921)
  Pallas kernels: 199 us -> 181 us
    pallas_call x1, Pallas kernels: 199 us -> 181 us  [run_kernel(): pl.pallas_call(kernel, out_shape=out_shape, in_specs=[pl.BlockSpec(memory...]
where the time goes in v2:
time: 209 us
  Pallas kernels  181 us (87%)
  local copies, waits for them, and re-layouts  16.2 us (8%)
  other arithmetic  10.4 us (5%)
    pallas_call x1, Pallas kernels, run_kernel(): pl.pallas_call(kernel, out_shape=out_shape, in_specs=[pl.BlockSpec(memory...  181 us

profile of v2, /device:TPU:1, one launch (start us, length us, event | category | flops | bytes accessed | tf_op | source)
XLA Modules:
  0.0 208.8 jit_solution(11182152792869298817)
XLA Ops:
  0.6 0.0 copy-start.2
  0.7 0.7 dynamic-slice_bitcast_fusion.1
  1.4 0.2 reduce-window.4
  1.6 0.7 convert_bitcast_fusion.5
  2.2 0.6 fusion.10
  2.8 1.3 fusion.4
  4.1 0.7 pad_select_fusion.gain_src
  4.8 1.6 convert_bitcast_fusion.4.o_src
  6.4 1.1 convert_element_type.142
  7.6 0.5 convert_element_type.143
  8.1 0.0 copy-done.2
  8.1 0.5 convert_element_type.145
  8.7 0.0 copy-start.3
  8.7 0.1 pad_bitcast_fusion
  8.8 0.0 copy-start
  8.8 0.9 pad_maximum_fusion.gu_src
  9.7 0.1 copy-done.3
  9.8 0.8 convert_bitcast_fusion.2.d_src
  10.6 0.0 copy-done
  10.7 0.3 convert_element_type.139
  10.9 0.2 copy.37
  11.1 1.2 reshape.146.q_src
  12.3 1.8 fusion
  14.2 181.3 %two_layers.1 = (bf16[2,4,64,384]{3,2,1,0:T(8,128)(2,1)}, bf16[2,4,64,128]{3,2,1,0:T(8,128)(2,1)}, bf16[2,4,64,768]{3,2,1,0:T(8,128)(2,1)}, bf16[2,176,512]{2,1,...) custom-call(s32[2,3]{1,0:T(2,128)} %bitcast.43, ...), custom_call_target="tpu_custom_call" | custom-call | tf_op jit(solution)/shard_map/two_layers/pallas_call | solution.py:938
  195.5 0.0 copy-start.5
  195.5 1.4 dynamic-slice_bitcast_fusion
  196.9 0.9 convert_bitcast_fusion.3
  197.8 0.2 copy.31
  198.0 0.9 reshape.149
  198.9 0.0 copy-done.5
  198.9 0.1 convert_bitcast_fusion.1
  199.0 0.0 copy-start.4
  199.0 0.6 copy.34
  199.6 1.5 reshape.152
  201.1 0.0 copy-done.4
  201.1 0.1 convert_bitcast_fusion
  201.1 0.6 copy.29
  201.7 0.8 reshape.153
  202.6 0.0 copy-start.1
  202.6 0.2 copy.30
  202.8 1.3 reshape.148
  204.1 0.0 copy-done.1
  204.1 0.1 slice_bitcast_fusion
  204.1 0.1 slice_convert_fusion
  204.2 0.5 copy.33
  204.7 1.4 reshape.151
  206.1 0.1 slice_convert_fusion.1
  206.2 0.0 copy-start.6
  206.2 0.5 copy.32
  206.7 1.4 reshape.150
  208.1 0.0 copy-done.6
  208.1 0.7 copy.39
  (6 shorter events, 0.2 us)
Async XLA Ops:
  0.6 7.5 %copy-start.2 = (f32[1,64,2816]{2,1,0:T(8,128)S(1)}, f32[1,64,2816]{2,1,0:T(8,128)}, u32[]{:S(2)}) copy-start(f32[1,64,2816]{2,1,0:T(8,128)} %param.13) | copy-start | bytes 2162692
  8.7 1.2 copy-start.3
  8.8 1.8 copy-start
  195.5 3.4 %copy-start.5 = (bf16[2,176,512]{2,1,0:T(8,128)(2,1)S(1)}, bf16[2,176,512]{2,1,0:T(8,128)(2,1)}, u32[]{:S(2)}) copy-start(bf16[2,176,512]{2,1,0:T(8,128)(2,1)} %get-tuple-element.17) | copy-start | bytes 1081348
  199.0 2.1 copy-start.4
  202.6 1.5 copy-start.1
  206.2 1.9 copy-start.6

commit v3 on v2

--- a/solution.py
+++ b/solution.py
@@ -1,5 +1,6 @@
 import jax
 import jax.numpy as jnp
+import numpy as np
 from jax import lax
 from jax.experimental import pallas as pl
 from jax.experimental.pallas import tpu as pltpu
@@ -34,18 +35,19 @@
 
 N_SEND = 64
 N_RECV = 264
-N_LOC = 12
+N_LOC = 18
 GROUP_BYTES = 4 * 1024 * 1024
 
 
 def kernel(
-    lengths, ends, q_src, o_src, gu_src, d_src, gain_src, cos_ref, sa_ref, sb_ref,
+    lengths, ends, q_w, o_w, gate_w, up_w, d_w, gains, angles,
     oq_hbm, oo_hbm, ogu_hbm, od_hbm, edge_hbm, gsum_hbm, dummy,
     Wq, Wo, Wgu, Wd, Gn,
     E, X1, DY0, N1, N1s, N2, N2s, H, QKV, PR, O, Os, GU, M, Ms, DGU, DGUs, DP, DPs, DHB, DHBs, DYs, DH,
     PS, PRV,
     Gq, Go, Ggu, Gd, R1q, R1o, R1gu, R1d, R2q, R2o, R2gu, R2d, Sq, So, Sgu, Sd, OUTq, OUTo, OUTgu, OUTd,
     FSq, FSo, FSgu, FSd, GS, GR, TT, EO,
+    CS, QT, GT, OT, DT, NT, gain_in,
     ssem, rsem, lsem,
 ):
     s = lax.axis_index("section")
@@ -92,8 +94,8 @@
     def rc(src, dst, to, recv=None, cond=None):
         recv = new_recv() if recv is None else recv
         if cond is None:
-            if not groups or groups[-1][1] + size(src) > GROUP_BYTES:
-                groups.append([counter[2], 0])
+            if not groups or groups[-1][2] or groups[-1][1] + size(src) > GROUP_BYTES:
+                groups.append([counter[2], 0, False])
                 counter[2] += 1
             groups[-1][1] += size(src)
             i = groups[-1][0]
@@ -125,10 +127,17 @@
             src_ref=ref, dst_ref=ref, send_sem=ssem.at[0], recv_sem=rsem.at[recv], device_id=SIB, device_id_type=MESH,
         ).wait_recv()
 
-    def flush():
-        for i, total in groups:
+    def close():
+        if groups:
+            groups[-1][2] = True
+        return len(groups)
+
+    def flush(first, last):
+        for i, total, _ in groups[first:last]:
             ref = dummy.at[pl.ds(0, total // 4096)]
             pltpu.make_async_copy(ref, ref, ssem.at[i]).wait()
+
+    def flush_conditional():
         for cond, desc in sent:
             @pl.when(cond)
             def _(desc=desc):
@@ -205,27 +214,82 @@
     tx = lax.rem(x + 3 - 2 * k, 4)
     TO = dev(tx, y, z, k)
     REG = {"q": (Wq, 768), "o": (Wo, 1024), "gu": (Wgu, 2 * FP)}
-    pre, loc = {}, {}
-
-    def src_of(name, sl):
-        if name == "q":
-            return q_src.at[sl, :, half(768)]
-        if name == "gu":
-            return gu_src.at[sl, :, half(2 * FP)]
-        return o_src.at[:, half(1024)]
-
-    loc["g"] = local(gain_src, Gn.at[s, z, y])
-    pre["g"] = rc(gain_src, Gn.at[s, z, y], TO)
-    loc["g"].start()
+    pre = {}
+    down_rows = pl.ds(pl.multiple_of(y * DR, 16), DR)
+    slices = (x, tx)
+    q_in = GU.at[1, 0, pl.ds(128, 128), pl.ds(0, 384)]
+    gu_in = GU.at[1, 0, pl.ds(0, 128), :]
+    d_in = GU.at[1, 1, pl.ds(0, DR), pl.ds(0, 512)]
+    o_in = GU.at[1, 1, pl.ds(192, SH), pl.ds(0, 512)]
+    q_cp = []
+    for j in range(2):
+        for i in range(3):
+            piece = 3 * k + i
+            col = D * lax.div(piece, 2) + HX * slices[j] + 128 * lax.rem(piece, 2)
+            q_cp.append(local(q_w.at[0, :, pl.ds(pl.multiple_of(col, 128), 128)],
+                              GU.at[1, 0, pl.ds(128 + SH * j, SH), pl.ds(128 * i, 128)]))
+    o_cp = local(o_w.at[0, :, half(D)], o_in)
+    d_cp = local(d_w.at[0, :, half(D)], d_in)
+    gu_cp = []
+    for w in (gate_w, up_w):
+        pair = []
+        for j in range(2):
+            col = 2 * FX * lax.div(slices[j], 2) + (FX - 64) * lax.rem(slices[j], 2)
+            pair.append((w.at[0, :, pl.ds(pl.multiple_of(col, 128), FP)], GU.at[1, 0, pl.ds(SH * j, SH), :]))
+        gu_cp.append(pair)
+    gu_cp = [[local(*c) for c in gu_cp[0]], None, gu_cp[1]]
+    gu_cp[1] = [pltpu.make_async_copy(*c, lsem.at[counter[1] - 2 + j]) for j, c in enumerate(gu_cp.pop())]
+    for cp in q_cp:
+        cp.start()
+    for kk in range(2):
+        @pl.when(k == kk)
+        def _(kk=kk):
+            for cp in gu_cp[kk]:
+                cp.start()
+    o_cp.start()
+    d_cp.start()
+
+    odd = lax.rem(dp, 2) == 1
+    gz = jnp.zeros((2, SH), F32)
+    gv = gains[0].astype(F32)
+    NT[...] = jnp.zeros((16, 128), BF)
+    gain_in[...] = jnp.zeros((16, 128), F32)
+    gain_in[0:2, :] = jnp.where(odd, jnp.concatenate([gz, gv], axis=1), jnp.concatenate([gv, gz], axis=1))
+    NT[...] = gain_in[...].astype(BF)
+    Gn[s, z, y] = NT[...]
+    pre["g"] = rc(NT, Gn.at[s, z, y], TO)
     pre["g"].start()
-    for name, (W, width) in REG.items():
-        pre[name] = rc(src_of(name, tx), W.at[s, z, y, :, half(width)], TO)
-        pre[name].start()
-        loc[name] = local(src_of(name, x), W.at[s, z, y, :, half(width)])
-        loc[name].start()
-    down_rows = pl.ds(pl.multiple_of(y * DR, 16), DR)
-    pre["d"] = rc(d_src.at[:, half(D)], Wd.at[s, down_rows, half(D)], TO, cond=(z == tx))
-    loc["d"] = local(d_src.at[:, half(D)], Wd.at[s, down_rows, half(D)])
+
+    for cp in q_cp:
+        cp.wait()
+    QT[...] = q_in[SH : 2 * SH, :].astype(BF)
+    pre["q"] = rc(QT, Wq.at[s, z, y, :, half(768)], TO)
+    pre["q"].start()
+    Wq[s, z, y, :, half(768)] = q_in[0:SH, :].astype(BF)
+
+    o_cp.wait()
+    OT[...] = o_in[...].astype(BF)
+    pre["o"] = rc(OT, Wo.at[s, z, y, :, half(D)], TO)
+    pre["o"].start()
+    Wo[s, z, y, :, half(D)] = OT[...]
+
+    wide = lax.broadcasted_iota(jnp.int32, (SH, FP), 1)
+
+    def hidden_slice(j):
+        v = gu_in[SH * j : SH * (j + 1), :]
+        v = jnp.where(lax.rem(slices[j], 2) == 1, pltpu.roll(v, FP - 64, 1), v)
+        return jnp.where(wide < FX, v, 0.0).astype(BF)
+
+    for cp in gu_cp[0]:
+        cp.wait()
+    GT[...] = hidden_slice(1)
+    pre["gu"] = rc(GT, Wgu.at[s, z, y, :, half(2 * FP)], TO)
+    pre["gu"].start()
+    Wgu[s, z, y, :, half(2 * FP)] = hidden_slice(0)
+
+    d_cp.wait()
+    DT[...] = d_in[...].astype(BF)
+    pre["d"] = rc(DT, Wd.at[s, down_rows, half(D)], TO, cond=(z == tx))
 
     @pl.when(z == tx)
     def _():
@@ -233,20 +297,16 @@
 
     @pl.when(z == x)
     def _():
-        loc["d"].start()
+        Wd[s, down_rows, half(D)] = DT[...]
 
     mine = pl.ds(pl.multiple_of(xh * 128 + k * 64, 64), 64)
-    e_loc = local(ends.at[k], E.at[s, mine])
+    e_loc = local(ends.at[0, k, 0], E.at[s, mine])
     e_loc.start()
-    e_sib = push(ends.at[1 - k], E.at[s, mine], SIB)
+    e_sib = push(ends.at[0, 1 - k, 0], E.at[s, mine], SIB)
 
     ag = {}
 
     def ready(l, name):
-        @pl.when(s == l)
-        def _():
-            loc[name].wait()
-
         @pl.when(s != l)
         def _():
             pre[name].wait_recv()
@@ -371,17 +431,23 @@
             "gu": (Ggu, R1gu, R2gu, Sgu, OUTgu, FSgu, FP)}
     rs = {}
 
+    def grad_ref(name, l):
+        if name == "gu" and l == 0:
+            return Wgu.at[1, :, :, :, pl.ds(0, FP)]
+        return GRAD[name][0].at[0 if name == "gu" else l]
+
     def r1a(l, name):
         if name == "d":
             def part(j, h):
                 return Gd.at[l, pl.ds(pl.multiple_of(j * DR, 16), DR), pl.ds(h * 256, 256)]
             rs[l, name, 1] = Reduce(RY, part, lambda n, h: R1d.at[l, n, :, pl.ds(h * 256, 256)], R1d.at[l, pl.ds(1, 2)]).a()
             return
-        G, R1, R2, S, OUT, FS, width = GRAD[name]
+        _, R1, R2, S, OUT, FS, width = GRAD[name]
+        G = grad_ref(name, l)
         rs[l, name, 1] = (
-            Reduce(RZ, lambda j, h: G.at[l, j, :, rows16(0, h)], lambda n, h: R1.at[l, 0, n, :, rows16(0, h)],
+            Reduce(RZ, lambda j, h: G.at[j, :, rows16(0, h)], lambda n, h: R1.at[l, 0, n, :, rows16(0, h)],
                    R1.at[l, 0, pl.ds(1, 2)]).a(),
-            Reduce(RY, lambda j, h: G.at[l, :, j, rows16(32, h)], lambda n, h: R1.at[l, 1, n, :, rows16(0, h)],
+            Reduce(RY, lambda j, h: G.at[:, j, rows16(32, h)], lambda n, h: R1.at[l, 1, n, :, rows16(0, h)],
                    R1.at[l, 1, pl.ds(1, 2)]).a(),
         )
 
@@ -408,13 +474,14 @@
                 to[1].start()
             rs[l, name, 2] = to
             return
-        G, R1, R2, S, OUT, FS, width = GRAD[name]
+        _, R1, R2, S, OUT, FS, width = GRAD[name]
+        G = grad_ref(name, l)
         first[0].c()
-        S[l, 0] = (G[l, z, :, pl.ds(0, 32)].astype(F32) + R1[l, 0, 1].astype(F32) + R1[l, 0, 2].astype(F32)).astype(BF)
+        S[l, 0] = (G[z, :, pl.ds(0, 32)].astype(F32) + R1[l, 0, 1].astype(F32) + R1[l, 0, 2].astype(F32)).astype(BF)
         a = Reduce(RY, lambda j, h: S.at[l, 0, j, rows16(0, h)], lambda n, h: R2.at[l, 0, n, rows16(0, h)],
                    R2.at[l, 0, pl.ds(1, 2)]).a()
         first[1].c()
-        S[l, 1] = (G[l, :, y, pl.ds(32, 32)].astype(F32) + R1[l, 1, 1].astype(F32) + R1[l, 1, 2].astype(F32)).astype(BF)
+        S[l, 1] = (G[:, y, pl.ds(32, 32)].astype(F32) + R1[l, 1, 1].astype(F32) + R1[l, 1, 2].astype(F32)).astype(BF)
         b = Reduce(RZ, lambda j, h: S.at[l, 1, j, rows16(0, h)], lambda n, h: R2.at[l, 1, n, rows16(0, h)],
                    R2.at[l, 1, pl.ds(1, 2)]).a()
         rs[l, name, 2] = (a, b)
@@ -528,8 +595,8 @@
                 swap.wait_recv()
         return finish, done
 
-    e0 = lengths[k, 0]
-    e1 = e0 + lengths[k, 1]
+    e0 = lengths[k, 0, 0]
+    e1 = e0 + lengths[k, 0, 1]
     qi = lax.broadcasted_iota(jnp.int32, (T, T), 0)
     ki = lax.broadcasted_iota(jnp.int32, (T, T), 1)
 
@@ -544,11 +611,30 @@
     def head(value, hh):
         return jnp.where((lane < 64) if hh == 0 else (lane >= 64), value, jnp.zeros_like(value))
 
+    def make_angles():
+        row = lax.broadcasted_iota(jnp.int32, (T, T), 0)
+        start = jnp.where(row >= e1, e1, jnp.where(row >= e0, e0, 0))
+        pick = jnp.where(ki == row - start, 1.0, 0.0).astype(BF)
+        cos = dot(pick, angles[:, 0:128]) + dot(pick, angles[:, 128:256])
+        sin = dot(pick, angles[:, 256:384]) + dot(pick, angles[:, 384:512])
+        first = (lane < 32) | ((lane >= 64) & (lane < 96))
+        CS[0] = cos
+        CS[1] = jnp.where(first, -sin, 0.0)
+        CS[2] = jnp.where(first, 0.0, sin)
+
+    def turn(v, sign):
+        tiles = []
+        for t in range(2):
+            u = v[:, 128 * t : 128 * (t + 1)]
+            rot = pltpu.roll(u, 96, 1) * CS[1] + pltpu.roll(u, 32, 1) * CS[2]
+            tiles.append(u * CS[0] + rot if sign > 0 else u * CS[0] - rot)
+        return jnp.concatenate(tiles, axis=1)
+
     def rope(v):
-        return v * cos_ref[...] + pltpu.roll(v, HX - 32, 1) * sa_ref[...] + pltpu.roll(v, 32, 1) * sb_ref[...]
+        return turn(v, 1)
 
     def rope_t(v):
-        return v * cos_ref[...] - pltpu.roll(v, HX - 32, 1) * sa_ref[...] - pltpu.roll(v, 32, 1) * sb_ref[...]
+        return turn(v, -1)
 
     def gain(l, i):
         tiles = []
@@ -626,6 +712,14 @@
         part = dot(M[l], Wd[l]).astype(BF)
         return scatter_sums(i, lambda b: part[b * 64 : (b + 1) * 64])
 
+    def gain_grad(i, row, ref):
+        total = jnp.zeros((1, D), F32)
+        for b in range(4):
+            v = ref[pl.ds(b * BT, BT), :].astype(F32)
+            inv = lax.rsqrt(jnp.mean(v * v, axis=-1, keepdims=True) + EPS)
+            total = total + jnp.sum(PS[i, b].astype(F32) * (v * inv), axis=0, keepdims=True)
+        GS[0, row : row + 1] = total
+
     def back_ff(l, DY, i):
         dy = DY[...]
         dm = dot_nt(dy, Wd[l])
@@ -646,7 +740,7 @@
 
     def grads_gu(l, nsib, gsib):
         wait_recv([nsib, gsib])
-        Ggu[l] = (dot_tn(N2[l], DGU[l, k]) + dot_tn(N2s[l], DGUs[l])).astype(BF).reshape(4, 4, SH, FP)
+        grad_ref("gu", l)[...] = (dot_tn(N2[l], DGU[l, k]) + dot_tn(N2s[l], DGUs[l])).astype(BF).reshape(4, 4, SH, FP)
         r1a(l, "gu")
 
     def back_hidden(l, DY, i, got):
@@ -654,7 +748,6 @@
         hf = H[l, own, :]
         g = gain(l, 1)
         inv = lax.rsqrt(jnp.mean(hf * hf, axis=-1, keepdims=True) + EPS)
-        GS[0, 2 * l + 1 : 2 * l + 2] = jnp.sum(dn * hf * inv, axis=0, keepdims=True)
         e = dn * g
         dh = DY[own, :].astype(F32) + inv * e - hf * (inv * inv * inv) * jnp.mean(e * hf, axis=-1, keepdims=True)
         DH[l] = dh
@@ -717,7 +810,6 @@
         xf = XR[own, :].astype(F32)
         g = gain(l, 0)
         inv = lax.rsqrt(jnp.mean(xf * xf, axis=-1, keepdims=True) + EPS)
-        GS[0, 2 * l : 2 * l + 1] = jnp.sum(dn * xf * inv, axis=0, keepdims=True)
         e = dn * g
         dx = DH[l] + inv * e - xf * (inv * inv * inv) * jnp.mean(e * xf, axis=-1, keepdims=True)
         return dx.astype(BF)
@@ -748,34 +840,38 @@
     e_sib.wait_recv()
     mine2 = pl.ds(pl.multiple_of(xh * 128, 128), 128)
     e_got = push3([E.at[s, mine2]] * 3, [E.at[s, mine2]] * 3, PX)
-    for name in NAMES:
+    for name in ("q", "o", "gu"):
         s1b(0, name)
-    for name in NAMES:
+    s2a(0, "q")
+    for name in ("g", "q", "o", "gu"):
         s1a(1, name)
     s2a(0, "g")
-    s2a(0, "q")
     s2a(0, "o")
     s2a(0, "gu")
+    make_angles()
+    s1b(0, "d")
+    s2b(0, "q")
+    s1a(1, "d")
+    s2a(0, "d")
+    s2b(0, "o")
+    s2b(0, "gu")
+    s3(0, "q")
     s3(0, "g")
     wait_recv(e_got)
-    dysib = [None, push(DY1.at[:, other_half(D)], DYs.at[1], SIB)]
     n1sib = [norm_one(0, X0), None]
-    s2b(0, "q")
-    s2a(0, "d")
-    s2b(0, "o")
-    s3(0, "q")
-    s2b(0, "gu")
-    for name in NAMES:
+    for name in ("q", "o", "gu"):
         s1b(1, name)
+    s2b(0, "d")
     ag_done(0, "q")
     project(0)
-    s2b(0, "d")
     s3(0, "o")
     got = attend(0)
+    dysib = [None, push(DY1.at[:, other_half(D)], DYs.at[1], SIB)]
     s2a(1, "g")
     s2a(1, "q")
+    s1b(1, "d")
+    s3(0, "gu")
     got.b()
-    s3(0, "gu")
     s2a(1, "o")
     s2a(1, "gu")
     s3(0, "d")
@@ -785,21 +881,22 @@
     s2b(1, "q")
     ag_done(0, "gu")
     msib[0] = gate_up(0)
+    ag_done(0, "d")
+    got = down(0, 0)
     s2a(1, "d")
     s2b(1, "o")
-    ag_done(0, "d")
-    got = down(0, 0)
+    got.b()
     s2b(1, "gu")
     s3(1, "g")
-    s3(1, "q")
-    got.b()
-    s2b(1, "d")
-    s3(1, "o")
     X1[own, :] = (summed(0, got) + H[0, own, :]).astype(BF)
     got = gather_rows(X1)
+    s3(1, "q")
+    s2b(1, "d")
+    got.b()
+    s3(1, "o")
     s3(1, "gu")
-    got.b()
     s3(1, "d")
+    early = close()
     got.c()
     n1sib[1] = norm_one(1, X1)
     ag_done(1, "q")
@@ -814,97 +911,140 @@
     y_red = down(1, 1)
 
     gsib, got = back_ff(1, DY1, 2)
+    grads_d(1, DY1, msib[1], dysib[1])
+    gain_grad(2, 3, H.at[1])
+    got.b()
     y_red.b()
-    grads_d(1, DY1, msib[1], dysib[1])
-    got.b()
     grads_gu(1, nsib[1], gsib)
-    y_fin, y_done = edge(1, (summed(1, y_red) + H[1, own, :]).astype(BF))
     got = back_hidden(1, DY1, 2, got)
     r1b(1, "d")
+    y_fin, y_done = edge(1, (summed(1, y_red) + H[1, own, :]).astype(BF))
     got.b()
     hsib, psib, got = back_attend(1, got, 3)
+    grads_o(1, osib[1], hsib)
+    gain_grad(3, 2, X1)
+    got.b()
     grads_q(1, n1sib[1], psib)
-    got.b()
-    grads_o(1, osib[1], hsib)
     r1b(1, "gu")
     r2a(1, "d")
     DY0[own, :] = back_input(1, X1, 3, got)
     got = gather_rows(DY0)
     y_fin()
+    r1b(1, "o")
+    got.b()
     r1b(1, "q")
-    got.b()
-    r1b(1, "o")
     r2a(1, "gu")
     r2b(1, "d")
     got.c()
     dysib[0] = push(DY0.at[:, other_half(D)], DYs.at[0], SIB)
 
     gsib, got = back_ff(0, DY0, 4)
-    grads_d(0, DY0, msib[0], dysib[0])
+    r2a(1, "o")
+    gain_grad(4, 1, H.at[0])
     got.b()
     r2a(1, "q")
-    r2a(1, "o")
+    grads_d(0, DY0, msib[0], dysib[0])
+    flush(0, early)
     grads_gu(0, nsib[0], gsib)
     r2b(1, "gu")
     rs3(1, "d")
     got = back_hidden(0, DY0, 4, got)
     r1b(0, "d")
+    r2b(1, "o")
+    r2b(1, "q")
     got.b()
-    r2b(1, "q")
-    r2b(1, "o")
+    rs3(1, "gu")
     hsib, psib, got = back_attend(0, got, 5)
+    gain_grad(5, 0, X0)
+    g0 = gsum_a(0, PX)
+    grads_o(0, osib[0], hsib)
+    got.b()
     grads_q(0, n1sib[0], psib)
-    got.b()
-    grads_o(0, osib[0], hsib)
     r1b(0, "gu")
+    gsum_b(g0)
+    g0 = gsum_a(1, PY)
     r2a(0, "d")
-    rs3(1, "gu")
-    rs3(1, "q")
-    rs3(1, "o")
     dx = back_input(0, X0, 5, got)
     x_fin, x_done = edge(0, dx)
-    g0 = gsum_a(0, PX)
+    r1b(0, "o")
     r1b(0, "q")
-    r1b(0, "o")
+    gsum_b(g0)
+    g0 = gsum_a(2, PZ)
+    rs3(1, "o")
+    rs3(1, "q")
     r2a(0, "gu")
     r2b(0, "d")
-    gsum_b(g0)
-    g0 = gsum_a(1, PY)
+    r2a(0, "o")
+    r2a(0, "q")
     x_fin()
-    for name in ("d", "gu", "q", "o"):
+    for name in ("d", "gu"):
         rs4(1, name)
-    r2a(0, "q")
-    r2a(0, "o")
-    gsum_b(g0)
-    g0 = gsum_a(2, PZ)
-    rs3(0, "d")
-    r2b(0, "gu")
-    r2b(0, "q")
-    r2b(0, "o")
     gsum_b(g0)
     g0 = gsum_a(3, [SIB])
+    r2b(0, "gu")
+    rs3(0, "d")
+    r2b(0, "o")
+    r2b(0, "q")
+    for name in ("o", "q"):
+        rs4(1, name)
     rs3(0, "gu")
+    rs3(0, "o")
     rs3(0, "q")
-    rs3(0, "o")
+    for name in ("d", "gu", "o", "q"):
+        rs4(0, name)
     gsum_b(g0)
-    for name in ("d", "gu", "q", "o"):
-        rs4(0, name)
-    for name in ("d", "gu", "q", "o"):
+    x_done()
+    y_done()
+    for name in ("d", "gu", "o", "q"):
         rs5(1, name)
         rs5(0, name)
-    x_done()
-    y_done()
     outs = [local(a, b) for a, b in
             ((OUTq, oq_hbm), (OUTo, oo_hbm), (OUTgu, ogu_hbm), (OUTd, od_hbm), (EO, edge_hbm), (GS.at[4], gsum_hbm))]
     for o in outs:
         o.start()
-    flush()
+    flush(early, len(groups))
+    flush_conditional()
     for o in outs:
         o.wait()
     assert counter[0] <= N_RECV and counter[1] <= N_LOC and counter[2] <= N_SEND, counter
 
 
-def run_kernel(lengths, ends, q_src, o_src, gu_src, d_src, gain_src, cos, sa, sb):
+def epilogue(*refs):
+    given, (edges, qkv, out, gate, up, down, gg), held, sem = refs[:6], refs[6:13], refs[13:19], refs[19]
+    copies = [pltpu.make_async_copy(a, b, sem.at[i]) for i, (a, b) in enumerate(zip(given, held))]
+    for cp in copies:
+        cp.start()
+    for cp in copies:
+        cp.wait()
+    oq, oo, ogu, od, edge, gsum = held
+    s = lax.axis_index("section")
+    dp = lax.axis_index("dp")
+    edges[0, :, 0] = edge[...]
+    for x in range(4):
+        a, b = oq[0, x].astype(F32), oq[1, x].astype(F32)
+        qkv[0, :, HX * x : HX * (x + 1)] = a[:, 0:256]
+        qkv[0, :, D + HX * x : D + HX * x + 128] = a[:, 256:384]
+        qkv[0, :, D + HX * x + 128 : D + HX * (x + 1)] = b[:, 0:128]
+        qkv[0, :, 2 * D + HX * x : 2 * D + HX * (x + 1)] = b[:, 128:384]
+        for h in range(2):
+            out[0, :, HX * x + 128 * h : HX * x + 128 * (h + 1)] = oo[h, x].astype(F32)
+    for h, ref in ((0, gate), (1, up)):
+        for p in range(2):
+            a = ogu[h, 2 * p].astype(F32)
+            b = pltpu.roll(ogu[h, 2 * p + 1].astype(F32), 64, 1)
+            c = 2 * FX * p
+            ref[0, :, c : c + 640] = a[:, 0:640]
+            ref[0, :, c + 640 : c + 768] = a[:, 640:768] + b[:, 0:128]
+            ref[0, :, c + 768 : c + 2 * FX] = b[:, 128:768]
+    for h in range(2):
+        down[0, :, 512 * h : 512 * (h + 1)] = od[h].astype(F32)
+    tile = gsum[:, pl.ds(pl.multiple_of(128 * lax.div(dp, 2), 128), 128)]
+    tile = jnp.where(lax.rem(dp, 2) == 1, pltpu.roll(tile, 64, 1), tile)
+    rows = jnp.where(s == 1, tile[2:4], tile[0:2])
+    gg[0] = rows[:, 0:SH]
+
+
+def run_kernel(lengths, ends, qkv_w, out_w, gate_w, up_w, down_w, gains, angles):
     V = pltpu.VMEM
     sh = jax.ShapeDtypeStruct
     any_ = pl.BlockSpec(memory_space=pl.ANY)
@@ -925,7 +1065,7 @@
         V((2, T, 768), BF), V((2, T, 384), BF),
         V((2, T, D), BF), V((2, T, 128), BF), V((2, T, 512), BF), V((2, BT, D), F32),
         V((6, 4, BT, D), BF), V((6, 3, BT, D), BF),
-        V((2, 4, 4, SH, 384), BF), V((2, 4, 4, SH, 128), BF), V((2, 4, 4, SH, FP), BF), V((2, FP, 512), BF),
+        V((2, 4, 4, SH, 384), BF), V((2, 4, 4, SH, 128), BF), V((1, 4, 4, SH, FP), BF), V((2, FP, 512), BF),
         V((2, 2, 3, 4, 32, 384), BF), V((2, 2, 3, 4, 32, 128), BF), V((2, 2, 3, 4, 32, FP), BF),
         V((2, 3, DR, 512), BF),
         V((2, 2, 3, 32, 384), BF), V((2, 2, 3, 32, 128), BF), V((2, 2, 3, 32, FP), BF), V((2, 3, DR, 512), BF),
@@ -933,60 +1073,50 @@
         V((2, 4, SH, 384), BF), V((2, 4, SH, 128), BF), V((2, 4, SH, FP), BF), V((2, DR, 512), BF),
         V((SH, 384), BF), V((SH, 128), BF), V((SH, FP), BF), V((DR, 512), BF),
         V((5, 8, D), F32), V((4, 3, 8, D), F32), V((2, 2, BT, D), BF), V((2, BT, D), BF),
+        V((3, T, 128), F32), V((SH, 384), BF), V((SH, FP), BF), V((SH, 512), BF), V((DR, 512), BF),
+        V((16, 128), BF), V((16, 128), F32),
         pltpu.SemaphoreType.DMA((N_SEND,)), pltpu.SemaphoreType.DMA((N_RECV,)), pltpu.SemaphoreType.DMA((N_LOC,)),
     ]
     return pl.pallas_call(
         kernel,
         out_shape=out_shape,
-        in_specs=[pl.BlockSpec(memory_space=pltpu.SMEM)] + [any_] * 6 + [vm] * 3,
+        in_specs=[pl.BlockSpec(memory_space=pltpu.SMEM)] + [any_] * 6 + [vm] * 2,
         out_specs=[any_] * 7,
         scratch_shapes=scratch,
         name="two_layers",
         compiler_params=pltpu.CompilerParams(
             collective_id=0, has_side_effects=True, vmem_limit_bytes=64 * 1024 * 1024 - 65536
         ),
-    )(lengths, ends, q_src, o_src, gu_src, d_src, gain_src, cos, sa, sb)
-
-
-def tables(doc_lengths):
-    ends = jnp.cumsum(doc_lengths)
-    i = jnp.arange(T, dtype=jnp.int32)
-    start = jnp.where(i >= ends[1], ends[1], jnp.where(i >= ends[0], ends[0], 0))
-    pos = (i - start).astype(F32)
-    lane = jnp.arange(HX, dtype=jnp.int32) % 64
-    freq = 10000.0 ** (-(lane % 32).astype(F32) / 32.0)
-    phase = pos[:, None] * freq[None, :]
-    cos, sin = jnp.cos(phase), jnp.sin(phase)
-    first = (lane < 32)[None, :]
-    return cos, jnp.where(first, -sin, 0.0), jnp.where(first, 0.0, sin)
+    )(lengths, ends, qkv_w, out_w, gate_w, up_w, down_w, gains, angles)
+
+
+def angle_table():
+    pos = np.arange(T, dtype=np.float64)[:, None]
+    freq = 10000.0 ** (-(np.arange(128) % 32) / 32.0)
+    parts = []
+    for v in (np.cos(pos * freq), np.sin(pos * freq)):
+        high = v.astype(jnp.bfloat16)
+        parts += [high, (v - high.astype(np.float64)).astype(jnp.bfloat16)]
+    return np.concatenate(parts, axis=1)
 
 
 def per_device(ends_in, lengths, qkv_w, out_w, gate_w, up_w, down_w, gains):
-    s = lax.axis_index("section")
-    d = lax.axis_index("dp")
-    k = lax.rem(lax.axis_index("ctx"), 2)
-    ends = ends_in[0, :, 0]
-    doc = lengths[:, 0]
-    q_src = qkv_w[0].astype(BF).reshape(SH, 3, 4, HX).transpose(2, 0, 1, 3).reshape(4, SH, 768)
-
-    def ff_slices(w):
-        return jnp.pad(w.astype(BF).reshape(SH, 4, FX), ((0, 0), (0, 0), (0, FP - FX))).transpose(1, 0, 2)
-
-    gu_src = jnp.concatenate([ff_slices(gate_w[0]), ff_slices(up_w[0])], axis=2)
-    o_src = out_w[0].astype(BF)
-    d_src = down_w[0].astype(BF)
-    gb = gains[0].astype(BF)
-    odd = lax.rem(d, 2) == 1
-    gain_src = jnp.where(odd, jnp.pad(gb, ((0, 14), (64, 0))), jnp.pad(gb, ((0, 14), (0, 64))))
-    cos, sa, sb = tables(lax.dynamic_index_in_dim(doc, k, 0, keepdims=False))
-    oq, oo, ogu, od, edge, gsum, _ = run_kernel(doc, ends, q_src, o_src, gu_src, d_src, gain_src, cos, sa, sb)
-    qkv = oq.transpose(2, 1, 0, 3).reshape(SH, 4, 3, HX).transpose(0, 2, 1, 3).reshape(SH, 3 * D).astype(F32)
-    out = oo.transpose(2, 1, 0, 3).reshape(SH, D).astype(F32)
-    gate = ogu[0].transpose(1, 0, 2)[:, :, :FX].reshape(SH, FF).astype(F32)
-    up = ogu[1].transpose(1, 0, 2)[:, :, :FX].reshape(SH, FF).astype(F32)
-    down = od.transpose(1, 0, 2).reshape(DR, D).astype(F32)
-    gg = lax.dynamic_slice(gsum, (2 * s, d * SH), (2, SH))
-    return edge[None, :, None], qkv[None], out[None], gate[None], up[None], down[None], gg[None]
+    oq, oo, ogu, od, edge, gsum, _ = run_kernel(
+        lengths, ends_in, qkv_w, out_w, gate_w, up_w, down_w, gains, jnp.asarray(angle_table()))
+    sh = jax.ShapeDtypeStruct
+    return pl.pallas_call(
+        epilogue,
+        out_shape=[
+            sh((1, 2, 1, BT, D), BF), sh((1, SH, 3 * D), F32), sh((1, SH, D), F32), sh((1, SH, FF), F32),
+            sh((1, SH, FF), F32), sh((1, DR, D), F32), sh((1, 2, SH), F32),
+        ],
+        in_specs=[pl.BlockSpec(memory_space=pl.ANY)] * 6,
+        out_specs=[pl.BlockSpec(memory_space=pltpu.VMEM)] * 7,
+        scratch_shapes=[pltpu.VMEM(v.shape, v.dtype) for v in (oq, oo, ogu, od, edge, gsum)]
+        + [pltpu.SemaphoreType.DMA((6,))],
+        name="place_outputs",
+        compiler_params=pltpu.CompilerParams(vmem_limit_bytes=63 * 1024 * 1024),
+    )(oq, oo, ogu, od, edge, gsum)
 
 
 def solution(mesh):

time: 209 us -> 181 us (0.87)
  local copies, waits for them, and re-layouts: 16.2 us -> 0 us
  other arithmetic: 10.4 us -> 0 us
    convert_element_type x18 -> x0, local copies, waits for them, and re-layouts: 11.3 us -> none  [the longest x4 2.91 us: per_device(): oq.transpose(2, 1, 0, 3).reshape(SH, 4, 3, HX).transpose(0, 2, 1, 3)]
    convert_element_type x12 -> x0, other arithmetic: 6.78 us -> none  [the longest x1 1.61 us: per_device(): o_src = out_w[0].astype(BF)]
    pallas_call x1, Pallas kernels: 181 us -> 176 us  [run_kernel(): pl.pallas_call(kernel, out_shape=out_shape, in_specs=[pl.BlockSpec(memory...]
    pallas_call x0 -> x1, Pallas kernels: none -> 3.5 us  [per_device(): pl.pallas_call(epilogue, out_shape=[sh((1, 2, 1, BT, D), BF), sh((1, SH,...]
    select_n x2 -> x0, other arithmetic: 2.5 us -> none  [the longest x1 1.84 us: tables(): return (cos, jnp.where(first, -sin, 0.0), jnp.where(first, 0.0, sin))]
where the time goes in v3:
time: 181 us
  Pallas kernels  180 us (99%)
    pallas_call x1, Pallas kernels, run_kernel(): pl.pallas_call(kernel, out_shape=out_shape, in_specs=[pl.BlockSpec(memory...  176 us

profile of v3, /device:TPU:1, one launch (start us, length us, event | category | flops | bytes accessed | tf_op | source)
XLA Modules:
  0.0 180.7 jit_solution(9772567936726519457)
XLA Ops:
  0.6 176.4 %two_layers.1 = (bf16[2,4,64,384]{3,2,1,0:T(8,128)(2,1)}, bf16[2,4,64,128]{3,2,1,0:T(8,128)(2,1)}, bf16[2,4,64,768]{3,2,1,0:T(8,128)(2,1)}, bf16[2,176,512]{2,1,...) custom-call(s32[2,1,3]{2,1,0:T(1,128)} %lengths.1, ...), custom_call_target="tpu_custom_call" | custom-call | tf_op jit(solution)/shard_map/two_layers/pallas_call | solution.py:1080
  177.0 3.5 %place_outputs.1 = (bf16[1,2,1,64,1024]{4,3,2,1,0:T(8,128)(2,1)}, f32[1,64,3072]{2,1,0:T(8,128)}, f32[1,64,1024]{2,1,0:T(8,128)}, f32[1,64,2816]{2,1,0:T(8,128)}...) custom-call(bf16[2,4,64,384]{3,2,1,0:T(8,128)(2,1)} %get-tuple-element.13.refs_0_, ...), custom_call_target="tpu_custom_call" | custom-call | tf_op jit(solution)/shard_map/place_outputs/pallas_call | solution.py:1107

commit v4 on v3

v4 whole, which is shorter than its diff:
```python
import jax
import jax.numpy as jnp
import numpy as np
from jax import lax
from jax.experimental import pallas as pl
from jax.experimental.pallas import tpu as pltpu
from jax.sharding import PartitionSpec as P

T = 256
D = 1024
FF = 2816
FX = FF // 4
FP = 768
HX = 256
SH = 64
DR = 176
BT = 64
TH = 128
BH = 32
EPS = 1e-5
MESH = pl.DeviceIdType.MESH
BF = jnp.bfloat16
F32 = jnp.float32


def dot(a, b):
    return jnp.dot(a, b, preferred_element_type=F32)


def dot_nt(a, b):
    return lax.dot_general(a, b, (((1,), (1,)), ((), ())), preferred_element_type=F32)


def dot_tn(a, b):
    return lax.dot_general(a, b, (((0,), (0,)), ((), ())), preferred_element_type=F32)


N_SEND = 76
N_RECV = 244
N_LOC = 18
GROUP_BYTES = 4 * 1024 * 1024


def kernel(
    lengths, ends, q_w, o_w, gate_w, up_w, d_w, gains, angles,
    oq_hbm, oo_hbm, ogu_hbm, od_hbm, edge_hbm, gsum_hbm, dummy,
    Wq, Wo, Wgu, Wd, Gn,
    E, X1, DY0, N1, N1s, N2, N2s, H, QKV, PR, O, Os, GU, M, Ms, DGU, DGUs, DP, DPs, DHB, DHBs, DYs, DH, KV0, ED,
    PS, PRV,
    Gq, Go, Ggu, Gd, R1q, R1o, R1gu, R1d, R2q, R2o, R2gu, R2d, Sq, So, Sgu, Sd, OUTq, OUTo, OUTgu, OUTd,
    FSq, FSo, FSgu, FSd, GS, GR, TT, EO,
    CS, QT, GT, OT, DT, NT, gain_in,
    ssem, rsem, lsem,
):
    s = lax.axis_index("section")
    dp = lax.axis_index("dp")
    c = lax.axis_index("ctx")
    xh = lax.div(c, 2)
    k = lax.rem(c, 2)
    x = xh * 2 + s
    z = lax.div(dp, 4)
    y = lax.rem(dp, 4)

    def dev(x_, y_, z_, k_):
        return (lax.rem(x_, 2), z_ * 4 + y_, lax.div(x_, 2) * 2 + k_)

    def ring(v):
        return [lax.rem(v + 1, 4), lax.rem(v + 3, 4), lax.rem(v + 2, 4)]

    X3, Y3, Z3 = ring(x), ring(y), ring(z)
    PX = [dev(v, y, z, k) for v in X3]
    PY = [dev(x, v, z, k) for v in Y3]
    PZ = [dev(x, y, v, k) for v in Z3]
    SIB = dev(x, y, z, 1 - k)

    bar = pltpu.get_barrier_semaphore()
    partners = PX + PY + PZ + [SIB]
    for p in partners:
        pl.semaphore_signal(bar, inc=1, device_id=p, device_id_type=MESH)
    pl.semaphore_wait(bar, len(partners))

    counter = [0, 0, 0]
    sent = []
    groups = []

    def size(ref):
        n = 2 if ref.dtype == BF else 4
        for v in ref.shape:
            n *= v
        return n

    def new_recv():
        counter[0] += 1
        return counter[0] - 1

    def rc(src, dst, to, recv=None, cond=None):
        recv = new_recv() if recv is None else recv
        if cond is None:
            if not groups or groups[-1][2] or groups[-1][1] + size(src) > GROUP_BYTES:
                groups.append([counter[2], 0, False])
                counter[2] += 1
            groups[-1][1] += size(src)
            i = groups[-1][0]
        else:
            i = counter[2]
            counter[2] += 1
        desc = pltpu.make_async_remote_copy(
            src_ref=src, dst_ref=dst, send_sem=ssem.at[i], recv_sem=rsem.at[recv],
            device_id=to, device_id_type=MESH,
        )
        if cond is not None:
            sent.append((cond, desc))
        return desc

    def push(src, dst, to, recv=None):
        desc = rc(src, dst, to, recv)
        desc.start()
        return desc

    def push3(srcs, dsts, to):
        return [push(a, b, t) for a, b, t in zip(srcs, dsts, to)]

    def wait_recv(descs):
        for desc in descs:
            desc.wait_recv()

    def wait_bytes(ref, recv):
        pltpu.make_async_remote_copy(
            src_ref=ref, dst_ref=ref, send_sem=ssem.at[0], recv_sem=rsem.at[recv], device_id=SIB, device_id_type=MESH,
        ).wait_recv()

    def close():
        if groups:
            groups[-1][2] = True
        return len(groups)

    def flush(first, last):
        for i, total, _ in groups[first:last]:
            ref = dummy.at[pl.ds(0, total // 4096)]
            pltpu.make_async_copy(ref, ref, ssem.at[i]).wait()

    def flush_conditional():
        for cond, desc in sent:
            @pl.when(cond)
            def _(desc=desc):
                desc.wait_send()

    class Gather:
        def __init__(self, ring, blk, some, direct=False):
            (self.p, self.m, self.o), self.me, self.to = ring
            self.blk, self.some, self.direct = blk, some, direct

        def a(self):
            self.r = [new_recv() for _ in range(1 if self.direct else 3)]
            if self.direct:
                for to in self.to:
                    push(self.blk(self.me, None), self.blk(self.me, None), to, self.r[0])
                return self
            h0, h1 = self.blk(self.me, 0), self.blk(self.me, 1)
            push(h0, h0, self.to[0], self.r[0])
            push(h1, h1, self.to[1], self.r[1])
            push(h1, h1, self.to[0], self.r[2])
            push(h0, h0, self.to[1], self.r[2])
            return self

        def b(self):
            if not self.direct:
                left, right = self.blk(self.m, 0), self.blk(self.p, 1)
                wait_bytes(left, self.r[0])
                push(left, left, self.to[0], self.r[2])
                wait_bytes(right, self.r[1])
                push(right, right, self.to[1], self.r[2])
            return self

        def c(self):
            if self.direct:
                wait_bytes(self.some(3), self.r[0])
            else:
                wait_bytes(self.some(2), self.r[2])

    class Reduce:
        def __init__(self, ring, part, buf, some, direct=False):
            (self.p, self.m, self.o), self.me, self.to = ring
            self.part, self.buf, self.some, self.direct = part, buf, some, direct
            self.terms = (0, 1, 2) if direct else (1, 2)

        def a(self):
            self.r = [new_recv() for _ in range(1 if self.direct else 3)]
            part, buf = self.part, self.buf
            if self.direct:
                for i, (j, to) in enumerate(zip((self.p, self.m, self.o), self.to)):
                    push(part(j, None), buf(i, None), to, self.r[0])
                return self
            push(part(self.o, 0), buf(0, 0), self.to[0], self.r[0])
            push(part(self.o, 1), buf(0, 1), self.to[1], self.r[1])
            push(part(self.p, 1), buf(1, 1), self.to[0], self.r[2])
            push(part(self.m, 0), buf(2, 0), self.to[1], self.r[2])
            return self

        def b(self):
            if self.direct:
                return self
            part, buf = self.part, self.buf
            for h, j, to in ((0, self.p, self.to[0]), (1, self.m, self.to[1])):
                ref, got = part(j, h), buf(0, h)
                wait_bytes(got, self.r[h])
                ref[...] = (ref[...].astype(F32) + got[...].astype(F32)).astype(BF)
                push(ref, buf(1 + h, h), to, self.r[2])
            return self

        def c(self):
            if self.direct:
                wait_bytes(self.some(0, 3), self.r[0])
            else:
                wait_bytes(self.some(1, 2), self.r[2])

        def total(self):
            value = self.part(self.me, None)[...].astype(F32)
            for i in self.terms:
                value = value + self.buf(i, None)[...].astype(F32)
            return value

    RX, RY, RZ = (X3, x, PX), (Y3, y, PY), (Z3, z, PZ)

    def path_rows(path, paths, h):
        n = 64 // len(paths)
        base = n * paths.index(path)
        return pl.ds(base, n) if h is None else pl.ds(base + h * (n // 2), n // 2)

    def sub(base, width, h):
        return pl.ds(base, width) if h is None else pl.ds(base + h * (width // 2), width // 2)

    def local(src, dst):
        i = counter[1]
        counter[1] += 1
        return pltpu.make_async_copy(src, dst, lsem.at[i])

    def half(width):
        return pl.ds(pl.multiple_of(k * (width // 2), 128), width // 2)

    def other_half(width):
        return pl.ds(pl.multiple_of((1 - k) * (width // 2), 128), width // 2)

    tx = lax.rem(x + 3 - 2 * k, 4)
    TO = dev(tx, y, z, k)
    REG = {"q": (Wq, 768), "o": (Wo, 1024), "gu": (Wgu, 2 * FP)}
    pre = {}
    down_rows = pl.ds(pl.multiple_of(y * DR, 16), DR)
    slices = (x, tx)
    q_in = GU.at[1, 0, pl.ds(128, 128), pl.ds(0, 384)]
    gu_in = GU.at[1, 0, pl.ds(0, 128), :]
    d_in = GU.at[1, 1, pl.ds(0, DR), pl.ds(0, 512)]
    o_in = GU.at[1, 1, pl.ds(192, SH), pl.ds(0, 512)]
    q_cp = []
    for j in range(2):
        for i in range(3):
            piece = 3 * k + i
            col = D * lax.div(piece, 2) + HX * slices[j] + 128 * lax.rem(piece, 2)
            q_cp.append(local(q_w.at[0, :, pl.ds(pl.multiple_of(col, 128), 128)],
                              GU.at[1, 0, pl.ds(128 + SH * j, SH), pl.ds(128 * i, 128)]))
    o_cp = local(o_w.at[0, :, half(D)], o_in)
    d_cp = local(d_w.at[0, :, half(D)], d_in)
    gu_cp = []
    for w in (gate_w, up_w):
        pair = []
        for j in range(2):
            col = 2 * FX * lax.div(slices[j], 2) + (FX - 64) * lax.rem(slices[j], 2)
            pair.append((w.at[0, :, pl.ds(pl.multiple_of(col, 128), FP)], GU.at[1, 0, pl.ds(SH * j, SH), :]))
        gu_cp.append(pair)
    gu_cp = [[local(*c) for c in gu_cp[0]], None, gu_cp[1]]
    gu_cp[1] = [pltpu.make_async_copy(*c, lsem.at[counter[1] - 2 + j]) for j, c in enumerate(gu_cp.pop())]
    for cp in q_cp:
        cp.start()
    for kk in range(2):
        @pl.when(k == kk)
        def _(kk=kk):
            for cp in gu_cp[kk]:
                cp.start()
    o_cp.start()
    d_cp.start()

    odd = lax.rem(dp, 2) == 1
    gz = jnp.zeros((2, SH), F32)
    gv = gains[0].astype(F32)
    NT[...] = jnp.zeros((16, 128), BF)
    gain_in[...] = jnp.zeros((16, 128), F32)
    gain_in[0:2, :] = jnp.where(odd, jnp.concatenate([gz, gv], axis=1), jnp.concatenate([gv, gz], axis=1))
    NT[...] = gain_in[...].astype(BF)
    Gn[z, y, s] = NT[...]
    pre["g"] = rc(NT, Gn.at[z, y, s], TO)
    pre["g"].start()

    for cp in q_cp:
        cp.wait()
    QT[...] = q_in[SH : 2 * SH, :].astype(BF)
    pre["q"] = rc(QT, Wq.at[s, z, y, :, half(768)], TO)
    pre["q"].start()
    Wq[s, z, y, :, half(768)] = q_in[0:SH, :].astype(BF)

    o_cp.wait()
    OT[...] = o_in[...].astype(BF)
    pre["o"] = rc(OT, Wo.at[s, z, y, :, half(D)], TO)
    pre["o"].start()
    Wo[s, z, y, :, half(D)] = OT[...]

    wide = lax.broadcasted_iota(jnp.int32, (SH, FP), 1)

    def hidden_slice(j):
        v = gu_in[SH * j : SH * (j + 1), :]
        v = jnp.where(lax.rem(slices[j], 2) == 1, pltpu.roll(v, FP - 64, 1), v)
        return jnp.where(wide < FX, v, 0.0).astype(BF)

    for cp in gu_cp[0]:
        cp.wait()
    GT[...] = hidden_slice(1)
    pre["gu"] = rc(GT, Wgu.at[s, z, y, :, half(2 * FP)], TO)
    pre["gu"].start()
    Wgu[s, z, y, :, half(2 * FP)] = hidden_slice(0)

    d_cp.wait()
    DT[...] = d_in[...].astype(BF)
    pre["d"] = rc(DT, Wd.at[s, down_rows, half(D)], TO, cond=(z == tx))

    @pl.when(z == tx)
    def _():
        pre["d"].start()

    @pl.when(z == x)
    def _():
        Wd[s, down_rows, half(D)] = DT[...]

    mine = pl.ds(pl.multiple_of(xh * 128 + k * 64, 64), 64)
    e_loc = local(ends.at[0, k, 0], E.at[s, mine])
    e_loc.start()
    e_sib = push(ends.at[0, 1 - k, 0], E.at[s, mine], SIB)

    ag = {}

    def ready(l, name):
        @pl.when(s != l)
        def _():
            pre[name].wait_recv()

    def quarter(h):
        return half(D) if h is None else pl.ds(pl.multiple_of(k * 512 + h * 256, 128), 256)

    is_src, is_p, is_m, is_f = z == x, z == X3[0], z == X3[1], z == X3[2]

    AG_PATHS = {(l, name): "AB" for l in range(2) for name in REG}
    AG_DIRECT = ((0, "q"),)

    def g1():
        for l in range(2):
            ready(l, "g")
        ref = Gn.at[z, y]
        ag["g"] = new_recv()
        for to in PY:
            push(ref, ref, to, ag["g"])

    def g2():
        wait_bytes(Gn.at[z, pl.ds(0, 3)], ag["g"])
        ref = Gn.at[z]
        ag["g"] = new_recv()
        for to in PZ:
            push(ref, ref, to, ag["g"])

    def g3():
        wait_bytes(Gn.at[pl.ds(0, 3)], ag["g"])

    def s1a(l, name):
        if name == "d":
            ref = Wd.at[l, down_rows, half(D)]
            idx = new_recv()
            up = rc(ref, ref, PZ[0], recv=idx, cond=is_src)
            dn = rc(ref, ref, PZ[1], recv=idx, cond=is_src)

            @pl.when(is_src)
            def _():
                ready(l, "d")
                up.start()
                dn.start()
            ag[l, "d", 1] = up, idx
            return
        ready(l, name)
        W, width = REG[name]
        cols = half(width)
        paths, direct = AG_PATHS[l, name], (l, name) in AG_DIRECT
        first = []
        for path in paths:
            rows = lambda h, path=path: path_rows(path, paths, h)
            if path == "A":
                g = Gather(RY, lambda j, h, rows=rows: W.at[l, z, j, rows(h), cols],
                           lambda n, rows=rows: W.at[l, z, pl.ds(0, n), rows(None), cols], direct)
            else:
                g = Gather(RZ, lambda j, h, rows=rows: W.at[l, j, y, rows(h), cols],
                           lambda n, rows=rows: W.at[l, pl.ds(0, n), y, rows(None), cols], direct)
            first.append(g.a())
        ag[l, name, 1] = first

    def s1b(l, name):
        first = ag[l, name, 1]
        if name == "d":
            got, idx = first
            h0, h1 = Wd.at[l, down_rows, quarter(0)], Wd.at[l, down_rows, quarter(1)]
            to_f = [rc(h0, h0, PZ[0], recv=idx, cond=is_p), rc(h1, h1, PZ[1], recv=idx, cond=is_m)]
            for cond, desc in zip((is_p, is_m), to_f):
                @pl.when(cond)
                def _(desc=desc):
                    got.wait_recv()
                    desc.start()
            return
        for g in first:
            g.b()

    def s2a(l, name):
        first = ag[l, name, 1]
        if name == "d":
            @pl.when(is_f)
            def _():
                first[0].wait_recv()

            def blk(j, h):
                return Wd.at[l, pl.ds(pl.multiple_of(j * DR, 16), DR), quarter(h)]
            ag[l, name, 2] = [Gather(RY, blk, lambda n: Wd.at[l, pl.ds(0, n * DR), half(D)]).a()]
            return
        W, width = REG[name]
        cols = half(width)
        paths, direct = AG_PATHS[l, name], (l, name) in AG_DIRECT
        second = []
        for path, g in zip(paths, first):
            rows = lambda h, path=path: path_rows(path, paths, h)
            g.c()
            if path == "A":
                g = Gather(RZ, lambda j, h, rows=rows: W.at[l, j, :, rows(h), cols],
                           lambda n, rows=rows: W.at[l, pl.ds(0, n), :, rows(None), cols], direct)
            else:
                g = Gather(RY, lambda j, h, rows=rows: W.at[l, :, j, rows(h), cols],
                           lambda n, rows=rows: W.at[l, :, pl.ds(0, n), rows(None), cols], direct)
            second.append(g.a())
        ag[l, name, 2] = second

    def s2b(l, name):
        for g in ag[l, name, 2]:
            g.b()

    def s3(l, name):
        for g in ag[l, name, 2]:
            g.c()
        if name == "d":
            ref = Wd.at[l, pl.ds(0, FX), half(D)]
        else:
            W, width = REG[name]
            ref = W.at[l, :, :, :, half(width)]
        ag[l, name, 3] = push(ref, ref, SIB)

    def ag_done(l, name):
        wait_recv([ag[l, name, 3]])

    class Share:
        def __init__(self, ref, three):
            self.r, self.three = new_recv(), three
            for to in PX:
                push(ref, ref, to, self.r)

        def c(self):
            wait_bytes(self.three, self.r)

    class Meet:
        def __init__(self, i, a, part):
            self.i, self.a, self.r = i, a, new_recv()
            for j in range(4):
                PS[i, a, j] = part[BH * j : BH * (j + 1)]
            for n, (j, to) in enumerate(zip(X3, PX)):
                push(PS.at[i, a, j], PRV.at[i, a, n], to, self.r)

        def c(self):
            wait_bytes(PRV.at[self.i, self.a], self.r)
            total = PS[self.i, self.a, x].astype(F32)
            for n in range(3):
                total = total + PRV[self.i, self.a, n].astype(F32)
            return total

    def rows_of(a):
        return pl.ds(TH * a, TH)

    def own(a):
        return pl.ds(pl.multiple_of(TH * a + BH * x, BH), BH)

    def share_rows(ref, a):
        return Share(ref.at[own(a)], ref.at[pl.ds(0, 3 * BH)])

    GRAD = {"q": (Gq, R1q, R2q, Sq, OUTq, FSq, 384), "o": (Go, R1o, R2o, So, OUTo, FSo, 128),
            "gu": (Ggu, R1gu, R2gu, Sgu, OUTgu, FSgu, FP)}
    rs = {}

    def grad_ref(name, l):
        if name == "gu" and l == 0:
            return Wgu.at[1, :, :, :, pl.ds(0, FP)]
        return GRAD[name][0].at[0 if name == "gu" else l]

    RS_PATHS = {(l, name): "AB" for l in range(2) for name in GRAD}
    RS_DIRECT = ((0, "q"), (0, "o"))

    def r1a(l, name):
        if name == "d":
            def part(j, h):
                return Gd.at[l, pl.ds(pl.multiple_of(j * DR, 16), DR), sub(0, 512, h)]
            rs[l, name, 1] = [Reduce(RY, part, lambda n, h: R1d.at[l, n, :, sub(0, 512, h)],
                                     lambda i0, n: R1d.at[l, pl.ds(i0, n)]).a()]
            return
        _, R1, R2, S, OUT, FS, width = GRAD[name]
        G = grad_ref(name, l)
        paths, direct = RS_PATHS[l, name], (l, name) in RS_DIRECT
        first = []
        for path in paths:
            rows = lambda h, path=path: path_rows(path, paths, h)
            buf = lambda n, h, rows=rows: R1.at[l, n, :, rows(h)]
            some = lambda i0, n, rows=rows: R1.at[l, pl.ds(i0, n), :, rows(None)]
            if path == "A":
                r = Reduce(RZ, lambda j, h, rows=rows: G.at[j, :, rows(h)], buf, some, direct)
            else:
                r = Reduce(RY, lambda j, h, rows=rows: G.at[:, j, rows(h)], buf, some, direct)
            first.append(r.a())
        rs[l, name, 1] = first

    def r1b(l, name):
        for r in rs[l, name, 1]:
            r.b()

    def r2a(l, name):
        first = rs[l, name, 1]
        if name == "d":
            first[0].c()
            Sd[l] = first[0].total().astype(BF)
            idx = new_recv()
            to = [rc(Sd.at[l, :, pl.ds(0, 256)], R2d.at[l, 0, :, pl.ds(0, 256)], PZ[1], recv=idx, cond=is_f),
                  rc(Sd.at[l, :, pl.ds(256, 256)], R2d.at[l, 0, :, pl.ds(256, 256)], PZ[0], recv=idx, cond=is_f)]

            @pl.when(is_f)
            def _():
                to[0].start()
                to[1].start()
            rs[l, name, 2] = to
            return
        _, R1, R2, S, OUT, FS, width = GRAD[name]
        paths, direct = RS_PATHS[l, name], (l, name) in RS_DIRECT
        second = []
        for path, r in zip(paths, first):
            rows = lambda h, path=path: path_rows(path, paths, h)
            r.c()
            S[l, :, rows(None)] = r.total().astype(BF)
            r = Reduce(RY if path == "A" else RZ, lambda j, h, rows=rows: S.at[l, j, rows(h)],
                       lambda n, h, rows=rows: R2.at[l, n, rows(h)],
                       lambda i0, n, rows=rows: R2.at[l, pl.ds(i0, n), rows(None)], direct)
            second.append(r.a())
        rs[l, name, 2] = second

    def r2b(l, name):
        second = rs[l, name, 2]
        if name == "d":
            idx = [new_recv(), new_recv()]
            fin = [rc(Sd.at[l], R2d.at[l, 1], PZ[1], recv=idx[0], cond=is_p),
                   rc(Sd.at[l], R2d.at[l, 2], PZ[0], recv=idx[1], cond=is_m)]
            for cond, got, h, desc in ((is_p, second[0], 0, fin[0]), (is_m, second[1], 1, fin[1])):
                @pl.when(cond)
                def _(got=got, h=h, desc=desc):
                    got.wait_recv()
                    cols = pl.ds(256 * h, 256)
                    Sd[l, :, cols] = (Sd[l, :, cols].astype(F32) + R2d[l, 0, :, cols].astype(F32)).astype(BF)
                    desc.start()
            rs[l, name, 3] = fin
            return
        for r in second:
            r.b()

    def rs3(l, name):
        idx = new_recv()
        if name == "d":
            fin = rs[l, name, 3]
            far = rc(OUTd.at[k], OUTd.at[k], PX[2], recv=idx, cond=is_src & (s == l))
            near = [rc(FSd, OUTd.at[k], PX[j], recv=idx, cond=is_src & (s != l)) for j in range(2)]

            @pl.when(is_src)
            def _():
                wait_recv(fin)
                total = (Sd[l].astype(F32) + R2d[l, 1].astype(F32) + R2d[l, 2].astype(F32)).astype(BF)

                @pl.when(s == l)
                def _():
                    OUTd[k] = total
                    far.start()

                @pl.when(s != l)
                def _():
                    FSd[...] = total
                    for desc in near:
                        desc.start()
            rs[l, name, 4] = far
            return
        _, R1, R2, S, OUT, FS, width = GRAD[name]
        paths = RS_PATHS[l, name]
        second = rs[l, name, 2]
        for r in second:
            r.c()
        sums = [(path_rows(path, paths, None), r.total().astype(BF)) for path, r in zip(paths, second)]
        slot = OUT.at[k, x]
        far = rc(slot, slot, PX[2], recv=idx, cond=(s == l))
        near = [rc(FS, slot, PX[j], recv=idx, cond=(s != l)) for j in range(2)]

        @pl.when(s == l)
        def _():
            for rows, value in sums:
                OUT[k, x, rows] = value
            far.start()

        @pl.when(s != l)
        def _():
            for rows, value in sums:
                FS[rows] = value
            for desc in near:
                desc.start()
        rs[l, name, 4] = idx

    def rs4(l, name):
        got = rs[l, name, 4]
        ref = OUTd.at[k] if name == "d" else GRAD[name][4].at[k]
        fin = rc(ref, ref, SIB, cond=(s == l))

        @pl.when(s == l)
        def _():
            if name == "d":
                @pl.when(z != x)
                def _():
                    got.wait_recv()
            else:
                wait_bytes(GRAD[name][4].at[k, pl.ds(0, 3)], got)
            fin.start()
        rs[l, name, 5] = fin

    def rs5(l, name):
        @pl.when(s == l)
        def _():
            rs[l, name, 5].wait_recv()

    landed = {}

    def edge(l, a, value):
        if l not in landed:
            landed[l] = new_recv()
        goal = 2 * a + l
        ED[l, a] = value

        @pl.when(x == goal)
        def _():
            TT[l, x] = value

        for j in range(3):
            desc = rc(ED.at[l, a], TT.at[l, x], PX[j], recv=landed[l], cond=(X3[j] == goal))

            @pl.when(X3[j] == goal)
            def _(desc=desc):
                desc.start()

    swaps = {}

    def edge_swap(l):
        swaps[l] = rc(TT.at[l, pl.ds(2 * (1 - k), 2)], EO.at[k], SIB, cond=(s == l))

        @pl.when(s == l)
        def _():
            wait_bytes(TT.at[l, pl.ds(0, 3)], landed[l])
            swaps[l].start()
            EO[k] = TT[l, pl.ds(2 * k, 2)]

    def edge_done(l):
        @pl.when(s == l)
        def _():
            swaps[l].wait_recv()

    e0 = lengths[k, 0, 0]
    e1 = e0 + lengths[k, 0, 1]
    def doc(i):
        return jnp.where(i >= e0, 1, 0) + jnp.where(i >= e1, 1, 0)

    def keys(a):
        return TH * (a + 1)

    def allowed(a):
        qi = lax.broadcasted_iota(jnp.int32, (TH, keys(a)), 0) + TH * a
        ki = lax.broadcasted_iota(jnp.int32, (TH, keys(a)), 1)
        return (doc(qi) == doc(ki)) & (ki <= qi)

    def head(value, hh):
        lane = lax.broadcasted_iota(jnp.int32, value.shape, 1)
        return jnp.where((lane < 64) if hh == 0 else (lane >= 64), value, jnp.zeros_like(value))

    def make_angles():
        row = lax.broadcasted_iota(jnp.int32, (T, T), 0)
        ki = lax.broadcasted_iota(jnp.int32, (T, T), 1)
        lane = lax.broadcasted_iota(jnp.int32, (T, 128), 1)
        start = jnp.where(row >= e1, e1, jnp.where(row >= e0, e0, 0))
        pick = jnp.where(ki == row - start, 1.0, 0.0).astype(BF)
        cos = dot(pick, angles[:, 0:128]) + dot(pick, angles[:, 128:256])
        sin = dot(pick, angles[:, 256:384]) + dot(pick, angles[:, 384:512])
        first = (lane < 32) | ((lane >= 64) & (lane < 96))
        CS[0] = cos
        CS[1] = jnp.where(first, -sin, 0.0)
        CS[2] = jnp.where(first, 0.0, sin)

    def turn(v, sign, a):
        r = rows_of(a)
        tiles = []
        for t in range(2):
            u = v[:, 128 * t : 128 * (t + 1)]
            rot = pltpu.roll(u, 96, 1) * CS[1, r] + pltpu.roll(u, 32, 1) * CS[2, r]
            tiles.append(u * CS[0, r] + rot if sign > 0 else u * CS[0, r] - rot)
        return jnp.concatenate(tiles, axis=1)

    def gain(l, i):
        tiles = []
        for t in range(8):
            a = Gn[t // 2, 2 * (t % 2), l].astype(F32) + Gn[t // 2, 2 * (t % 2) + 1, l].astype(F32)
            tiles.append(a[i : i + 1])
        return jnp.concatenate(tiles, axis=1)

    def norm_rows(ref, out, g, a):
        for b in range(2):
            r = pl.ds(TH * a + 64 * b, 64)
            v = ref[r, :].astype(F32)
            inv = lax.rsqrt(jnp.mean(v * v, axis=-1, keepdims=True) + EPS)
            out[r, :] = (v * inv * g).astype(BF)

    def wq(l):
        return Wq[l].reshape(D, 768)

    def project(l, XR, a):
        r = rows_of(a)
        norm_rows(XR, N1.at[l], gain(l, 0), a)
        n = N1[l, r]
        w = wq(l)
        QKV[l, 0, r] = turn(dot(n, w[:, 0:256]), 1, a).astype(BF)
        QKV[l, 1, r] = turn(dot(n, w[:, 256:512]), 1, a).astype(BF)
        v = dot(n, w[:, 512:768])
        if l == 1:
            v = 0.5 * v + 0.5 * QKV[0, 2, r].astype(F32)
        QKV[l, 2, r] = v.astype(BF)

    def attend(l, a):
        ok = allowed(a)
        r, nk = rows_of(a), keys(a)
        for t in range(2):
            cols = pl.ds(128 * t, 128)
            qt, kt, vt = QKV[l, 0, r, cols], QKV[l, 1, 0:nk, cols], QKV[l, 2, 0:nk, cols]
            acc = jnp.zeros((TH, 128), F32)
            for hh in range(2):
                sc = jnp.where(ok, dot_nt(head(qt, hh), kt) * 0.125, -1e30)
                ex = jnp.exp(sc - jnp.max(sc, axis=-1, keepdims=True))
                pr = (ex / jnp.sum(ex, axis=-1, keepdims=True)).astype(BF)
                PR[l, 2 * t + hh, r, 0:nk] = pr
                acc = acc + dot(pr, head(vt, hh))
            O[l, x, r, cols] = acc.astype(BF)
        return Share(O.at[l, x, r], O.at[l, pl.ds(0, 3), r])

    def feed(l, XR, got, i, a):
        r = rows_of(a)
        got.c()
        o = jnp.concatenate([O[l, b, r] for b in range(4)], axis=1)
        H[l, r] = XR[r, :].astype(F32) + dot(o, Wo[l].reshape(D, D))
        norm_rows(H.at[l], N2.at[l], gain(l, 1), a)
        if a == 0:
            ag_done(l, "gu")
        n = N2[l, r]
        GU[l, 0, r] = dot(n, Wgu[l, :, :, :, 0:FP].reshape(D, FP))
        GU[l, 1, r] = dot(n, Wgu[l, :, :, :, FP : 2 * FP].reshape(D, FP))
        for b in range(2):
            q = pl.ds(TH * a + 64 * b, 64)
            ga, up = GU[l, 0, q, :], GU[l, 1, q, :]
            M[l, q, :] = (ga * jax.nn.sigmoid(ga) * up).astype(BF)
        if a == 0:
            ag_done(l, "d")
        return Meet(i, a, dot(M[l, r], Wd[l]).astype(BF))

    def gain_grad(i, row, ref):
        total = jnp.zeros((1, D), F32)
        for a in range(2):
            for j in range(4):
                v = ref[pl.ds(TH * a + BH * j, BH), :].astype(F32)
                inv = lax.rsqrt(jnp.mean(v * v, axis=-1, keepdims=True) + EPS)
                total = total + jnp.sum(PS[i, a, j].astype(F32) * (v * inv), axis=0, keepdims=True)
        GS[0, row : row + 1] = total

    def back_ff(l, DY, i, a):
        r = rows_of(a)
        dm = dot_nt(DY[r, :], Wd[l])
        ga, up = GU[l, 0, r], GU[l, 1, r]
        sg = jax.nn.sigmoid(ga)
        DGU[l, 0, r] = (dm * up * sg * (1.0 + ga * (1.0 - sg))).astype(BF)
        DGU[l, 1, r] = (dm * ga * sg).astype(BF)
        part = (dot_nt(DGU[l, 0, r], Wgu[l, :, :, :, 0:FP].reshape(D, FP))
                + dot_nt(DGU[l, 1, r], Wgu[l, :, :, :, FP : 2 * FP].reshape(D, FP))).astype(BF)
        return Meet(i, a, part)

    def grads_d(l, DY, msib, dysib):
        wait_recv([msib, dysib])
        Gd[l] = (dot_tn(M[l], DY[:, half(D)]) + dot_tn(Ms[l], DYs[l])).astype(BF)
        r1a(l, "d")

    def grads_gu(l, nsib, gsib):
        wait_recv([nsib, gsib])
        grad_ref("gu", l)[...] = (dot_tn(N2[l], DGU[l, k]) + dot_tn(N2s[l], DGUs[l])).astype(BF).reshape(4, 4, SH, FP)
        r1a(l, "gu")

    def back_hidden(l, DY, got, a):
        dn = got.c()
        hf = H[l, own(a), :]
        inv = lax.rsqrt(jnp.mean(hf * hf, axis=-1, keepdims=True) + EPS)
        e = dn * gain(l, 1)
        dh = DY[own(a), :].astype(F32) + inv * e - hf * (inv * inv * inv) * jnp.mean(e * hf, axis=-1, keepdims=True)
        DH[l, a] = dh
        DHB[l, own(a), :] = dh.astype(BF)
        return share_rows(DHB.at[l], a)

    def back_attend(l, got, i, a):
        r, nk = rows_of(a), keys(a)
        got.c()
        do = dot_nt(DHB[l, r], Wo[l, x].reshape(HX, D)).astype(BF)
        dqs, dks, dvs = [], [], []
        for t in range(2):
            cols = pl.ds(128 * t, 128)
            qt, kt, vt = QKV[l, 0, r, cols], QKV[l, 1, 0:nk, cols], QKV[l, 2, 0:nk, cols]
            dot_ = do[:, 128 * t : 128 * (t + 1)]
            dq = jnp.zeros((TH, 128), F32)
            dk = dv = jnp.zeros((nk, 128), F32)
            for hh in range(2):
                pr = PR[l, 2 * t + hh, r, 0:nk]
                pf = pr.astype(F32)
                dom = head(dot_, hh)
                dpp = dot_nt(dom, vt)
                ds = (pf * (dpp - jnp.sum(pf * dpp, axis=-1, keepdims=True))).astype(BF)
                dq = dq + dot(ds, head(kt, hh))
                dk = dk + dot_tn(ds, head(qt, hh))
                dv = dv + dot_tn(pr, dom)
            dqs.append(dq)
            dks.append(dk)
            dvs.append(dv)
        dq, dk, dv = (jnp.concatenate(v, axis=1) for v in (dqs, dks, dvs))
        if a == 1:
            KV0[0] = dk[0:TH]
            KV0[1] = dv[0:TH]
            dk, dv = dk[TH:], dv[TH:]
        else:
            dk, dv = dk + KV0[0], dv + KV0[1]
        DP[l, r, 0:256] = turn((dq * 0.125).astype(BF).astype(F32), -1, a).astype(BF)
        DP[l, r, 256:512] = turn((dk * 0.125).astype(BF).astype(F32), -1, a).astype(BF)
        if l == 1:
            DP[l, r, 512:768] = (0.5 * dv.astype(BF).astype(F32)).astype(BF)
        else:
            DP[l, r, 512:768] = (dv + DP[1, r, 512:768].astype(F32)).astype(BF)
        return Meet(i, a, dot_nt(DP[l, r], wq(l)).astype(BF))

    def grads_q(l, n1sib, psib):
        wait_recv([n1sib, psib])
        Gq[l] = (dot_tn(N1[l], DP[l, :, half(768)]) + dot_tn(N1s[l], DPs[l])).astype(BF).reshape(4, 4, SH, 384)
        r1a(l, "q")

    def push_heads(l):
        hs = pl.ds(pl.multiple_of(x * HX + (1 - k) * 128, 128), 128)
        return push(DHB.at[l, :, hs], DHBs.at[l], SIB)

    def grads_o(l, osib, hsib):
        wait_recv([osib, hsib])
        hs = pl.ds(pl.multiple_of(x * HX + k * 128, 128), 128)
        for b in range(4):
            Go[l, b] = (dot_tn(O[l, b], DHB[l, :, hs]) + dot_tn(Os[l, b], DHBs[l])).astype(BF).reshape(4, SH, 128)
        r1a(l, "o")

    def back_input(l, XR, got, a):
        dn = got.c()
        xf = XR[own(a), :].astype(F32)
        inv = lax.rsqrt(jnp.mean(xf * xf, axis=-1, keepdims=True) + EPS)
        e = dn * gain(l, 0)
        dx = DH[l, a] + inv * e - xf * (inv * inv * inv) * jnp.mean(e * xf, axis=-1, keepdims=True)
        return dx.astype(BF)

    def gsum_a(i, to):
        idx = new_recv()
        for j, t in enumerate(to):
            push(GS.at[i], GR.at[i, j], t, idx)
        return i, len(to), idx

    def gsum_b(sent_to):
        i, n, idx = sent_to
        wait_bytes(GR.at[i, pl.ds(0, n)], idx)
        total = GS[i]
        for j in range(n):
            total = total + GR[i, j]
        GS[i + 1] = total

    X0 = E.at[0]
    DY1 = E.at[1]
    GS[0] = jnp.zeros((8, D), F32)
    for l in range(2):
        Wd[l, FX:FP, :] = jnp.zeros((FP - FX, D), BF)
    s1a(0, "q")
    g1()
    s1a(0, "o")
    s1a(0, "gu")
    s1a(0, "d")
    e_loc.wait()
    e_sib.wait_recv()
    mine2 = pl.ds(pl.multiple_of(xh * 128, 128), 128)
    e_got = push3([E.at[s, mine2]] * 3, [E.at[s, mine2]] * 3, PX)
    s2a(0, "q")
    g2()
    s1b(0, "o")
    s1b(0, "gu")
    make_angles()
    s3(0, "q")
    s2a(0, "o")
    s2a(0, "gu")
    s1b(0, "d")
    s1a(1, "q")
    g3()
    wait_recv(e_got)
    s1a(1, "o")
    s1a(1, "gu")
    s1a(1, "d")
    s2a(0, "d")
    ag_done(0, "q")
    n1sib, osib, nsib, msib = [None, None], [None, None], [None, None], [None, None]
    project(0, X0, 0)
    g0 = attend(0, 0)
    s2b(0, "o")
    s2b(0, "gu")
    project(0, X0, 1)
    n1sib[0] = push(N1.at[0], N1s.at[0], SIB)
    g1 = attend(0, 1)
    dysib = [None, push(DY1.at[:, other_half(D)], DYs.at[1], SIB)]
    s3(0, "o")
    s2b(0, "d")
    for name in ("q", "o", "gu"):
        s1b(1, name)
    s3(0, "gu")
    s2a(1, "q")
    s1b(1, "d")
    s3(0, "d")
    s2a(1, "o")
    s2a(1, "gu")
    ag_done(0, "o")
    m0 = feed(0, X0, g0, 0, 0)
    s2b(1, "q")
    m1 = feed(0, X0, g1, 0, 1)
    osib[0] = push(O.at[0], Os.at[0], SIB)
    nsib[0] = push(N2.at[0], N2s.at[0], SIB)
    msib[0] = push(M.at[0], Ms.at[0], SIB)
    s2a(1, "d")
    s2b(1, "o")
    X1[own(0), :] = (m0.c() + H[0, own(0), :]).astype(BF)
    g0 = share_rows(X1, 0)
    s2b(1, "gu")
    X1[own(1), :] = (m1.c() + H[0, own(1), :]).astype(BF)
    g1 = share_rows(X1, 1)
    s3(1, "q")
    s2b(1, "d")
    s3(1, "o")
    g0.c()
    ag_done(1, "q")
    project(1, X1, 0)
    g0 = attend(1, 0)
    s3(1, "gu")
    s3(1, "d")
    early = close()
    g1.c()
    project(1, X1, 1)
    n1sib[1] = push(N1.at[1], N1s.at[1], SIB)
    g1 = attend(1, 1)
    ag_done(1, "o")
    y0 = feed(1, X1, g0, 1, 0)
    y1 = feed(1, X1, g1, 1, 1)
    osib[1] = push(O.at[1], Os.at[1], SIB)
    nsib[1] = push(N2.at[1], N2s.at[1], SIB)
    msib[1] = push(M.at[1], Ms.at[1], SIB)

    m1 = back_ff(1, DY1, 2, 1)
    m0 = back_ff(1, DY1, 2, 0)
    gsib = push(DGU.at[1, 1 - k], DGUs.at[1], SIB)
    grads_d(1, DY1, msib[1], dysib[1])
    g1 = back_hidden(1, DY1, m1, 1)
    grads_gu(1, nsib[1], gsib)
    g0 = back_hidden(1, DY1, m0, 0)
    r1b(1, "d")
    m1 = back_attend(1, g1, 3, 1)
    m0 = back_attend(1, g0, 3, 0)
    hsib = push_heads(1)
    psib = push(DP.at[1, :, other_half(768)], DPs.at[1], SIB)
    r1b(1, "gu")
    edge(1, 0, (y0.c() + H[1, own(0), :]).astype(BF))
    edge(1, 1, (y1.c() + H[1, own(1), :]).astype(BF))
    grads_q(1, n1sib[1], psib)
    DY0[own(1), :] = back_input(1, X1, m1, 1)
    g1 = share_rows(DY0, 1)
    DY0[own(0), :] = back_input(1, X1, m0, 0)
    g0 = share_rows(DY0, 0)
    r2a(1, "d")
    grads_o(1, osib[1], hsib)
    r2a(1, "gu")

    g1.c()
    m1 = back_ff(0, DY0, 4, 1)
    g0.c()
    m0 = back_ff(0, DY0, 4, 0)
    gsib = push(DGU.at[0, 1 - k], DGUs.at[0], SIB)
    dysib[0] = push(DY0.at[:, other_half(D)], DYs.at[0], SIB)
    r2b(1, "d")
    r1b(1, "q")
    flush(0, early)
    grads_d(0, DY0, msib[0], dysib[0])
    g1 = back_hidden(0, DY0, m1, 1)
    grads_gu(0, nsib[0], gsib)
    g0 = back_hidden(0, DY0, m0, 0)
    r1b(1, "o")
    r2b(1, "gu")
    m1 = back_attend(0, g1, 5, 1)
    m0 = back_attend(0, g0, 5, 0)
    hsib = push_heads(0)
    psib = push(DP.at[0, :, other_half(768)], DPs.at[0], SIB)
    r1b(0, "d")
    gain_grad(5, 0, X0)
    gain_grad(4, 1, H.at[0])
    gain_grad(3, 2, X1)
    gain_grad(2, 3, H.at[1])
    g = gsum_a(0, PX)
    r1b(0, "gu")
    grads_q(0, n1sib[0], psib)
    grads_o(0, osib[0], hsib)
    r2a(1, "q")
    r2a(1, "o")
    edge(0, 1, back_input(0, X0, m1, 1))
    edge(0, 0, back_input(0, X0, m0, 0))
    rs3(1, "d")
    r2a(0, "d")
    gsum_b(g)
    g = gsum_a(1, PY)
    r2a(0, "gu")
    r2a(0, "q")
    r2a(0, "o")
    edge_swap(0)
    r2b(0, "d")
    rs3(1, "gu")
    gsum_b(g)
    g = gsum_a(2, PZ)
    r2b(1, "q")
    r2b(1, "o")
    r2b(0, "gu")
    edge_swap(1)
    rs4(1, "d")
    rs3(0, "q")
    rs3(0, "o")
    rs3(0, "d")
    gsum_b(g)
    g = gsum_a(3, [SIB])
    rs3(1, "q")
    rs3(1, "o")
    rs3(0, "gu")
    rs4(1, "gu")
    rs4(0, "q")
    rs4(0, "o")
    rs4(0, "d")
    rs4(1, "q")
    rs4(1, "o")
    gsum_b(g)
    edge_done(0)
    edge_done(1)
    rs4(0, "gu")
    for name in ("d", "q", "o", "gu"):
        rs5(1, name)
        rs5(0, name)
    outs = [local(a, b) for a, b in
            ((OUTq, oq_hbm), (OUTo, oo_hbm), (OUTgu, ogu_hbm), (OUTd, od_hbm), (EO, edge_hbm), (GS.at[4], gsum_hbm))]
    for o in outs:
        o.start()
    flush(early, len(groups))
    flush_conditional()
    for o in outs:
        o.wait()
    assert counter[0] <= N_RECV and counter[1] <= N_LOC and counter[2] <= N_SEND, counter


def epilogue(*refs):
    given, (edges, qkv, out, gate, up, down, gg), held, sem = refs[:6], refs[6:13], refs[13:19], refs[19]
    copies = [pltpu.make_async_copy(a, b, sem.at[i]) for i, (a, b) in enumerate(zip(given, held))]
    for cp in copies:
        cp.start()
    for cp in copies:
        cp.wait()
    oq, oo, ogu, od, edge, gsum = held
    s = lax.axis_index("section")
    dp = lax.axis_index("dp")
    edges[0, :, 0] = edge[...].reshape(2, BT, D)
    for x in range(4):
        a, b = oq[0, x].astype(F32), oq[1, x].astype(F32)
        qkv[0, :, HX * x : HX * (x + 1)] = a[:, 0:256]
        qkv[0, :, D + HX * x : D + HX * x + 128] = a[:, 256:384]
        qkv[0, :, D + HX * x + 128 : D + HX * (x + 1)] = b[:, 0:128]
        qkv[0, :, 2 * D + HX * x : 2 * D + HX * (x + 1)] = b[:, 128:384]
        for h in range(2):
            out[0, :, HX * x + 128 * h : HX * x + 128 * (h + 1)] = oo[h, x].astype(F32)
    for h, ref in ((0, gate), (1, up)):
        for p in range(2):
            a = ogu[h, 2 * p].astype(F32)
            b = pltpu.roll(ogu[h, 2 * p + 1].astype(F32), 64, 1)
            c = 2 * FX * p
            ref[0, :, c : c + 640] = a[:, 0:640]
            ref[0, :, c + 640 : c + 768] = a[:, 640:768] + b[:, 0:128]
            ref[0, :, c + 768 : c + 2 * FX] = b[:, 128:768]
    for h in range(2):
        down[0, :, 512 * h : 512 * (h + 1)] = od[h].astype(F32)
    tile = gsum[:, pl.ds(pl.multiple_of(128 * lax.div(dp, 2), 128), 128)]
    tile = jnp.where(lax.rem(dp, 2) == 1, pltpu.roll(tile, 64, 1), tile)
    rows = jnp.where(s == 1, tile[2:4], tile[0:2])
    gg[0] = rows[:, 0:SH]


def run_kernel(lengths, ends, qkv_w, out_w, gate_w, up_w, down_w, gains, angles):
    V = pltpu.VMEM
    sh = jax.ShapeDtypeStruct
    any_ = pl.BlockSpec(memory_space=pl.ANY)
    vm = pl.BlockSpec(memory_space=pltpu.VMEM)
    out_shape = [
        sh((2, 4, SH, 384), BF), sh((2, 4, SH, 128), BF), sh((2, 4, SH, FP), BF), sh((2, DR, 512), BF),
        sh((2, 2, BH, D), BF), sh((8, D), F32), sh((GROUP_BYTES // 4096, 16, 128), BF),
    ]
    scratch = [
        V((2, 4, 4, SH, 768), BF), V((2, 4, 4, SH, D), BF), V((2, 4, 4, SH, 2 * FP), BF), V((2, FP, D), BF),
        V((4, 4, 2, 16, 128), BF),
        V((2, T, D), BF), V((T, D), BF), V((T, D), BF),
        V((2, T, D), BF), V((2, T, D), BF), V((2, T, D), BF), V((2, T, D), BF),
        V((2, T, D), F32), V((2, 3, T, HX), BF), V((2, 4, T, T), BF),
        V((2, 4, T, HX), BF), V((2, 4, T, HX), BF),
        V((2, 2, T, FP), F32), V((2, T, FP), BF), V((2, T, FP), BF),
        V((2, 2, T, FP), BF), V((2, T, FP), BF),
        V((2, T, 768), BF), V((2, T, 384), BF),
        V((2, T, D), BF), V((2, T, 128), BF), V((2, T, 512), BF), V((2, 2, BH, D), F32),
        V((2, TH, HX), F32), V((2, 2, BH, D), BF),
        V((6, 2, 4, BH, D), BF), V((6, 2, 3, BH, D), BF),
        V((2, 4, 4, SH, 384), BF), V((2, 4, 4, SH, 128), BF), V((1, 4, 4, SH, FP), BF), V((2, FP, 512), BF),
        V((2, 3, 4, SH, 384), BF), V((2, 3, 4, SH, 128), BF), V((2, 3, 4, SH, FP), BF), V((2, 3, DR, 512), BF),
        V((2, 3, SH, 384), BF), V((2, 3, SH, 128), BF), V((2, 3, SH, FP), BF), V((2, 3, DR, 512), BF),
        V((2, 4, SH, 384), BF), V((2, 4, SH, 128), BF), V((2, 4, SH, FP), BF), V((2, DR, 512), BF),
        V((2, 4, SH, 384), BF), V((2, 4, SH, 128), BF), V((2, 4, SH, FP), BF), V((2, DR, 512), BF),
        V((SH, 384), BF), V((SH, 128), BF), V((SH, FP), BF), V((DR, 512), BF),
        V((5, 8, D), F32), V((4, 3, 8, D), F32), V((2, 4, BH, D), BF), V((2, 2, BH, D), BF),
        V((3, T, 128), F32), V((SH, 384), BF), V((SH, FP), BF), V((SH, 512), BF), V((DR, 512), BF),
        V((16, 128), BF), V((16, 128), F32),
        pltpu.SemaphoreType.DMA((N_SEND,)), pltpu.SemaphoreType.DMA((N_RECV,)), pltpu.SemaphoreType.DMA((N_LOC,)),
    ]
    return pl.pallas_call(
        kernel,
        out_shape=out_shape,
        in_specs=[pl.BlockSpec(memory_space=pltpu.SMEM)] + [any_] * 6 + [vm] * 2,
        out_specs=[any_] * 7,
        scratch_shapes=scratch,
        name="two_layers",
        compiler_params=pltpu.CompilerParams(
            collective_id=0, has_side_effects=True, vmem_limit_bytes=64 * 1024 * 1024 - 65536
        ),
    )(lengths, ends, qkv_w, out_w, gate_w, up_w, down_w, gains, angles)


def angle_table():
    pos = np.arange(T, dtype=np.float64)[:, None]
    freq = 10000.0 ** (-(np.arange(128) % 32) / 32.0)
    parts = []
    for v in (np.cos(pos * freq), np.sin(pos * freq)):
        high = v.astype(jnp.bfloat16)
        parts += [high, (v - high.astype(np.float64)).astype(jnp.bfloat16)]
    return np.concatenate(parts, axis=1)


def per_device(ends_in, lengths, qkv_w, out_w, gate_w, up_w, down_w, gains):
    oq, oo, ogu, od, edge, gsum, _ = run_kernel(
        lengths, ends_in, qkv_w, out_w, gate_w, up_w, down_w, gains, jnp.asarray(angle_table()))
    sh = jax.ShapeDtypeStruct
    return pl.pallas_call(
        epilogue,
        out_shape=[
            sh((1, 2, 1, BT, D), BF), sh((1, SH, 3 * D), F32), sh((1, SH, D), F32), sh((1, SH, FF), F32),
            sh((1, SH, FF), F32), sh((1, DR, D), F32), sh((1, 2, SH), F32),
        ],
        in_specs=[pl.BlockSpec(memory_space=pl.ANY)] * 6,
        out_specs=[pl.BlockSpec(memory_space=pltpu.VMEM)] * 7,
        scratch_shapes=[pltpu.VMEM(v.shape, v.dtype) for v in (oq, oo, ogu, od, edge, gsum)]
        + [pltpu.SemaphoreType.DMA((6,))],
        name="place_outputs",
        compiler_params=pltpu.CompilerParams(vmem_limit_bytes=63 * 1024 * 1024),
    )(oq, oo, ogu, od, edge, gsum)


def solution(mesh):
    in_specs = (
        P("section", None, "dp", "ctx", None),
        P(None, "dp", None),
        P("section", "dp", None),
        P("section", "dp", None),
        P("section", "dp", None),
        P("section", "dp", None),
        P("section", "dp", None),
        P("section", None, "dp"),
    )
    out_specs = (
        P("section", None, "dp", "ctx", None),
        P("section", "dp", None),
        P("section", "dp", None),
        P("section", "dp", None),
        P("section", "dp", None),
        P("section", "dp", None),
        P("section", None, "dp"),
    )
    return jax.shard_map(per_device, mesh=mesh, in_specs=in_specs, out_specs=out_specs, check_vma=False)
```

time: 181 us -> 163 us (0.901)
  Pallas kernels: 180 us -> 161 us
    pallas_call x1, Pallas kernels: 176 us -> 157 us  [run_kernel(): pl.pallas_call(kernel, out_shape=out_shape, in_specs=[pl.BlockSpec(memory...]
where the time goes in v4:
time: 163 us; the launch traced here: 161 us
  Pallas kernels  161 us (99%)
    pallas_call x1, Pallas kernels, run_kernel(): pl.pallas_call(kernel, out_shape=out_shape, in_specs=[pl.BlockSpec(memory...  157 us
    pallas_call x1, Pallas kernels, per_device(): pl.pallas_call(epilogue, out_shape=[sh((1, 2, 1, BT, D), BF), sh((1, SH,...  3.5 us

profile of v4, /device:TPU:1, one launch (start us, length us, event | category | flops | bytes accessed | tf_op | source)
XLA Modules:
  0.0 161.4 jit_solution(16106268429139410309)
XLA Ops:
  0.6 157.1 %two_layers.1 = (bf16[2,4,64,384]{3,2,1,0:T(8,128)(2,1)}, bf16[2,4,64,128]{3,2,1,0:T(8,128)(2,1)}, bf16[2,4,64,768]{3,2,1,0:T(8,128)(2,1)}, bf16[2,176,512]{2,1,...) custom-call(s32[2,1,3]{2,1,0:T(1,128)} %lengths.1, ...), custom_call_target="tpu_custom_call" | custom-call | tf_op jit(solution)/shard_map/two_layers/pallas_call | solution.py:1157
  157.7 3.5 %place_outputs.1 = (bf16[1,2,1,64,1024]{4,3,2,1,0:T(8,128)(2,1)}, f32[1,64,3072]{2,1,0:T(8,128)}, f32[1,64,1024]{2,1,0:T(8,128)}, f32[1,64,2816]{2,1,0:T(8,128)}...) custom-call(bf16[2,4,64,384]{3,2,1,0:T(8,128)(2,1)} %get-tuple-element.13.refs_0_, ...), custom_call_target="tpu_custom_call" | custom-call | tf_op jit(solution)/shard_map/place_outputs/pallas_call | solution.py:1184

commit v5 on v4

--- a/solution.py
+++ b/solution.py
@@ -77,7 +77,6 @@
     partners = PX + PY + PZ + [SIB]
     for p in partners:
         pl.semaphore_signal(bar, inc=1, device_id=p, device_id_type=MESH)
-    pl.semaphore_wait(bar, len(partners))
 
     counter = [0, 0, 0]
     sent = []
@@ -287,6 +286,7 @@
     gain_in[0:2, :] = jnp.where(odd, jnp.concatenate([gz, gv], axis=1), jnp.concatenate([gv, gz], axis=1))
     NT[...] = gain_in[...].astype(BF)
     Gn[z, y, s] = NT[...]
+    pl.semaphore_wait(bar, len(partners))
     pre["g"] = rc(NT, Gn.at[z, y, s], TO)
     pre["g"].start()
 
@@ -904,17 +904,17 @@
     s1a(0, "q")
     g1()
     s1a(0, "o")
-    s1a(0, "gu")
-    s1a(0, "d")
     e_loc.wait()
     e_sib.wait_recv()
     mine2 = pl.ds(pl.multiple_of(xh * 128, 128), 128)
     e_got = push3([E.at[s, mine2]] * 3, [E.at[s, mine2]] * 3, PX)
     s2a(0, "q")
+    s1a(0, "gu")
+    s1a(0, "d")
     g2()
     s1b(0, "o")
+    make_angles()
     s1b(0, "gu")
-    make_angles()
     s3(0, "q")
     s2a(0, "o")
     s2a(0, "gu")
@@ -986,8 +986,8 @@
     gsib = push(DGU.at[1, 1 - k], DGUs.at[1], SIB)
     grads_d(1, DY1, msib[1], dysib[1])
     g1 = back_hidden(1, DY1, m1, 1)
+    g0 = back_hidden(1, DY1, m0, 0)
     grads_gu(1, nsib[1], gsib)
-    g0 = back_hidden(1, DY1, m0, 0)
     r1b(1, "d")
     m1 = back_attend(1, g1, 3, 1)
     m0 = back_attend(1, g0, 3, 0)
@@ -1072,13 +1072,17 @@
     edge_done(0)
     edge_done(1)
     rs4(0, "gu")
-    for name in ("d", "q", "o", "gu"):
+    outs = []
+
+    def put(a, b):
+        outs.append(local(a, b))
+        outs[-1].start()
+    put(EO, edge_hbm)
+    put(GS.at[4], gsum_hbm)
+    for name, a, b in (("d", OUTd, od_hbm), ("q", OUTq, oq_hbm), ("o", OUTo, oo_hbm), ("gu", OUTgu, ogu_hbm)):
         rs5(1, name)
         rs5(0, name)
-    outs = [local(a, b) for a, b in
-            ((OUTq, oq_hbm), (OUTo, oo_hbm), (OUTgu, ogu_hbm), (OUTd, od_hbm), (EO, edge_hbm), (GS.at[4], gsum_hbm))]
-    for o in outs:
-        o.start()
+        put(a, b)
     flush(early, len(groups))
     flush_conditional()
     for o in outs:

time: 163 us -> 161 us (0.988)
  Pallas kernels: 161 us -> 158 us
    pallas_call x1, Pallas kernels: 157 us -> 155 us  [run_kernel(): pl.pallas_call(kernel, out_shape=out_shape, in_specs=[pl.BlockSpec(memory...]
where the time goes in v5:
time: 161 us; the launch traced here: 159 us
  Pallas kernels  158 us (98%)
    pallas_call x1, Pallas kernels, run_kernel(): pl.pallas_call(kernel, out_shape=out_shape, in_specs=[pl.BlockSpec(memory...  155 us
    pallas_call x1, Pallas kernels, per_device(): pl.pallas_call(epilogue, out_shape=[sh((1, 2, 1, BT, D), BF), sh((1, SH,...  3.5 us

profile of v5, /device:TPU:1, one launch (start us, length us, event | category | flops | bytes accessed | tf_op | source)
XLA Modules:
  0.0 159.1 jit_solution(14101351134244775513)
XLA Ops:
  0.6 154.8 %two_layers.1 = (bf16[2,4,64,384]{3,2,1,0:T(8,128)(2,1)}, bf16[2,4,64,128]{3,2,1,0:T(8,128)(2,1)}, bf16[2,4,64,768]{3,2,1,0:T(8,128)(2,1)}, bf16[2,176,512]{2,1,...) custom-call(s32[2,1,3]{2,1,0:T(1,128)} %lengths.1, ...), custom_call_target="tpu_custom_call" | custom-call | tf_op jit(solution)/shard_map/two_layers/pallas_call | solution.py:1161
  155.4 3.5 %place_outputs.1 = (bf16[1,2,1,64,1024]{4,3,2,1,0:T(8,128)(2,1)}, f32[1,64,3072]{2,1,0:T(8,128)}, f32[1,64,1024]{2,1,0:T(8,128)}, f32[1,64,2816]{2,1,0:T(8,128)}...) custom-call(bf16[2,4,64,384]{3,2,1,0:T(8,128)(2,1)} %get-tuple-element.13.refs_0_, ...), custom_call_target="tpu_custom_call" | custom-call | tf_op jit(solution)/shard_map/place_outputs/pallas_call | solution.py:1188

commit v6 on v5

--- a/solution.py
+++ b/solution.py
@@ -35,9 +35,9 @@
     return lax.dot_general(a, b, (((0,), (0,)), ((), ())), preferred_element_type=F32)
 
 
-N_SEND = 76
-N_RECV = 244
-N_LOC = 18
+N_SEND = 73
+N_RECV = 207
+N_LOC = 17
 GROUP_BYTES = 4 * 1024 * 1024
 
 
@@ -499,7 +499,7 @@
         return GRAD[name][0].at[0 if name == "gu" else l]
 
     RS_PATHS = {(l, name): "AB" for l in range(2) for name in GRAD}
-    RS_DIRECT = ((0, "q"), (0, "o"))
+    RS_DIRECT = ((0, "q"), (0, "o"), (1, "q"), (1, "o"))
 
     def r1a(l, name):
         if name == "d":

time: 161 us -> 162 us (level)
  no operation moved by 1% of the time
where the time goes in v6:
time: 162 us; the launch traced here: 159 us
  Pallas kernels  159 us (98%)
    pallas_call x1, Pallas kernels, run_kernel(): pl.pallas_call(kernel, out_shape=out_shape, in_specs=[pl.BlockSpec(memory...  155 us
    pallas_call x1, Pallas kernels, per_device(): pl.pallas_call(epilogue, out_shape=[sh((1, 2, 1, BT, D), BF), sh((1, SH,...  3.5 us

profile of v6, /device:TPU:1, one launch (start us, length us, event | category | flops | bytes accessed | tf_op | source)
XLA Modules:
  0.0 159.4 jit_solution(12300957096158217937)
XLA Ops:
  0.6 155.1 %two_layers.1 = (bf16[2,4,64,384]{3,2,1,0:T(8,128)(2,1)}, bf16[2,4,64,128]{3,2,1,0:T(8,128)(2,1)}, bf16[2,4,64,768]{3,2,1,0:T(8,128)(2,1)}, bf16[2,176,512]{2,1,...) custom-call(s32[2,1,3]{2,1,0:T(1,128)} %lengths.1, ...), custom_call_target="tpu_custom_call" | custom-call | tf_op jit(solution)/shard_map/two_layers/pallas_call | solution.py:1161
  155.8 3.5 %place_outputs.1 = (bf16[1,2,1,64,1024]{4,3,2,1,0:T(8,128)(2,1)}, f32[1,64,3072]{2,1,0:T(8,128)}, f32[1,64,1024]{2,1,0:T(8,128)}, f32[1,64,2816]{2,1,0:T(8,128)}...) custom-call(bf16[2,4,64,384]{3,2,1,0:T(8,128)(2,1)} %get-tuple-element.13.refs_0_, ...), custom_call_target="tpu_custom_call" | custom-call | tf_op jit(solution)/shard_map/place_outputs/pallas_call | solution.py:1188
